TPU v7x, 32 devices: a whole 2x2x4 slice. The times are simulated.
32 devices in a mesh: dp: 8 (over z, core), ctx: 4 (over y, x).
Axes of the slice: x: 2, y: 2, z: 4, core: 2. Of those that a mesh axis runs over, the one named last changes fastest.
Arguments:
- tokens: bfloat16 [16, 1024, 2048], P('dp', 'ctx'), may hold values from -6 to 6
- span_order: int32 [16, 8], P('dp'), may hold values from 0 to 7, as said below
- out_grad: bfloat16 [16, 1024, 2048], P('dp', 'ctx'), may hold values from -6 to 6
- first_gain: bfloat16 [2048], P(('dp', 'ctx')), may hold values from 0.5 to 1.5
- query_weight: bfloat16 [2048, 2048], P(('dp', 'ctx')), may hold values from -0.125 to 0.125
- key_matrix: bfloat16 [2048, 512], P(('dp', 'ctx')), may hold values from -0.125 to 0.125
- value_matrix: bfloat16 [2048, 512], P(('dp', 'ctx')), may hold values from -0.125 to 0.125
- merge_weight: bfloat16 [2048, 2048], P(('dp', 'ctx')), may hold values from -2 to 2
- second_gain: bfloat16 [2048], P(('dp', 'ctx')), may hold values from 0.5 to 1.5
- gate_weight: bfloat16 [2048, 8192], P(('dp', 'ctx')), may hold values from -0.125 to 0.125
- up_weight: bfloat16 [2048, 8192], P(('dp', 'ctx')), may hold values from -0.125 to 0.125
- down_weight: bfloat16 [2048, 8192], P(('dp', 'ctx')), may hold values from -0.0625 to 0.0625
Outputs:
- block_output: bfloat16 [16, 1024, 2048], P('dp', 'ctx')
- input_grad: float32 [16, 1024, 2048], P('dp', 'ctx')
- first_gain_grad: float32 [2048], P(('dp', 'ctx'))
- query_grad: float32 [2048, 2048], P(('dp', 'ctx'))
- key_grad: float32 [2048, 512], P(('dp', 'ctx'))
- value_grad: float32 [2048, 512], P(('dp', 'ctx'))
- merge_grad: float32 [2048, 2048], P(('dp', 'ctx'))
- second_gain_grad: float32 [2048], P(('dp', 'ctx'))
- gate_grad: float32 [2048, 8192], P(('dp', 'ctx'))
- up_grad: float32 [2048, 8192], P(('dp', 'ctx'))
- down_grad: float32 [2048, 8192], P(('dp', 'ctx'))
Inputs may be any that keep to these rules, and one draw needn't show every extreme that they name: `span_order`: each row lists every span number 0 to 7 once; slots 2 c and 2 c + 1 hold spans j and 7 - j for some j, in either order.
All inputs are finite; a program needn't handle non-finite values.
Results may differ from a plain program's by a relative error of at most 0.014.
Values may be sent and summed in bfloat16 or wider, within the bound.
A program may use at most 768 MiB of HBM per device.

v0:
```python
import math

import jax
import jax.numpy as jnp
from jax import lax
from jax.sharding import PartitionSpec as P

HEAD_SIZE = 64


EPS = 1e-05
THETA = 500000.0


def rope_tables(positions):
    half_dim = HEAD_SIZE // 2
    frequency = jnp.exp(
        jnp.arange(half_dim, dtype=jnp.float32) * (-2.0 * math.log(THETA) / HEAD_SIZE)
    )
    angles = positions.astype(jnp.float32)[:, None] * frequency[None, :]
    return (jnp.cos(angles)[:, None, :], jnp.sin(angles)[:, None, :])


def rotate(head_rows, cos_table, sin_table):
    half_dim = head_rows.shape[-1] // 2
    leading = head_rows[..., :half_dim]
    trailing = head_rows[..., half_dim:]
    return jnp.concatenate(
        [leading * cos_table - trailing * sin_table, trailing * cos_table + leading * sin_table],
        axis=-1,
    )


def norm_forward(values):
    inverse_rms = lax.rsqrt(jnp.mean(values * values, axis=-1, keepdims=True) + EPS)
    return (values * inverse_rms, inverse_rms)


def norm_backward(grad_normed, normed, inverse_rms, gain_vec):
    grad_hat = grad_normed * gain_vec
    grad_input = inverse_rms * (
        grad_hat - normed * jnp.mean(grad_hat * normed, axis=-1, keepdims=True)
    )
    return (grad_input, jnp.sum(grad_normed * normed, axis=0))


def dot_plain(left, right):
    return jnp.dot(left, right, preferred_element_type=jnp.float32)


def dot_rows(left, right):
    return lax.dot_general(
        left, right, (((1,), (1,)), ((), ())), preferred_element_type=jnp.float32
    )


def dot_tokens(left, right):
    return lax.dot_general(
        left, right, (((0,), (0,)), ((), ())), preferred_element_type=jnp.float32
    )


def to_groups(flat_rows, kv_heads):
    row_total = flat_rows.shape[0]
    return (
        flat_rows.reshape(row_total, kv_heads, -1, HEAD_SIZE)
        .transpose(1, 2, 0, 3)
        .reshape(kv_heads, -1, HEAD_SIZE)
    )


def from_groups(grouped, row_total):
    kv_heads = grouped.shape[0]
    return (
        grouped.reshape(kv_heads, -1, row_total, HEAD_SIZE)
        .transpose(2, 0, 1, 3)
        .reshape(row_total, -1)
    )


def keys_to_groups(flat_rows, kv_heads):
    return flat_rows.reshape(flat_rows.shape[0], kv_heads, HEAD_SIZE).transpose(1, 0, 2)


def keys_from_groups(grouped):
    return grouped.transpose(1, 0, 2).reshape(grouped.shape[1], -1)


def attention_terms(gain_one_part, rows, gain_two_part):
    attn_in, grad_query, grad_key, grad_value, attn_out, merge_in = rows[:6]
    return (
        gain_one_part,
        dot_tokens(attn_in, grad_query),
        dot_tokens(attn_in, grad_key),
        dot_tokens(attn_in, grad_value),
        dot_tokens(merge_in, attn_out),
        gain_two_part,
    )


def feed_builder(rows, row_count):
    feed_in, grad_gate, grad_up, activated, down_in = rows[6:]
    right_side = jnp.stack([grad_gate, grad_up, activated], axis=1)
    feed_width = grad_gate.shape[1]
    left_side = jnp.stack([feed_in, feed_in, down_in], axis=1)
    term = jnp.einsum("tjr,tjf->rjf", left_side, right_side, preferred_element_type=jnp.float32)
    return term.reshape(row_count, 3 * feed_width)


def body(
    tokens,
    span_order,
    out_grad,
    first_gain,
    query_weight,
    key_matrix,
    value_matrix,
    merge_weight,
    second_gain,
    gate_weight,
    up_weight,
    down_weight,
):
    micro_count = tokens.shape[0]
    local_len = tokens.shape[1]
    ctx_count = lax.axis_size("ctx")
    seq_total = local_len * ctx_count
    span_len = local_len // 2
    kv_heads = key_matrix.shape[1] // HEAD_SIZE
    group_size = query_weight.shape[1] // (HEAD_SIZE * kv_heads)
    score_scale = HEAD_SIZE ** (-0.5)
    ctx_rank = lax.axis_index("ctx")
    weight_rows = gate_weight.shape[0]
    attention_kept = (
        lax.all_gather(first_gain, ("dp", "ctx"), axis=0, tiled=True),
        lax.all_gather(query_weight, ("dp", "ctx"), axis=0, tiled=True),
        lax.all_gather(key_matrix, ("dp", "ctx"), axis=0, tiled=True),
        lax.all_gather(value_matrix, ("dp", "ctx"), axis=0, tiled=True),
        lax.all_gather(merge_weight, ("dp", "ctx"), axis=0, tiled=True),
    )
    feed_kept = (
        lax.all_gather(second_gain, ("dp", "ctx"), axis=0, tiled=True),
        lax.all_gather(gate_weight, ("dp", "ctx"), axis=0, tiled=True),
        lax.all_gather(up_weight, ("dp", "ctx"), axis=0, tiled=True),
        lax.all_gather(down_weight, ("dp", "ctx"), axis=0, tiled=True),
    )
    outputs = []
    input_grads = []
    kept_rows = []
    gain_one_sum = None
    gain_two_sum = None
    attention_sums = None
    feed_sum = None
    for batch_index in range(micro_count):
        ordering_row = span_order[batch_index]
        key_positions = (
            ordering_row[:, None] * span_len + jnp.arange(span_len, dtype=jnp.int32)[None, :]
        ).reshape(seq_total)
        query_positions = lax.dynamic_slice_in_dim(key_positions, ctx_rank * local_len, local_len)
        cos_table, sin_table = rope_tables(query_positions)
        row_positions = jnp.tile(query_positions, group_size)
        allowed = row_positions[:, None] >= key_positions[None, :]
        gain_full, query_full, key_full, value_full, merge_full = attention_kept
        gain_one = gain_full.astype(jnp.float32)
        inputs = tokens[batch_index].astype(jnp.float32)
        normed_one, inverse_one = norm_forward(inputs)
        attn_in = (normed_one * gain_one).astype(jnp.bfloat16)
        query_pre = dot_plain(attn_in, query_full)
        queries = (
            rotate(query_pre.reshape(local_len, -1, HEAD_SIZE), cos_table, sin_table)
            .reshape(local_len, -1)
            .astype(jnp.bfloat16)
        )
        key_pre = dot_plain(attn_in, key_full)
        keys_own = (
            rotate(key_pre.reshape(local_len, -1, HEAD_SIZE), cos_table, sin_table)
            .reshape(local_len, -1)
            .astype(jnp.bfloat16)
        )
        values_own = dot_plain(attn_in, value_full).astype(jnp.bfloat16)
        keys_all, values_all = (
            lax.all_gather(keys_own, "ctx", axis=0, tiled=True),
            lax.all_gather(values_own, "ctx", axis=0, tiled=True),
        )
        query_groups = to_groups(queries, kv_heads)
        key_groups = keys_to_groups(keys_all, kv_heads)
        value_groups = keys_to_groups(values_all, kv_heads)
        scores = (
            jnp.einsum("hqd,hkd->hqk", query_groups, key_groups, preferred_element_type=jnp.float32)
            * score_scale
        )
        masked = jnp.where(allowed[None], scores, -1e30)
        row_max = jnp.max(masked, axis=-1, keepdims=True)
        log_total = row_max + jnp.log(jnp.sum(jnp.exp(masked - row_max), axis=-1, keepdims=True))
        probs_low = jnp.exp(masked - log_total).astype(jnp.bfloat16)
        attended = jnp.einsum(
            "hqk,hkd->hqd", probs_low, value_groups, preferred_element_type=jnp.float32
        )
        attn_out = from_groups(attended, local_len).astype(jnp.bfloat16)
        hidden_one = inputs + dot_rows(attn_out, merge_full)
        feed_gain_full, gate_full, up_full, down_full = feed_kept
        gain_two = feed_gain_full.astype(jnp.float32)
        normed_two, inverse_two = norm_forward(hidden_one)
        feed_in = (normed_two * gain_two).astype(jnp.bfloat16)
        gate_pre = dot_plain(feed_in, gate_full)
        up_pre = dot_plain(feed_in, up_full)
        activated = (jax.nn.silu(gate_pre) * up_pre).astype(jnp.bfloat16)
        outputs.append((hidden_one + dot_rows(activated, down_full)).astype(jnp.bfloat16))
        cotangent = out_grad[batch_index].astype(jnp.float32)
        down_in = cotangent.astype(jnp.bfloat16)
        grad_act = dot_plain(down_in, down_full)
        sigmoid_gate = jax.nn.sigmoid(gate_pre)
        grad_gate = (
            grad_act * up_pre * sigmoid_gate * (1.0 + gate_pre * (1.0 - sigmoid_gate))
        ).astype(jnp.bfloat16)
        grad_up = (grad_act * (gate_pre * sigmoid_gate)).astype(jnp.bfloat16)
        grad_feed_in = dot_rows(grad_gate, gate_full) + dot_rows(grad_up, up_full)
        grad_middle, gain_two_part = norm_backward(grad_feed_in, normed_two, inverse_two, gain_two)
        grad_hidden = cotangent + grad_middle
        merge_in = grad_hidden.astype(jnp.bfloat16)
        grad_attn = dot_plain(merge_in, merge_full).astype(jnp.bfloat16)
        grad_groups = to_groups(grad_attn, kv_heads)
        scores_again = (
            jnp.einsum("hqd,hkd->hqk", query_groups, key_groups, preferred_element_type=jnp.float32)
            * score_scale
        )
        probs = jnp.exp(jnp.where(allowed[None], scores_again, -1e30) - log_total)
        probs_again = probs.astype(jnp.bfloat16)
        grad_probs = jnp.einsum(
            "hqd,hkd->hqk", grad_groups, value_groups, preferred_element_type=jnp.float32
        )
        row_dot = jnp.sum(probs * grad_probs, axis=-1, keepdims=True)
        grad_scores = (probs * (grad_probs - row_dot)).astype(jnp.bfloat16)
        grad_query_groups = (
            jnp.einsum("hqk,hkd->hqd", grad_scores, key_groups, preferred_element_type=jnp.float32)
            * score_scale
        )
        grad_key_groups = (
            jnp.einsum(
                "hqk,hqd->hkd", grad_scores, query_groups, preferred_element_type=jnp.float32
            )
            * score_scale
        )
        grad_value_groups = jnp.einsum(
            "hqk,hqd->hkd", probs_again, grad_groups, preferred_element_type=jnp.float32
        )
        key_part, value_part = (
            lax.psum_scatter(
                keys_from_groups(grad_key_groups), "ctx", scatter_dimension=0, tiled=True
            ),
            lax.psum_scatter(
                keys_from_groups(grad_value_groups), "ctx", scatter_dimension=0, tiled=True
            ),
        )
        grad_query = (
            rotate(
                from_groups(grad_query_groups, local_len).reshape(local_len, -1, HEAD_SIZE),
                cos_table,
                -sin_table,
            )
            .reshape(local_len, -1)
            .astype(jnp.bfloat16)
        )
        grad_key = (
            rotate(key_part.reshape(local_len, -1, HEAD_SIZE), cos_table, -sin_table)
            .reshape(local_len, -1)
            .astype(jnp.bfloat16)
        )
        grad_value = value_part.astype(jnp.bfloat16)
        grad_attn_in = (
            dot_rows(grad_query, query_full)
            + dot_rows(grad_key, key_full)
            + dot_rows(grad_value, value_full)
        )
        grad_lower, gain_one_part = norm_backward(grad_attn_in, normed_one, inverse_one, gain_one)
        input_grads.append(grad_hidden + grad_lower)
        batch_row_list = (
            attn_in,
            grad_query,
            grad_key,
            grad_value,
            attn_out,
            merge_in,
            feed_in,
            grad_gate,
            grad_up,
            activated,
            down_in,
        )
        kept_rows.append(batch_row_list)
        gain_one_sum = gain_one_part if gain_one_sum is None else gain_one_sum + gain_one_part
        gain_two_sum = gain_two_part if gain_two_sum is None else gain_two_sum + gain_two_part
    stacked = tuple(
        (jnp.concatenate([entry[member] for entry in kept_rows], axis=0) for member in range(11))
    )
    attention_sums = lax.psum_scatter(
        attention_terms(gain_one_sum, stacked, gain_two_sum),
        ("dp", "ctx"),
        scatter_dimension=0,
        tiled=True,
    )
    feed_sum = lax.psum_scatter(
        feed_builder(stacked, weight_rows * lax.axis_size(("dp", "ctx"))),
        ("dp", "ctx"),
        scatter_dimension=0,
        tiled=True,
    )
    first_total, query_total, key_total, value_total, merge_total, second_total = attention_sums
    feed_width = gate_weight.shape[1]
    return (
        jnp.stack(outputs),
        jnp.stack(input_grads),
        first_total,
        query_total,
        key_total,
        value_total,
        merge_total,
        second_total,
        feed_sum[:, :feed_width],
        feed_sum[:, feed_width : 2 * feed_width],
        feed_sum[:, 2 * feed_width :],
    )


def solution(mesh):
    in_specs = (
        P("dp", "ctx", None),
        P("dp", None),
        P("dp", "ctx", None),
        P(("dp", "ctx")),
        P(("dp", "ctx"), None),
        P(("dp", "ctx"), None),
        P(("dp", "ctx"), None),
        P(("dp", "ctx"), None),
        P(("dp", "ctx")),
        P(("dp", "ctx"), None),
        P(("dp", "ctx"), None),
        P(("dp", "ctx"), None),
    )
    out_specs = (
        P("dp", "ctx", None),
        P("dp", "ctx", None),
        P(("dp", "ctx")),
        P(("dp", "ctx"), None),
        P(("dp", "ctx"), None),
        P(("dp", "ctx"), None),
        P(("dp", "ctx"), None),
        P(("dp", "ctx")),
        P(("dp", "ctx"), None),
        P(("dp", "ctx"), None),
        P(("dp", "ctx"), None),
    )
    return jax.shard_map(body, mesh=mesh, in_specs=in_specs, out_specs=out_specs, check_vma=False)
```

profile of v0, /device:TPU:0, one launch (start us, length us, event | category | flops | bytes accessed | tf_op | source)
XLA Modules:
  0.0 4241.7 jit_solution(3570470800718138556)
XLA Ops:
  10.4 42.1 all-reduce.5
  78.1 50.0 %all-gather.14.cloned.1.call-done = bf16[2048,512]{1,0:T(8,128)(2,1)} async-done(((bf16[64,512]{1,0:T(8,128)(2,1)}), bf16[2048,512]{1,0:T(8,128)(2,1)}) %all-gather.14.cloned.1.call-update) | async-done | bytes 2097168 | tf_op jit(solution)/shard_map/all_gather | solution.py:137
  158.4 26.6 all-gather.32.cloned.1.call-done
  187.3 78.0 %all-gather.12.cloned.1.call-done = bf16[2048,2048]{1,0:T(8,128)(2,1)} async-done(((bf16[64,2048]{1,0:T(8,128)(2,1)}), bf16[2048,2048]{1,0:T(8,128)(2,1)}) %all-gather.12.cloned.1.call-update) | async-done | bytes 8388624 | tf_op jit(solution)/shard_map/all_gather | solution.py:136
  412.9 185.5 %all-gather.26.cloned.1.call-done = bf16[2048,8192]{1,0:T(8,128)(2,1)} async-done(((bf16[64,8192]{1,0:T(8,128)(2,1)}), bf16[2048,8192]{1,0:T(8,128)(2,1)}) %all-gather.26.cloned.1.call-update) | async-done | bytes 33554448 | tf_op jit(solution)/shard_map/all_gather | solution.py:144
  616.5 177.7 %all-gather.24.cloned.1.call-done = bf16[2048,8192]{1,0:T(8,128)(2,1)} async-done(((bf16[64,8192]{1,0:T(8,128)(2,1)}), bf16[2048,8192]{1,0:T(8,128)(2,1)}) %all-gather.24.cloned.1.call-update) | async-done | bytes 33554448 | tf_op jit(solution)/shard_map/all_gather | solution.py:143
  812.0 178.0 %all-gather.28.cloned.1.call-done = bf16[2048,8192]{1,0:T(8,128)(2,1)} async-done(((bf16[64,8192]{1,0:T(8,128)(2,1)}), bf16[2048,8192]{1,0:T(8,128)(2,1)}) %all-gather.28.cloned.1.call-update) | async-done | bytes 33554448 | tf_op jit(solution)/shard_map/all_gather | solution.py:145
  990.0 28.4 multiply_convert_fusion.4
  1088.7 28.8 multiply_convert_fusion.2
  1134.4 19.3 multiply_reduce_fusion.2
  1211.7 23.7 multiply_reduce_fusion
  1235.5 30.0 multiply_convert_fusion
  1275.8 23.5 multiply_reduce_fusion.1
  1299.4 29.7 multiply_convert_fusion.1
  1363.1 82.9 %fusion.2 = f32[3,8192,2048]{2,1,0:T(8,128)} fusion(bf16[512,1,8192]{2,0,1:T(8,128)(2,1)} %maximum_bitcast_fusion.2, bf16[512,1,8192]{2,0,1:T(8,128)(2,1)} %maximum_bitcast_fusion.1, bf16[512,1,8192]{2,0,1:T(8,128)(2,1)} %maximum_bitcast_fusion, bf16[512,1,2048]{2,0,1:T(8,128)(2,1)S(1)} %copy-done.35, bf16[512,1,2048]{2,0,1:T(8,128)(2,1)} %maximum_bitcast_fusion.3), kind=kOutput, calls=%fused_computation.12 | convolution fusion | flops 51571064832 | bytes 230686720 | tf_op jit(solution)/shard_map/tjr,tjf->rjf/dot_general | solution.py:106
  1446.0 193.9 %copy.112 = f32[2048,24576]{1,0:T(8,128)} copy(f32[2048,24576]{0,1:T(8,128)} %bitcast.74) | data formatting | bytes 402653184 | tf_op jit(solution)/shard_map/reshape | solution.py:107
  1712.7 24.1 fusion.34
  1736.8 24.7 fusion.33
  1787.4 38.5 all-reduce.4
  1840.2 1389.0 %reduce-scatter.26.cloned.1.call-done = f32[64,24576]{1,0:T(8,128)} async-done(((f32[2048,24576]{1,0:T(8,128)}), f32[64,24576]{1,0:T(8,128)}) %reduce-scatter.26.cloned.1.call-update) | async-done | bytes 6291472 | tf_op jit(solution)/shard_map/reduce_scatter | solution.py:302
  3234.9 137.4 %reduce-scatter.22.cloned.1.call-done = f32[64,512]{1,0:T(8,128)} async-done(((f32[2048,512]{1,0:T(8,128)}), f32[64,512]{1,0:T(8,128)}) %reduce-scatter.22.cloned.1.call-update) | async-done | bytes 131088 | tf_op jit(solution)/shard_map/reduce_scatter | solution.py:296
  3372.3 141.8 %reduce-scatter.20.cloned.1.call-done = f32[64,512]{1,0:T(8,128)} async-done(((f32[2048,512]{1,0:T(8,128)}), f32[64,512]{1,0:T(8,128)}) %reduce-scatter.20.cloned.1.call-update) | async-done | bytes 131088 | tf_op jit(solution)/shard_map/reduce_scatter | solution.py:296
  3514.1 358.7 %reduce-scatter.24.cloned.1.call-done = f32[64,2048]{1,0:T(8,128)} async-done(((f32[2048,2048]{1,0:T(8,128)}), f32[64,2048]{1,0:T(8,128)}) %reduce-scatter.24.cloned.1.call-update) | async-done | bytes 524304 | tf_op jit(solution)/shard_map/reduce_scatter | solution.py:296
  3872.7 361.8 %reduce-scatter.18.cloned.1.call-done = f32[64,2048]{1,0:T(8,128)} async-done(((f32[2048,2048]{1,0:T(8,128)}), f32[64,2048]{1,0:T(8,128)}) %reduce-scatter.18.cloned.1.call-update) | async-done | bytes 524304 | tf_op jit(solution)/shard_map/reduce_scatter | solution.py:296
  (339 shorter events, 551.8 us)
Async XLA Ops:
  7.2 62.9 %all-gather.18.cloned.1.call-start = ((), (), s32[]{:S(2)}) async-start(), calls=%async_computation.12 | async-start | bytes 2162688 | tf_op jit(solution)/shard_map/all_gather | solution.py:138
  7.9 120.3 %all-gather.14.cloned.1.call-start = ((), (), s32[]{:S(2)}) async-start(), calls=%async_computation.10 | async-start | bytes 2162688 | tf_op jit(solution)/shard_map/all_gather | solution.py:137
  8.7 147.5 %all-gather.20.cloned.1.call-start = ((), (), s32[]{:S(2)}) async-start(), calls=%async_computation.13 | async-start | bytes 1310720 | tf_op jit(solution)/shard_map/all_gather | solution.py:183
  73.1 112.0 %all-gather.32.cloned.1.call-start = ((), (), s32[]{:S(2)}) async-start(), calls=%async_computation.19 | async-start | bytes 1310720 | tf_op jit(solution)/shard_map/all_gather | solution.py:183
  76.3 189.1 %all-gather.12.cloned.1.call-start = ((), (), s32[]{:S(2)}) async-start(), calls=%async_computation.9 | async-start | bytes 8650752 | tf_op jit(solution)/shard_map/all_gather | solution.py:136
  76.9 215.8 %all-gather.16.cloned.1.call-start = ((), (), s32[]{:S(2)}) async-start(), calls=%async_computation.11 | async-start | bytes 1310720 | tf_op jit(solution)/shard_map/all_gather | solution.py:182
  135.3 202.3 %all-gather.30.cloned.1.call-start = ((), (), s32[]{:S(2)}) async-start(), calls=%async_computation.18 | async-start | bytes 1310720 | tf_op jit(solution)/shard_map/all_gather | solution.py:182
  139.2 262.9 %all-gather.22.cloned.1.call-start = ((), (), s32[]{:S(2)}) async-start(), calls=%async_computation.14 | async-start | bytes 8650752 | tf_op jit(solution)/shard_map/all_gather | solution.py:139
  140.0 458.4 %all-gather.26.cloned.1.call-start = ((), (), s32[]{:S(2)}) async-start(), calls=%async_computation.16 | async-start | bytes 34603008 | tf_op jit(solution)/shard_map/all_gather | solution.py:144
  140.7 653.4 %all-gather.24.cloned.1.call-start = ((), (), s32[]{:S(2)}) async-start(), calls=%async_computation.15 | async-start | bytes 34603008 | tf_op jit(solution)/shard_map/all_gather | solution.py:143
  141.3 848.7 %all-gather.28.cloned.1.call-start = ((), (), s32[]{:S(2)}) async-start(), calls=%async_computation.17 | async-start | bytes 34603008 | tf_op jit(solution)/shard_map/all_gather | solution.py:145
  142.0 1498.0 %reduce-scatter.12.cloned.1.call-start = ((), (), s32[]{:S(2)}) async-start(), calls=%async_computation.21 | async-start | bytes 2621440 | tf_op jit(solution)/shard_map/reduce_scatter | solution.py:251
  142.3 1011.3 %copy-start.64 = (f32[2048]{0:T(1024)}, f32[2048]{0:T(1024)S(1)}, u32[]{:S(2)}) copy-start(f32[2048]{0:T(1024)S(1)} %convert_element_type.202) | copy-start | bytes 24580
  408.4 745.2 %copy-start.68 = (f32[256]{0:T(256)}, f32[256]{0:T(256)S(1)}, u32[]{:S(2)}) copy-start(f32[256]{0:T(256)S(1)} %add_rsqrt_fusion.2) | copy-start | bytes 3076
  412.6 741.0 %copy-start.70 = (f32[256]{0:T(256)}, f32[256]{0:T(256)S(1)}, u32[]{:S(2)}) copy-start(f32[256]{0:T(256)S(1)} %add_rsqrt_fusion) | copy-start | bytes 3076
  412.9 381.3 %copy-start.31 = (bf16[256,2048]{1,0:T(8,128)(2,1)}, bf16[256,2048]{1,0:T(8,128)(2,1)S(1)}, u32[]{:S(2)}) copy-start(bf16[256,2048]{1,0:T(8,128)(2,1)S(1)} %multiply_convert_fusion.9) | copy-start | bytes 3145732
  1192.1 449.1 %reduce-scatter.16.cloned.1.call-start = ((), (), s32[]{:S(2)}) async-start(), calls=%async_computation.23 | async-start | bytes 2621440 | tf_op jit(solution)/shard_map/reduce_scatter | solution.py:251
  1235.4 410.3 %reduce-scatter.14.cloned.1.call-start = ((), (), s32[]{:S(2)}) async-start(), calls=%async_computation.22 | async-start | bytes 2621440 | tf_op jit(solution)/shard_map/reduce_scatter | solution.py:248
  1299.3 348.3 %reduce-scatter.10.cloned.1.call-start = ((), (), s32[]{:S(2)}) async-start(), calls=%async_computation.20 | async-start | bytes 2621440 | tf_op jit(solution)/shard_map/reduce_scatter | solution.py:248
  1363.0 1866.2 %reduce-scatter.26.cloned.1.call-start = ((), (), s32[]{:S(2)}) async-start(), calls=%async_computation.28 | async-start | bytes 207618048 | tf_op jit(solution)/shard_map/reduce_scatter | solution.py:302
  1639.9 1732.4 %reduce-scatter.22.cloned.1.call-start = ((), (), s32[]{:S(2)}) async-start(), calls=%async_computation.26 | async-start | bytes 4325376 | tf_op jit(solution)/shard_map/reduce_scatter | solution.py:296
  1645.6 1868.5 %reduce-scatter.20.cloned.1.call-start = ((), (), s32[]{:S(2)}) async-start(), calls=%async_computation.25 | async-start | bytes 4325376 | tf_op jit(solution)/shard_map/reduce_scatter | solution.py:296
  1652.8 2219.9 %reduce-scatter.24.cloned.1.call-start = ((), (), s32[]{:S(2)}) async-start(), calls=%async_computation.27 | async-start | bytes 17301504 | tf_op jit(solution)/shard_map/reduce_scatter | solution.py:296
  1668.2 2566.4 %reduce-scatter.18.cloned.1.call-start = ((), (), s32[]{:S(2)}) async-start(), calls=%async_computation.24 | async-start | bytes 17301504 | tf_op jit(solution)/shard_map/reduce_scatter | solution.py:296
  (82 other events, 2821.5 us)
Sparse Core Ops, SparseCore 0:
  10.9 59.1 all-gather.17
  72.9 55.2 all-gather.13
  130.6 25.4 all-gather.19
  158.4 26.6 all-gather.31
  187.8 77.5 all-gather.11
  267.6 25.0 all-gather.15
  295.1 26.4 all-gather.29
  324.5 77.5 all-gather.21
  405.0 193.3 all-gather.25
  601.1 192.9 all-gather.23
  797.0 192.9 all-gather.27
  1192.2 33.3 reduce-scatter.11
  1235.5 33.6 reduce-scatter.15
  1299.4 33.2 reduce-scatter.13
  1363.1 32.9 reduce-scatter.9
  1640.0 1589.1 reduce-scatter.25
  3231.9 140.3 reduce-scatter.21
  3375.0 139.0 reduce-scatter.19
  3516.9 355.7 reduce-scatter.23
  3875.4 359.0 reduce-scatter.17
where the time goes:
time: 4250 us; the launch traced here: 4240 us
  waiting for transfers between devices  3140 us (74%)
  matrix products  615 us (14%)
  local copies, waits for them, and re-layouts  247 us (6%)
  other arithmetic  148 us (3%)
  blocking collectives  80.6 us (2%)
    reduce_scatter x1, waiting for transfers between devices, body(): lax.psum_scatter(feed_builder(stacked, weight_rows * lax.axis_size(('dp',...  1390 us
    reduce_scatter x4, waiting for transfers between devices, body(): lax.psum_scatter(attention_terms(gain_one_sum, stacked, gain_two_sum), ('...  1000 us
    reshape x1, local copies, waits for them, and re-layouts, feed_builder(): return term.reshape(row_count, 3 * feed_width)  194 us
    all_gather x1, waiting for transfers between devices, body(): lax.all_gather(up_weight, ('dp', 'ctx'), axis=0, tiled=True)  186 us
    all_gather x1, waiting for transfers between devices, body(): lax.all_gather(down_weight, ('dp', 'ctx'), axis=0, tiled=True)  178 us
    all_gather x1, waiting for transfers between devices, body(): lax.all_gather(gate_weight, ('dp', 'ctx'), axis=0, tiled=True)  178 us
    dot_general x14, matrix products, dot_plain(): return jnp.dot(left, right, preferred_element_type=jnp.float32)  160 us
    dot_general x14, matrix products, dot_rows(): lax.dot_general(left, right, (((1,), (1,)), ((), ())), preferred_element_...  151 us
  transfers between devices with their start and end apart: 20, of which 15 were waited for; matrix products, arithmetic and copies ran while one was open for 19% of the time, Pallas kernels for 0%

commit v1 on v0

v1 whole, which is shorter than its diff:
```python
import functools
import math

import jax
import jax.numpy as jnp
from jax import lax
from jax.experimental import pallas as pl
from jax.experimental.pallas import tpu as pltpu
from jax.sharding import PartitionSpec as P

HEAD_SIZE = 64
LANES = 128
EPS = 1e-05
THETA = 500000.0
QUERY_BLOCK = 256
F32 = jnp.float32
BF16 = jnp.bfloat16

NN = (((1,), (0,)), ((), ()))
NT = (((1,), (1,)), ((), ()))
TN = (((0,), (0,)), ((), ()))


def dot(left, right, dims=NN, out=F32):
    return lax.dot_general(left, right, dims, preferred_element_type=F32).astype(out)


def swap(block, bits):
    size = lax.axis_size("ctx")
    return lax.ppermute(block, "ctx", [(i, i ^ bits) for i in range(size)])


def square():
    return lax.axis_size("ctx") == 4


def gather_rows(own):
    if not square():
        return lax.all_gather(own, "ctx", axis=0, tiled=True)
    half = own.shape[0] // 2
    from_one, from_two = swap(own, 1), swap(own, 2)
    across_low = swap(from_one[:half], 2)
    across_high = swap(from_two[half:], 1)
    return jnp.concatenate([own, from_one, from_two, across_low, across_high], axis=0)


def scatter_rows(parts):
    if not square():
        return lax.psum_scatter(parts, "ctx", scatter_dimension=0, tiled=True).astype(F32)
    rows = parts.shape[0] // 4
    half = rows // 2
    block = parts.reshape(4, rows, -1)
    low = swap(block[3, :half], 1)
    high = swap(block[3, half:], 2)
    for_one = jnp.concatenate(
        [block[1, :half], (block[1, half:].astype(F32) + high.astype(F32)).astype(BF16)], axis=0
    )
    for_two = jnp.concatenate(
        [(block[2, :half].astype(F32) + low.astype(F32)).astype(BF16), block[2, half:]], axis=0
    )
    return (
        block[0].astype(F32) + swap(for_one, 1).astype(F32) + swap(for_two, 2).astype(F32)
    )


def exchange(block_for):
    size = lax.axis_size("ctx")
    rank = lax.axis_index("ctx")
    if not square():
        stacked = jnp.stack([block_for(t) for t in range(size)])
        return lax.all_to_all(stacked, "ctx", 0, 0)
    received = [block_for(rank)] + [swap(block_for(rank ^ m), m) for m in (1, 2, 3)]
    out = jnp.zeros((4,) + received[0].shape, received[0].dtype)
    for member, value in enumerate(received):
        out = lax.dynamic_update_index_in_dim(out, value, rank ^ member, 0)
    return out


def gather_columns(block_for):
    mine = exchange(block_for)
    mine = mine.reshape(-1, mine.shape[-1])
    return lax.all_gather(mine, "dp", axis=0, tiled=True)


def scatter_columns(grads):
    size = lax.axis_size("ctx")
    summed = lax.psum_scatter(grads, "dp", scatter_dimension=0, tiled=True)
    rows = summed.shape[0] // size
    return exchange(lambda t: lax.dynamic_slice_in_dim(summed, t * rows, rows, axis=0))


def swap_halves(rows):
    lane = lax.broadcasted_iota(jnp.int32, rows.shape, 1)
    return jnp.where(
        lane % HEAD_SIZE < HEAD_SIZE // 2,
        pltpu.roll(rows, LANES - HEAD_SIZE // 2, 1),
        pltpu.roll(rows, HEAD_SIZE // 2, 1),
    )


def both_halves(rows, half):
    lane = lax.broadcasted_iota(jnp.int32, rows.shape, 1)
    kept = jnp.where(lane // HEAD_SIZE == half, rows.astype(F32), 0.0)
    return (kept + pltpu.roll(kept, HEAD_SIZE, 1)).astype(BF16)


def two_heads(rows):
    lane = lax.broadcasted_iota(jnp.int32, rows.shape, 1)
    wide = rows.astype(F32)
    first = jnp.where(lane < HEAD_SIZE, wide, 0.0)
    second = jnp.where(lane < HEAD_SIZE, 0.0, wide)
    return jnp.concatenate([first, second], axis=0).astype(BF16)


def visible(size):
    key = lax.broadcasted_iota(jnp.int32, (size, 2 * size), 0)
    query = lax.broadcasted_iota(jnp.int32, (size, 2 * size), 1) % size
    return key <= query


def attention_forward_kernel(
    slot_ref, q_ref, k_ref, v_ref, cos_ref, sin_ref,
    out_ref, queries_ref, keys_ref, values_ref, total_ref, key_both, value_turned,
    *, span, pairs_of_head, pairs_of_block
):
    pair = pl.program_id(0)
    length = q_ref.shape[0]
    spans = length // span
    block = QUERY_BLOCK

    def place(index):
        return pl.ds(pl.multiple_of(slot_ref[index] * span, span), span)

    def turned(source, index):
        here = slice(index * span, (index + 1) * span)
        rows = source[place(index), :]
        return rows * cos_ref[here, :] + swap_halves(rows) * sin_ref[here, :]

    for index in range(spans):
        here = slice(index * span, (index + 1) * span)
        queries_ref[here, :] = turned(q_ref, index).astype(BF16)

    @pl.when(pair % pairs_of_block == 0)
    def _():
        for index in range(spans):
            here = slice(index * span, (index + 1) * span)
            keys_ref[here, :] = turned(k_ref, index).astype(BF16)
            values_ref[here, :] = v_ref[place(index), :].astype(BF16)

    @pl.when(pair % pairs_of_head == 0)
    def _():
        half = (pair // pairs_of_head) % 2
        key_both[...] = both_halves(keys_ref[...], half)
        value_both = both_halves(values_ref[...], half)
        value_turned[...] = value_both.astype(F32).T[:HEAD_SIZE].astype(BF16)

    mask = visible(block)
    for index in range(length // block):
        low, high = index * block, (index + 1) * block
        wide = two_heads(queries_ref[low:high, :] * jnp.asarray(HEAD_SIZE**-0.5, BF16))
        diagonal = jnp.where(mask, dot(key_both[low:high, :], wide, NT), -1e30)
        top = jnp.max(diagonal, axis=0, keepdims=True)
        if index:
            before = dot(key_both[:low, :], wide, NT)
            top = jnp.maximum(top, jnp.max(before, axis=0, keepdims=True))
        near = jnp.exp(diagonal - top)
        total = jnp.sum(near, axis=0, keepdims=True)
        attended = dot(value_turned[:, low:high], near.astype(BF16))
        if index:
            far = jnp.exp(before - top)
            total = total + jnp.sum(far, axis=0, keepdims=True)
            attended = attended + dot(value_turned[:, :low], far.astype(BF16))
        total_ref[0, index : index + 1, :] = top + jnp.log(total)
        attended = attended / total
        rows = jnp.concatenate([attended[:, :block], attended[:, block:]], axis=0).T.astype(BF16)
        for part in range(block // span):
            out_ref[place(index * (block // span) + part), :] = rows[
                part * span : (part + 1) * span
            ]


def attention_backward_kernel(
    slot_ref, queries_ref, keys_ref, values_ref, total_ref, grad_ref, cos_ref, sin_ref,
    grad_q_ref, grad_k_ref, grad_v_ref, key_both, value_both, key_turned, key_sum, value_sum,
    *, span, pairs_of_head
):
    pair = pl.program_id(0)
    length = queries_ref.shape[0]
    spans = length // span
    block = QUERY_BLOCK
    each = block // span
    half = (pair // pairs_of_head) % 2

    def place(index):
        return pl.ds(pl.multiple_of(slot_ref[index] * span, span), span)

    def turned_back(rows, index):
        here = slice(index * span, (index + 1) * span)
        return rows * cos_ref[here, :] - swap_halves(rows) * sin_ref[here, :]

    @pl.when(pair % pairs_of_head == 0)
    def _():
        key_both[...] = both_halves(keys_ref[...], half)
        value_both[...] = both_halves(values_ref[...], half)
        key_turned[...] = key_both[...].astype(F32).T[:HEAD_SIZE].astype(BF16)
        key_sum[...] = jnp.zeros_like(key_sum)
        value_sum[...] = jnp.zeros_like(value_sum)

    mask = visible(block)
    for index in range(length // block):
        low, high = index * block, (index + 1) * block
        wide = two_heads(queries_ref[low:high, :] * jnp.asarray(HEAD_SIZE**-0.5, BF16))
        grad = two_heads(
            jnp.concatenate(
                [grad_ref[place(index * each + part), :] for part in range(each)], axis=0
            )
        )
        total = total_ref[0, index : index + 1, :]
        ranges = [(low, high)] + ([(0, low)] if index else [])
        probs, grad_probs, row_dot = [], [], 0.0
        for start, stop in ranges:
            scores = dot(key_both[start:stop, :], wide, NT)
            if start == low:
                scores = jnp.where(mask, scores, -1e30)
            prob = jnp.exp(scores - total)
            grad_prob = dot(value_both[start:stop, :], grad, NT)
            row_dot = row_dot + jnp.sum(prob * grad_prob, axis=0, keepdims=True)
            probs.append(prob)
            grad_probs.append(grad_prob)
        turned = 0.0
        for (start, stop), prob, grad_prob in zip(ranges, probs, grad_probs):
            grad_score = (prob * (grad_prob - row_dot)).astype(BF16)
            value_sum[start:stop, :] += dot(prob.astype(BF16), grad)
            key_sum[start:stop, :] += dot(grad_score, wide)
            turned = turned + dot(key_turned[:, start:stop], grad_score)
        turned = turned * HEAD_SIZE**-0.5
        rows = jnp.concatenate([turned[:, :block], turned[:, block:]], axis=0).T
        for part in range(each):
            at = index * each + part
            grad_q_ref[place(at), :] = turned_back(
                rows[part * span : (part + 1) * span], at
            ).astype(BF16)

    @pl.when(pair % pairs_of_head == pairs_of_head - 1)
    def _():
        for index in range(spans):
            here = slice(index * span, (index + 1) * span)
            key_rows, value_rows = key_sum[here, :], value_sum[here, :]
            key_rows = turned_back(key_rows + pltpu.roll(key_rows, HEAD_SIZE, 1), index)
            value_rows = value_rows + pltpu.roll(value_rows, HEAD_SIZE, 1)
            lane = lax.broadcasted_iota(jnp.int32, key_rows.shape, 1)
            for target, rows in ((grad_k_ref, key_rows), (grad_v_ref, value_rows)):
                old = target[place(index), :].astype(F32)
                keep = (lane < HEAD_SIZE) & (half == 1)
                target[place(index), :] = jnp.where(keep, old, rows).astype(BF16)


def attention_sizes(query_width, group_size):
    pairs = query_width // LANES
    pairs_of_head = group_size // 2
    return pairs, pairs_of_head, 2 * pairs_of_head


def attention_forward(qkv, slots, cos_lanes, sin_lanes, query_width, key_width, group_size):
    length = qkv.shape[0]
    pairs, pairs_of_head, pairs_of_block = attention_sizes(query_width, group_size)
    key_at, value_at = query_width // LANES, (query_width + key_width) // LANES
    tile = (length, LANES)
    by_pair = pl.BlockSpec(tile, lambda p, s: (0, p))
    by_block = pl.BlockSpec(tile, lambda p, s: (0, p // pairs_of_block))
    whole = pl.BlockSpec(tile, lambda p, s: (0, 0))
    blocks = length // QUERY_BLOCK
    work = 2 * query_width * length * length
    return pl.pallas_call(
        functools.partial(
            attention_forward_kernel,
            span=length // slots.shape[0],
            pairs_of_head=pairs_of_head,
            pairs_of_block=pairs_of_block,
        ),
        grid_spec=pltpu.PrefetchScalarGridSpec(
            num_scalar_prefetch=1,
            grid=(pairs,),
            in_specs=[
                by_pair,
                pl.BlockSpec(tile, lambda p, s: (0, key_at + p // pairs_of_block)),
                pl.BlockSpec(tile, lambda p, s: (0, value_at + p // pairs_of_block)),
                whole,
                whole,
            ],
            out_specs=[
                by_pair,
                by_pair,
                by_block,
                by_block,
                pl.BlockSpec((1, blocks, 2 * QUERY_BLOCK), lambda p, s: (p, 0, 0)),
            ],
            scratch_shapes=[pltpu.VMEM(tile, BF16), pltpu.VMEM((HEAD_SIZE, length), BF16)],
        ),
        out_shape=[
            jax.ShapeDtypeStruct((length, query_width), BF16),
            jax.ShapeDtypeStruct((length, query_width), BF16),
            jax.ShapeDtypeStruct((length, key_width), BF16),
            jax.ShapeDtypeStruct((length, key_width), BF16),
            jax.ShapeDtypeStruct((pairs, blocks, 2 * QUERY_BLOCK), F32),
        ],
        compiler_params=pltpu.CompilerParams(
            dimension_semantics=("arbitrary",), vmem_limit_bytes=48 << 20
        ),
        cost_estimate=pl.CostEstimate(
            flops=8 * work, bytes_accessed=8 << 20, transcendentals=work // 128
        ),
        name="attention_forward",
    )(slots, qkv, qkv, qkv, cos_lanes, sin_lanes)


def attention_backward(kept, grad, slots, cos_lanes, sin_lanes, group_size):
    queries, keys, values, totals = kept
    length, query_width = queries.shape
    key_width = keys.shape[1]
    pairs, pairs_of_head, pairs_of_block = attention_sizes(query_width, group_size)
    tile = (length, LANES)
    by_pair = pl.BlockSpec(tile, lambda p, s: (0, p))
    by_block = pl.BlockSpec(tile, lambda p, s: (0, p // pairs_of_block))
    whole = pl.BlockSpec(tile, lambda p, s: (0, 0))
    blocks = length // QUERY_BLOCK
    work = 2 * query_width * length * length
    return pl.pallas_call(
        functools.partial(
            attention_backward_kernel, span=length // slots.shape[0], pairs_of_head=pairs_of_head
        ),
        grid_spec=pltpu.PrefetchScalarGridSpec(
            num_scalar_prefetch=1,
            grid=(pairs,),
            in_specs=[
                by_pair,
                by_block,
                by_block,
                pl.BlockSpec((1, blocks, 2 * QUERY_BLOCK), lambda p, s: (p, 0, 0)),
                by_pair,
                whole,
                whole,
            ],
            out_specs=[by_pair, by_block, by_block],
            scratch_shapes=[
                pltpu.VMEM(tile, BF16),
                pltpu.VMEM(tile, BF16),
                pltpu.VMEM((HEAD_SIZE, length), BF16),
                pltpu.VMEM(tile, F32),
                pltpu.VMEM(tile, F32),
            ],
        ),
        out_shape=[
            jax.ShapeDtypeStruct((length, query_width), BF16),
            jax.ShapeDtypeStruct((length, key_width), BF16),
            jax.ShapeDtypeStruct((length, key_width), BF16),
        ],
        compiler_params=pltpu.CompilerParams(
            dimension_semantics=("arbitrary",), vmem_limit_bytes=48 << 20
        ),
        cost_estimate=pl.CostEstimate(
            flops=20 * work, bytes_accessed=8 << 20, transcendentals=work // 128
        ),
        name="attention_backward",
    )(slots, queries, keys, values, totals, grad, cos_lanes, sin_lanes)


def feed_kernel(feed_ref, down_in_ref, pair_ref, down_ref, activated_ref, grads_ref):
    tile = down_ref.shape[1]
    both = dot(feed_ref[...], pair_ref[...])
    grad_act = dot(down_in_ref[...], down_ref[...])
    gate, up = both[:, :tile], both[:, tile:]
    sig = jax.nn.sigmoid(gate)
    silu = gate * sig
    activated_ref[...] = (silu * up).astype(BF16)
    grads_ref[:, :tile] = (grad_act * up * sig * (1.0 + gate * (1.0 - sig))).astype(BF16)
    grads_ref[:, tile:] = (grad_act * silu).astype(BF16)


def feed_middle(feed_in, down_in, weights, width, tile):
    rows, depth = feed_in.shape
    tiles = width // tile
    work = rows * depth * width
    return pl.pallas_call(
        feed_kernel,
        grid=(tiles,),
        in_specs=[
            pl.BlockSpec((rows, depth), lambda j: (0, 0), pipeline_mode=pl.Buffered(1)),
            pl.BlockSpec((rows, depth), lambda j: (0, 0), pipeline_mode=pl.Buffered(1)),
            pl.BlockSpec((depth, 2 * tile), lambda j: (0, j)),
            pl.BlockSpec((depth, tile), lambda j: (0, 2 * tiles + j)),
        ],
        out_specs=[
            pl.BlockSpec((rows, tile), lambda j: (0, j)),
            pl.BlockSpec((rows, 2 * tile), lambda j: (0, j)),
        ],
        out_shape=[
            jax.ShapeDtypeStruct((rows, width), BF16),
            jax.ShapeDtypeStruct((rows, 2 * width), BF16),
        ],
        compiler_params=pltpu.CompilerParams(
            dimension_semantics=("arbitrary",), vmem_limit_bytes=56 << 20
        ),
        cost_estimate=pl.CostEstimate(
            flops=6 * work,
            bytes_accessed=2 * (2 * rows * depth + 3 * depth * width + 3 * rows * width),
            transcendentals=rows * width,
        ),
        name="feed_middle",
    )(feed_in, down_in, weights, weights)


def norm_forward(values):
    inverse_rms = lax.rsqrt(jnp.mean(values * values, axis=-1, keepdims=True) + EPS)
    return (values * inverse_rms, inverse_rms)


def norm_backward(grad_normed, normed, inverse_rms, gain):
    grad_hat = grad_normed * gain
    grad_input = inverse_rms * (
        grad_hat - normed * jnp.mean(grad_hat * normed, axis=-1, keepdims=True)
    )
    return (grad_input, jnp.sum(grad_normed * normed, axis=0))


def rope_lanes(length):
    half = HEAD_SIZE // 2
    frequency = jnp.exp(
        jnp.arange(half, dtype=F32) * (-2.0 * math.log(THETA) / HEAD_SIZE)
    )
    angles = jnp.arange(length, dtype=jnp.int32).astype(F32)[:, None] * frequency[None, :]
    cosine, sine = jnp.cos(angles), jnp.sin(angles)
    return (
        jnp.concatenate([cosine] * 4, axis=1),
        jnp.concatenate([-sine, sine, -sine, sine], axis=1),
    )


def pad_columns(array, width):
    return jnp.pad(array, ((0, 0), (0, width - array.shape[1])))


def body(
    tokens, span_order, out_grad, first_gain, query_weight, key_matrix, value_matrix,
    merge_weight, second_gain, gate_weight, up_weight, down_weight,
):
    seqs, own_rows, depth = tokens.shape
    ctx = lax.axis_size("ctx")
    rank = lax.axis_index("ctx")
    length = own_rows * ctx
    spans = span_order.shape[1]
    weight_rows = gate_weight.shape[0]
    group_size = query_weight.shape[1] // key_matrix.shape[1]
    query_width = query_weight.shape[1] // ctx
    own_key_width = key_matrix.shape[1] // ctx
    key_width = -(-own_key_width // LANES) * LANES
    feed_width = gate_weight.shape[1] // ctx
    chunks = 2
    chunk = feed_width // chunks
    tile = min(512, chunk)

    def columns(weight, t, width, at=0):
        return lax.dynamic_slice_in_dim(weight, t * (weight.shape[1] // ctx) + at, width, axis=1)

    gain_columns = pad_columns(jnp.stack([first_gain, second_gain], axis=1), LANES)

    def projections_for(t):
        return jnp.concatenate(
            [
                columns(query_weight, t, query_width),
                pad_columns(columns(key_matrix, t, own_key_width), key_width),
                pad_columns(columns(value_matrix, t, own_key_width), key_width),
                gain_columns,
            ],
            axis=1,
        )

    def feed_for(part):
        def of(t):
            pieces = []
            for start in range(part * chunk, (part + 1) * chunk, tile):
                pieces += [
                    columns(gate_weight, t, tile, start),
                    columns(up_weight, t, tile, start),
                ]
            pieces.append(columns(down_weight, t, chunk, part * chunk))
            return jnp.concatenate(pieces, axis=1)

        return of

    projections = gather_columns(projections_for)
    merge = gather_columns(lambda t: columns(merge_weight, t, query_width))
    feeds = [gather_columns(feed_for(part)) for part in range(chunks)]

    qkv_width = query_width + 2 * key_width
    qkv_weight = projections[:, :qkv_width]
    gains = projections[:, qkv_width : qkv_width + 2].astype(F32)
    gain_one, gain_two = gains[:, 0], gains[:, 1]

    slots = jnp.argsort(span_order, axis=1).astype(jnp.int32)
    if square():
        slots = ((slots // 2) ^ rank) * 2 + slots % 2
    cos_lanes, sin_lanes = rope_lanes(length)

    inputs = [tokens[s].astype(F32) for s in range(seqs)]
    normed_one, inverse_one, attn_in = [], [], []
    for s in range(seqs):
        normed, inverse = norm_forward(inputs[s])
        normed_one.append(normed)
        inverse_one.append(inverse)
        attn_in.append(gather_rows((normed * gain_one).astype(BF16)))
    down_in = [gather_rows(out_grad[s]) for s in range(seqs)]
    attn_out, kept, hidden_one = [], [], []
    for s in range(seqs):
        qkv = dot(attn_in[s], qkv_weight)
        attended, *rest = attention_forward(
            qkv, slots[s], cos_lanes, sin_lanes, query_width, key_width, group_size
        )
        attn_out.append(attended)
        kept.append(rest)
        hidden_one.append(inputs[s] + scatter_rows(dot(attended, merge, NT, BF16)))

    normed_two, inverse_two, feed_in = [], [], []
    for s in range(seqs):
        normed, inverse = norm_forward(hidden_one[s])
        normed_two.append(normed)
        inverse_two.append(inverse)
        feed_in.append(gather_rows((normed * gain_two).astype(BF16)))
    middle = [
        [feed_middle(feed_in[s], down_in[s], feeds[part], chunk, tile) for part in range(chunks)]
        for s in range(seqs)
    ]
    blocks, grad_hidden, merge_in, gain_two_sum = [], [], [], 0.0
    for s in range(seqs):
        grad_feed_in = sum(
            dot(middle[s][part][1], feeds[part][:, : 2 * chunk], NT) for part in range(chunks)
        )
        grad_middle, gain_part = norm_backward(
            scatter_rows(grad_feed_in.astype(BF16)), normed_two[s], inverse_two[s], gain_two
        )
        gain_two_sum = gain_two_sum + gain_part
        grad_hidden.append(out_grad[s].astype(F32) + grad_middle)
        merge_in.append(gather_rows(grad_hidden[s].astype(BF16)))
    feed_tokens = jnp.concatenate(feed_in, axis=0)
    down_tokens = jnp.concatenate(down_in, axis=0)
    feed_sums = []
    for part in range(chunks):
        activated = jnp.concatenate([middle[s][part][0] for s in range(seqs)], axis=0)
        grads = jnp.concatenate([middle[s][part][1] for s in range(seqs)], axis=0)
        grads = jnp.concatenate(
            [dot(feed_tokens, grads, TN, BF16), dot(down_tokens, activated, TN, BF16)], axis=1
        )
        feed_sums.append(scatter_columns(grads))
    for s in range(seqs):
        branch = sum(
            dot(middle[s][part][0], feeds[part][:, 2 * chunk :], NT) for part in range(chunks)
        )
        blocks.append((hidden_one[s] + scatter_rows(branch.astype(BF16))).astype(BF16))

    grad_qkv, input_grad, gain_one_sum = [], [], 0.0
    for s in range(seqs):
        grad_attn = dot(merge_in[s], merge, NN, BF16)
        parts = attention_backward(
            kept[s], grad_attn, slots[s], cos_lanes, sin_lanes, group_size
        )
        grad_qkv.append(jnp.concatenate(parts, axis=1))
        grad_lower, gain_part = norm_backward(
            scatter_rows(dot(grad_qkv[s], qkv_weight, NT, BF16)),
            normed_one[s],
            inverse_one[s],
            gain_one,
        )
        gain_one_sum = gain_one_sum + gain_part
        input_grad.append(grad_hidden[s] + grad_lower)
    attention_grads = jnp.concatenate(
        [
            dot(jnp.concatenate(attn_in, axis=0), jnp.concatenate(grad_qkv, axis=0), TN, BF16),
            dot(jnp.concatenate(merge_in, axis=0), jnp.concatenate(attn_out, axis=0), TN, BF16),
            pad_columns(jnp.stack([gain_one_sum, gain_two_sum], axis=1).astype(BF16), LANES),
        ],
        axis=1,
    )
    attention_sums = scatter_columns(attention_grads)

    def spread(pieces):
        return pieces.astype(F32).transpose(1, 0, 2).reshape(pieces.shape[1], -1)

    def of_feed(kind):
        pieces = []
        for part in range(chunks):
            for at in range(chunk // tile):
                start = 2 * chunk + at * tile if kind == 2 else (2 * at + kind) * tile
                pieces.append(feed_sums[part][:, :, start : start + tile])
        return spread(jnp.concatenate(pieces, axis=2))

    key_at, value_at = query_width, query_width + key_width
    merge_at, gain_at = qkv_width, qkv_width + query_width
    gain_totals = jnp.sum(attention_sums[:, :, gain_at : gain_at + 2].astype(F32), axis=0)
    return (
        jnp.stack(blocks),
        jnp.stack(input_grad),
        gain_totals[:, 0],
        spread(attention_sums[:, :, :query_width]),
        spread(attention_sums[:, :, key_at : key_at + own_key_width]),
        spread(attention_sums[:, :, value_at : value_at + own_key_width]),
        spread(attention_sums[:, :, merge_at : merge_at + query_width]),
        gain_totals[:, 1],
        of_feed(0),
        of_feed(1),
        of_feed(2),
    )


def solution(mesh):
    rows = P(("dp", "ctx"), None)
    vector = P(("dp", "ctx"))
    acts = P("dp", "ctx", None)
    in_specs = (
        acts, P("dp", None), acts, vector, rows, rows, rows, rows, vector, rows, rows, rows,
    )
    out_specs = (acts, acts, vector, rows, rows, rows, rows, vector, rows, rows, rows)
    return jax.shard_map(body, mesh=mesh, in_specs=in_specs, out_specs=out_specs, check_vma=False)
```

time: 4250 us -> 1230 us (0.29)
  waiting for transfers between devices: 3140 us -> 539 us
  matrix products: 615 us -> 202 us
  Pallas kernels: 0 us -> 158 us
  local copies, waits for them, and re-layouts: 247 us -> 132 us
  starting transfers between devices: 1.15 us -> 87.1 us
  blocking collectives: 80.6 us -> 0 us
  other arithmetic: 148 us -> 84.3 us
    reduce_scatter x9 -> x3, waiting for transfers between devices: 2390 us -> 185 us  [scatter_columns(): summed = lax.psum_scatter(grads, 'dp', scatter_dimension=0, tiled=True)]
    all_gather x11 -> x4, waiting for transfers between devices: 742 us -> 0.01 us  [gather_columns(): return lax.all_gather(mine, 'dp', axis=0, tiled=True)]
    dot_general x45 -> x22, matrix products: 615 us -> 202 us  [dot(): lax.dot_general(left, right, dims, preferred_element_type=F32).astype(out)]
    ppermute x0 -> x85, waiting for transfers between devices: none -> 354 us  [swap(): return lax.ppermute(block, 'ctx', [(i, i ^ bits) for i in range(size)])]
    reshape x7 -> x3, local copies, waits for them, and re-layouts: 197 us -> 4.4 us  [spread(): return pieces.astype(F32).transpose(1, 0, 2).reshape(pieces.shape[1], -1)]
    pallas_call x0 -> x8, Pallas kernels: none -> 158 us  [the longest x4 83.6 us: feed_middle(): pl.pallas_call(feed_kernel, grid=(tiles,), in_specs=[pl.BlockSpec((rows,...]
    ppermute x0 -> x85, starting transfers between devices: none -> 86.8 us  [swap(): return lax.ppermute(block, 'ctx', [(i, i ^ bits) for i in range(size)])]
    unnamed x2 -> x0, blocking collectives: 80.6 us -> none
  transfers between devices with their start and end apart: 20 -> 92, of which waited for: 15 -> 51; matrix products, arithmetic and copies ran while one was open for 19% -> 28% of each run, Pallas kernels for 0% -> 9%
where the time goes in v1:
time: 1230 us; the launch traced here: 1220 us
  waiting for transfers between devices  539 us (44%)
  matrix products  202 us (16%)
  Pallas kernels  158 us (13%)
  local copies, waits for them, and re-layouts  132 us (11%)
  starting transfers between devices  87.1 us (7%)
  other arithmetic  84.3 us (7%)
  between operations  16.6 us (1%)
    ppermute x85, waiting for transfers between devices, swap(): return lax.ppermute(block, 'ctx', [(i, i ^ bits) for i in range(size)])  354 us
    dot_general x22, matrix products, dot(): lax.dot_general(left, right, dims, preferred_element_type=F32).astype(out)  202 us
    reduce_scatter x3, waiting for transfers between devices, scatter_columns(): summed = lax.psum_scatter(grads, 'dp', scatter_dimension=0, tiled=True)  185 us
    ppermute x85, starting transfers between devices, swap(): return lax.ppermute(block, 'ctx', [(i, i ^ bits) for i in range(size)])  86.8 us
    pallas_call x4, Pallas kernels, feed_middle(): pl.pallas_call(feed_kernel, grid=(tiles,), in_specs=[pl.BlockSpec((rows,...  83.6 us
    unnamed x231, local copies, waits for them, and re-layouts  61.7 us
    pallas_call x2, Pallas kernels, attention_backward(): pl.pallas_call(functools.partial(attention_backward_kernel, span=length /...  43 us
    pallas_call x2, Pallas kernels, attention_forward(): pl.pallas_call(functools.partial(attention_forward_kernel, span=length //...  31.4 us
  transfers between devices with their start and end apart: 92, of which 51 were waited for; matrix products, arithmetic and copies ran while one was open for 28% of the time, Pallas kernels for 9%

profile of v1, /device:TPU:0, one launch (start us, length us, event | category | flops | bytes accessed | tf_op | source)
XLA Modules:
  0.0 1218.9 jit_solution(903678695563853620)
XLA Ops:
  69.8 38.1 %collective-permute-done.25 = bf16[64,3072]{1,0:T(8,128)(2,1)S(1)} collective-permute-done((bf16[64,3072]{1,0:T(8,128)(2,1)}, bf16[64,3072]{1,0:T(8,128)(2,1)S(1)}, u32[]{:S(2)}, u32[]{:S(2)}) %collective-permute-start.25) | collective-permute-done | bytes 393248 | tf_op jit(solution)/shard_map/ppermute | solution.py:30
  186.2 15.6 %attention_forward.2 = (bf16[1024,512]{1,0:T(8,128)(2,1)S(1)}, bf16[1024,512]{1,0:T(8,128)(2,1)S(1)}, bf16[1024,128]{1,0:T(8,128)(2,1)S(1)}, bf16[1024,128]{1,0:T(8,128)(2,1)S(1)}, f32[4,4,512]{2,1,0:T(4,128)S(1)}) custom-call(s32[8]{0:T(128)S(1)} %get-tuple-element.75.slot_ref, f32[1024,768]{1,0:T(8,128)} %fusion.80.q_ref.k_ref.v_ref, ...), custom_call_target="tpu_custom_call" | custom-call | flops 8589934592 | bytes 8388608 | tf_op jit(solution)/shard_map/attention_forward/pallas_call | solution.py:274
  231.7 15.8 %attention_forward.3 = (bf16[1024,512]{1,0:T(8,128)(2,1)S(1)}, bf16[1024,512]{1,0:T(8,128)(2,1)S(1)}, bf16[1024,128]{1,0:T(8,128)(2,1)S(1)}, bf16[1024,128]{1,0:T(8,128)(2,1)S(1)}, f32[4,4,512]{2,1,0:T(4,128)S(1)}) custom-call(s32[8]{0:T(128)S(1)} %get-tuple-element.76.slot_ref, f32[1024,768]{1,0:T(8,128)} %fusion.78.q_ref.k_ref.v_ref, ...), custom_call_target="tpu_custom_call" | custom-call | flops 8589934592 | bytes 8388608 | tf_op jit(solution)/shard_map/attention_forward/pallas_call | solution.py:274
  291.1 20.8 %collective-permute-done.37 = bf16[256,2048]{1,0:T(8,128)(2,1)S(1)} collective-permute-done((bf16[256,2048]{1,0:T(8,128)(2,1)S(1)}, bf16[256,2048]{1,0:T(8,128)(2,1)S(1)}, u32[]{:S(2)}, u32[]{:S(2)}) %collective-permute-start.37) | collective-permute-done | bytes 1048608 | tf_op jit(solution)/shard_map/ppermute | solution.py:30
  387.2 20.9 %feed_middle.4 = (bf16[1024,1024]{1,0:T(8,128)(2,1)}, bf16[1024,2048]{1,0:T(8,128)(2,1)}) custom-call(bf16[1024,2048]{1,0:T(8,128)(2,1)} %copy-done.57, bf16[1024,2048]{1,0:T(8,128)(2,1)} %constant_dynamic-update-slice_fusion.10.down_in_ref, bf16[2048,3072]{1,0:T(8,128)(2,1)} %all-gather.9.cloned.1.call-done.pair_ref.down_ref, ...), custom_call_target="tpu_custom_call" | custom-call | flops 12884901888 | bytes 27262976 | tf_op jit(solution)/shard_map/feed_middle/pallas_call | solution.py:384
  408.2 20.8 %feed_middle.5 = (bf16[1024,1024]{1,0:T(8,128)(2,1)}, bf16[1024,2048]{1,0:T(8,128)(2,1)}) custom-call(bf16[1024,2048]{1,0:T(8,128)(2,1)} %copy-done.57, bf16[1024,2048]{1,0:T(8,128)(2,1)} %constant_dynamic-update-slice_fusion.10.down_in_ref, bf16[2048,3072]{1,0:T(8,128)(2,1)} %all-gather.11.cloned.1.call-done.pair_ref.down_ref, ...), custom_call_target="tpu_custom_call" | custom-call | flops 12884901888 | bytes 27262976 | tf_op jit(solution)/shard_map/feed_middle/pallas_call | solution.py:384
  428.9 14.9 %fusion.16 = f32[1024,2048]{1,0:T(8,128)} fusion(bf16[1024,2048]{1,0:T(8,128)(2,1)} %get-tuple-element.44, bf16[2048,3072]{1,0:T(8,128)(2,1)} %all-gather.11.cloned.1.call-done.pair_ref.down_ref), kind=kOutput, calls=%fused_computation.18 | convolution fusion | flops 8589934592 | bytes 20971520 | tf_op jit(solution)/shard_map/dot_general | solution.py:25
  481.1 21.1 %feed_middle.6 = (bf16[1024,1024]{1,0:T(8,128)(2,1)}, bf16[1024,2048]{1,0:T(8,128)(2,1)}) custom-call(bf16[1024,2048]{1,0:T(8,128)(2,1)} %get-tuple-element.246.feed_ref, bf16[1024,2048]{1,0:T(8,128)(2,1)} %get-tuple-element.250.down_in_ref, bf16[2048,3072]{1,0:T(8,128)(2,1)} %all-gather.9.cloned.1.call-done.pair_ref.down_ref, ...), custom_call_target="tpu_custom_call" | custom-call | flops 12884901888 | bytes 27262976 | tf_op jit(solution)/shard_map/feed_middle/pallas_call | solution.py:384
  502.2 20.8 %feed_middle.7 = (bf16[1024,1024]{1,0:T(8,128)(2,1)}, bf16[1024,2048]{1,0:T(8,128)(2,1)}) custom-call(bf16[1024,2048]{1,0:T(8,128)(2,1)} %get-tuple-element.246.feed_ref, bf16[1024,2048]{1,0:T(8,128)(2,1)} %get-tuple-element.250.down_in_ref, bf16[2048,3072]{1,0:T(8,128)(2,1)} %all-gather.11.cloned.1.call-done.pair_ref.down_ref, ...), custom_call_target="tpu_custom_call" | custom-call | flops 12884901888 | bytes 27262976 | tf_op jit(solution)/shard_map/feed_middle/pallas_call | solution.py:384
  542.0 13.4 %fusion.14 = f32[1024,2048]{1,0:T(8,128)} fusion(bf16[1024,2048]{1,0:T(8,128)(2,1)S(1)} %copy-done.82, bf16[2048,3072]{1,0:T(8,128)(2,1)} %all-gather.11.cloned.1.call-done.pair_ref.down_ref), kind=kOutput, calls=%fused_computation.16 | convolution fusion | flops 8589934592 | bytes 20971520 | tf_op jit(solution)/shard_map/dot_general | solution.py:25
  596.4 21.0 %collective-permute-done.53 = bf16[256,2048]{1,0:T(8,128)(2,1)S(1)} collective-permute-done((bf16[256,2048]{1,0:T(8,128)(2,1)S(1)}, bf16[256,2048]{1,0:T(8,128)(2,1)S(1)}, u32[]{:S(2)}, u32[]{:S(2)}) %collective-permute-start.53) | collective-permute-done | bytes 1048608 | tf_op jit(solution)/shard_map/ppermute | solution.py:30
  619.3 20.6 %collective-permute-done.29 = bf16[256,2048]{1,0:T(8,128)(2,1)S(1)} collective-permute-done((bf16[256,2048]{1,0:T(8,128)(2,1)S(1)}, bf16[256,2048]{1,0:T(8,128)(2,1)S(1)}, u32[]{:S(2)}, u32[]{:S(2)}) %collective-permute-start.29) | collective-permute-done | bytes 1048608 | tf_op jit(solution)/shard_map/ppermute | solution.py:30
  640.8 13.8 %collective-permute-done.49 = bf16[256,2048]{1,0:T(8,128)(2,1)S(1)} collective-permute-done((bf16[256,2048]{1,0:T(8,128)(2,1)S(1)}, bf16[256,2048]{1,0:T(8,128)(2,1)S(1)}, u32[]{:S(2)}, u32[]{:S(2)}) %collective-permute-start.49) | collective-permute-done | bytes 1048608 | tf_op jit(solution)/shard_map/ppermute | solution.py:30
  654.6 19.0 %collective-permute-done.65 = bf16[256,2048]{1,0:T(8,128)(2,1)S(1)} collective-permute-done((bf16[256,2048]{1,0:T(8,128)(2,1)S(1)}, bf16[256,2048]{1,0:T(8,128)(2,1)S(1)}, u32[]{:S(2)}, u32[]{:S(2)}) %collective-permute-start.65) | collective-permute-done | bytes 1048608 | tf_op jit(solution)/shard_map/ppermute | solution.py:30
  683.5 14.6 %collective-permute-done.56 = bf16[256,2048]{1,0:T(8,128)(2,1)S(1)} collective-permute-done((bf16[256,2048]{1,0:T(8,128)(2,1)S(1)}, bf16[256,2048]{1,0:T(8,128)(2,1)S(1)}, u32[]{:S(2)}, u32[]{:S(2)}) %collective-permute-start.56) | collective-permute-done | bytes 1048608 | tf_op jit(solution)/shard_map/ppermute | solution.py:30
  711.2 21.6 %attention_backward.2 = (bf16[1024,512]{1,0:T(8,128)(2,1)S(1)}, bf16[1024,128]{1,0:T(8,128)(2,1)S(1)}, bf16[1024,128]{1,0:T(8,128)(2,1)S(1)}) custom-call(s32[8]{0:T(128)S(1)} %copy-done.1, bf16[1024,512]{1,0:T(8,128)(2,1)S(1)} %get-tuple-element.45.queries_ref, bf16[1024,128]{1,0:T(8,128)(2,1)S(1)} %copy-done.9, bf16[1024,128]{1,0:T(8,128)(2,1)S(1)} %copy-done.11, ...), custom_call_target="tpu_custom_call" | custom-call | flops 21474836480 | bytes 8388608 | tf_op jit(solution)/shard_map/attention_backward/pallas_call | solution.py:328
  794.2 21.4 %attention_backward.3 = (bf16[1024,512]{1,0:T(8,128)(2,1)S(1)}, bf16[1024,128]{1,0:T(8,128)(2,1)S(1)}, bf16[1024,128]{1,0:T(8,128)(2,1)S(1)}) custom-call(s32[8]{0:T(128)S(1)} %get-tuple-element.76.slot_ref, bf16[1024,512]{1,0:T(8,128)(2,1)S(1)} %get-tuple-element.54.queries_ref, bf16[1024,128]{1,0:T(8,128)(2,1)S(1)} %get-tuple-element.55.keys_ref, ...), custom_call_target="tpu_custom_call" | custom-call | flops 21474836480 | bytes 8388608 | tf_op jit(solution)/shard_map/attention_backward/pallas_call | solution.py:328
  856.9 13.2 %fusion.37 = bf16[2048,1024]{0,1:T(8,128)(2,1)S(1)} fusion(bf16[2048,2048]{1,0:T(8,128)(2,1)} %get-tuple-element.249, bf16[1024,1024]{1,0:T(8,128)(2,1)} %get-tuple-element.41, bf16[1024,1024]{1,0:T(8,128)(2,1)} %get-tuple-element.38), kind=kOutput, calls=%fused_computation.35 | convolution fusion | flops 8600420352 | bytes 16777216 | tf_op jit(solution)/shard_map/dot_general | solution.py:25
  870.2 19.9 %fusion.11 = bf16[2048,2048]{0,1:T(8,128)(2,1)S(1)} fusion(bf16[2048,2048]{1,0:T(8,128)(2,1)} %get-tuple-element.245, bf16[1024,2048]{1,0:T(8,128)(2,1)S(1)} %copy-done.85, bf16[1024,2048]{1,0:T(8,128)(2,1)S(1)} %copy-done.81), kind=kOutput, calls=%fused_computation.15 | convolution fusion | flops 17200840704 | bytes 25165824 | tf_op jit(solution)/shard_map/dot_general | solution.py:25
  890.1 14.4 %pad_maximum_fusion = bf16[2048,3072]{0,1:T(8,128)(2,1)} fusion(bf16[2048,1024]{0,1:T(8,128)(2,1)S(1)} %fusion.37, bf16[2048,2048]{0,1:T(8,128)(2,1)S(1)} %fusion.11), kind=kLoop, calls=%fused_computation | loop fusion | flops 25165824 | bytes 25165824 | tf_op jit(solution)/shard_map/concatenate | solution.py:550
  917.7 19.9 %fusion.8 = bf16[2048,2048]{0,1:T(8,128)(2,1)S(1)} fusion(bf16[2048,2048]{1,0:T(8,128)(2,1)} %get-tuple-element.245, bf16[1024,2048]{1,0:T(8,128)(2,1)S(1)} %copy-done.83, bf16[1024,2048]{1,0:T(8,128)(2,1)S(1)} %copy-done.79), kind=kOutput, calls=%fused_computation.14 | convolution fusion | flops 17200840704 | bytes 25165824 | tf_op jit(solution)/shard_map/dot_general | solution.py:25
  937.6 14.4 %pad_maximum_fusion.1 = bf16[2048,3072]{0,1:T(8,128)(2,1)} fusion(bf16[2048,1024]{0,1:T(8,128)(2,1)S(1)} %fusion.34, bf16[2048,2048]{0,1:T(8,128)(2,1)S(1)} %fusion.8), kind=kLoop, calls=%fused_computation.1 | loop fusion | flops 25165824 | bytes 25165824 | tf_op jit(solution)/shard_map/concatenate | solution.py:550
  987.4 65.3 %reduce-scatter.6.cloned.1.call-done = bf16[256,3072]{0,1:T(8,128)(2,1)} async-done(((bf16[2048,3072]{0,1:T(8,128)(2,1)}), bf16[256,3072]{0,1:T(8,128)(2,1)}) %reduce-scatter.6.cloned.1.call-update) | async-done | bytes 1572880 | tf_op jit(solution)/shard_map/reduce_scatter | solution.py:87
  1062.4 120.2 %reduce-scatter.8.cloned.1.call-done = bf16[256,3072]{0,1:T(8,128)(2,1)} async-done(((bf16[2048,3072]{0,1:T(8,128)(2,1)}), bf16[256,3072]{0,1:T(8,128)(2,1)}) %reduce-scatter.8.cloned.1.call-update) | async-done | bytes 1572880 | tf_op jit(solution)/shard_map/reduce_scatter | solution.py:87
  (596 shorter events, 600.9 us)
Async XLA Ops:
  7.2 126.3 %all-gather.5.cloned.1.call-start = ((), (), s32[]{:S(2)}) async-start(), calls=%async_computation.3 | async-start | bytes 4128768 | tf_op jit(solution)/shard_map/all_gather | solution.py:82
  21.2 182.0 %all-gather.7.cloned.1.call-start = ((), (), s32[]{:S(2)}) async-start(), calls=%async_computation.4 | async-start | bytes 2359296 | tf_op jit(solution)/shard_map/all_gather | solution.py:82
  30.0 357.2 %all-gather.9.cloned.1.call-start = ((), (), s32[]{:S(2)}) async-start(), calls=%async_computation.5 | async-start | bytes 14155776 | tf_op jit(solution)/shard_map/all_gather | solution.py:82
  51.3 356.9 %all-gather.11.cloned.1.call-start = ((), (), s32[]{:S(2)}) async-start(), calls=%async_computation.6 | async-start | bytes 14155776 | tf_op jit(solution)/shard_map/all_gather | solution.py:82
  54.5 81.5 %collective-permute-start.18 = (bf16[256,2048]{1,0:T(8,128)(2,1)}, bf16[256,2048]{1,0:T(8,128)(2,1)}, u32[]{:S(2)}, u32[]{:S(2)}) collective-permute-start(bf16[256,2048]{1,0:T(8,128)(2,1)} %get-tuple-element.150), channel_id=1, source_target_pairs={{0,1},{1,0},{2,3},{3,2},{4,5},{5,4},{6,7},{7,6},{8,9},{9,8},{10,11... | collective-permute-start | bytes 3145736 | tf_op jit(solution)/shard_map/ppermute | solution.py:30
  55.8 82.4 %collective-permute-start.19 = (bf16[256,2048]{1,0:T(8,128)(2,1)}, bf16[256,2048]{1,0:T(8,128)(2,1)}, u32[]{:S(2)}, u32[]{:S(2)}) collective-permute-start(bf16[256,2048]{1,0:T(8,128)(2,1)} %get-tuple-element.150), channel_id=1, source_target_pairs={{0,2},{1,3},{2,0},{3,1},{4,6},{5,7},{6,4},{7,5},{8,10},{9,11},{10,... | collective-permute-start | bytes 3145736 | tf_op jit(solution)/shard_map/ppermute | solution.py:30
  57.5 84.5 %collective-permute-start.44 = (bf16[256,2048]{1,0:T(8,128)(2,1)}, bf16[256,2048]{1,0:T(8,128)(2,1)}, u32[]{:S(2)}, u32[]{:S(2)}) collective-permute-start(bf16[256,2048]{1,0:T(8,128)(2,1)} %get-tuple-element.151), channel_id=1, source_target_pairs={{0,1},{1,0},{2,3},{3,2},{4,5},{5,4},{6,7},{7,6},{8,9},{9,8},{10,11... | collective-permute-start | bytes 3145736 | tf_op jit(solution)/shard_map/ppermute | solution.py:30
  58.6 87.3 %collective-permute-start.45 = (bf16[256,2048]{1,0:T(8,128)(2,1)}, bf16[256,2048]{1,0:T(8,128)(2,1)}, u32[]{:S(2)}, u32[]{:S(2)}) collective-permute-start(bf16[256,2048]{1,0:T(8,128)(2,1)} %get-tuple-element.151), channel_id=1, source_target_pairs={{0,2},{1,3},{2,0},{3,1},{4,6},{5,7},{6,4},{7,5},{8,10},{9,11},{10,... | collective-permute-start | bytes 3145736 | tf_op jit(solution)/shard_map/ppermute | solution.py:30
  131.1 830.6 %reduce-scatter.4.cloned.1.call-start = ((), (), s32[]{:S(2)}) async-start(), calls=%async_computation.7 | async-start | bytes 6488064 | tf_op jit(solution)/shard_map/reduce_scatter | solution.py:87
  138.2 129.5 %collective-permute-start.20 = (bf16[128,2048]{1,0:T(8,128)(2,1)}, bf16[128,2048]{1,0:T(8,128)(2,1)}, u32[]{:S(2)}, u32[]{:S(2)}) collective-permute-start(bf16[128,2048]{1,0:T(8,128)(2,1)} %slice.447), channel_id=1, source_target_pairs={{0,2},{1,3},{2,0},{3,1},{4,6},{5,7},{6,4},{7,5},{8,10},{9,11},{10,... | collective-permute-start | bytes 1572872 | tf_op jit(solution)/shard_map/ppermute | solution.py:30
  142.0 128.3 %collective-permute-start.21 = (bf16[128,2048]{1,0:T(8,128)(2,1)}, bf16[128,2048]{1,0:T(8,128)(2,1)}, u32[]{:S(2)}, u32[]{:S(2)}) collective-permute-start(bf16[128,2048]{1,0:T(8,128)(2,1)} %slice.448), channel_id=1, source_target_pairs={{0,1},{1,0},{2,3},{3,2},{4,5},{5,4},{6,7},{7,6},{8,9},{9,8},{10,11... | collective-permute-start | bytes 1572872 | tf_op jit(solution)/shard_map/ppermute | solution.py:30
  270.3 91.8 %collective-permute-start.46 = (bf16[128,2048]{1,0:T(8,128)(2,1)S(1)}, bf16[128,2048]{1,0:T(8,128)(2,1)S(1)}, u32[]{:S(2)}, u32[]{:S(2)}) collective-permute-start(bf16[128,2048]{1,0:T(8,128)(2,1)S(1)} %copy-done.52), channel_id=1, source_target_pairs={{0,2},{1,3},{2,0},{3,1},{4,6},{5,7},{6,4},{7,5},{8,10},{9,11},{10,... | collective-permute-start | bytes 1572872 | tf_op jit(solution)/shard_map/ppermute | solution.py:30
  289.4 73.8 %collective-permute-start.47 = (bf16[128,2048]{1,0:T(8,128)(2,1)S(1)}, bf16[128,2048]{1,0:T(8,128)(2,1)S(1)}, u32[]{:S(2)}, u32[]{:S(2)}) collective-permute-start(bf16[128,2048]{1,0:T(8,128)(2,1)S(1)} %copy-done.51), channel_id=1, source_target_pairs={{0,1},{1,0},{2,3},{3,2},{4,5},{5,4},{6,7},{7,6},{8,9},{9,8},{10,11... | collective-permute-start | bytes 1572872 | tf_op jit(solution)/shard_map/ppermute | solution.py:30
  458.0 110.5 %collective-permute-start.52 = (bf16[128,2048]{1,0:T(8,128)(2,1)}, bf16[128,2048]{1,0:T(8,128)(2,1)S(1)}, u32[]{:S(2)}, u32[]{:S(2)}) collective-permute-start(bf16[128,2048]{1,0:T(8,128)(2,1)} %get-tuple-element.116), channel_id=1, source_target_pairs={{0,2},{1,3},{2,0},{3,1},{4,6},{5,7},{6,4},{7,5},{8,10},{9,11},{10,... | collective-permute-start | bytes 1572872 | tf_op jit(solution)/shard_map/ppermute | solution.py:30
  459.0 110.5 %collective-permute-start.54 = (bf16[128,2048]{1,0:T(8,128)(2,1)}, bf16[128,2048]{1,0:T(8,128)(2,1)}, u32[]{:S(2)}, u32[]{:S(2)}) collective-permute-start(bf16[128,2048]{1,0:T(8,128)(2,1)} %get-tuple-element.115), channel_id=1, source_target_pairs={{0,1},{1,0},{2,3},{3,2},{4,5},{5,4},{6,7},{7,6},{8,9},{9,8},{10,11... | collective-permute-start | bytes 1572872 | tf_op jit(solution)/shard_map/ppermute | solution.py:30
  478.9 93.4 %collective-permute-start.28 = (bf16[128,2048]{1,0:T(8,128)(2,1)}, bf16[128,2048]{1,0:T(8,128)(2,1)}, u32[]{:S(2)}, u32[]{:S(2)}) collective-permute-start(bf16[128,2048]{1,0:T(8,128)(2,1)} %get-tuple-element.122), channel_id=1, source_target_pairs={{0,2},{1,3},{2,0},{3,1},{4,6},{5,7},{6,4},{7,5},{8,10},{9,11},{10,... | collective-permute-start | bytes 1572872 | tf_op jit(solution)/shard_map/ppermute | solution.py:30
  479.9 93.6 %collective-permute-start.30 = (bf16[128,2048]{1,0:T(8,128)(2,1)}, bf16[128,2048]{1,0:T(8,128)(2,1)}, u32[]{:S(2)}, u32[]{:S(2)}) collective-permute-start(bf16[128,2048]{1,0:T(8,128)(2,1)} %get-tuple-element.121), channel_id=1, source_target_pairs={{0,1},{1,0},{2,3},{3,2},{4,5},{5,4},{6,7},{7,6},{8,9},{9,8},{10,11... | collective-permute-start | bytes 1572872 | tf_op jit(solution)/shard_map/ppermute | solution.py:30
  757.7 88.6 %collective-permute-start.61 = (bf16[256,2048]{1,0:T(8,128)(2,1)}, bf16[256,2048]{1,0:T(8,128)(2,1)S(1)}, u32[]{:S(2)}, u32[]{:S(2)}) collective-permute-start(bf16[256,2048]{1,0:T(8,128)(2,1)} %pad_maximum_fusion.15), channel_id=1, source_target_pairs={{0,1},{1,0},{2,3},{3,2},{4,5},{5,4},{6,7},{7,6},{8,9},{9,8},{10,11... | collective-permute-start | bytes 3145736 | tf_op jit(solution)/shard_map/ppermute | solution.py:30
  759.1 87.2 %collective-permute-start.63 = (bf16[256,2048]{1,0:T(8,128)(2,1)}, bf16[256,2048]{1,0:T(8,128)(2,1)S(1)}, u32[]{:S(2)}, u32[]{:S(2)}) collective-permute-start(bf16[256,2048]{1,0:T(8,128)(2,1)} %pad_maximum_fusion.16), channel_id=1, source_target_pairs={{0,2},{1,3},{2,0},{3,1},{4,6},{5,7},{6,4},{7,5},{8,10},{9,11},{10,... | collective-permute-start | bytes 3145736 | tf_op jit(solution)/shard_map/ppermute | solution.py:30
  856.9 195.8 %reduce-scatter.6.cloned.1.call-start = ((), (), s32[]{:S(2)}) async-start(), calls=%async_computation.8 | async-start | bytes 14155776 | tf_op jit(solution)/shard_map/reduce_scatter | solution.py:87
  904.5 278.1 %reduce-scatter.8.cloned.1.call-start = ((), (), s32[]{:S(2)}) async-start(), calls=%async_computation.9 | async-start | bytes 14155776 | tf_op jit(solution)/shard_map/reduce_scatter | solution.py:87
  1056.9 134.8 %collective-permute-start.79 = (bf16[64,3072]{1,0:T(8,128)(2,1)}, bf16[64,3072]{1,0:T(8,128)(2,1)}, u32[]{:S(2)}, u32[]{:S(2)}) collective-permute-start(bf16[64,3072]{1,0:T(8,128)(2,1)} %copy.110), channel_id=1, source_target_pairs={{0,1},{1,0},{2,3},{3,2},{4,5},{5,4},{6,7},{7,6},{8,9},{9,8},{10,11... | collective-permute-start | bytes 1179656 | tf_op jit(solution)/shard_map/ppermute | solution.py:30
  1059.4 133.9 %collective-permute-start.80 = (bf16[64,3072]{1,0:T(8,128)(2,1)}, bf16[64,3072]{1,0:T(8,128)(2,1)}, u32[]{:S(2)}, u32[]{:S(2)}) collective-permute-start(bf16[64,3072]{1,0:T(8,128)(2,1)} %copy.111), channel_id=1, source_target_pairs={{0,2},{1,3},{2,0},{3,1},{4,6},{5,7},{6,4},{7,5},{8,10},{9,11},{10,... | collective-permute-start | bytes 1179656 | tf_op jit(solution)/shard_map/ppermute | solution.py:30
  1061.9 132.5 %collective-permute-start.81 = (bf16[64,3072]{1,0:T(8,128)(2,1)}, bf16[64,3072]{1,0:T(8,128)(2,1)}, u32[]{:S(2)}, u32[]{:S(2)}) collective-permute-start(bf16[64,3072]{1,0:T(8,128)(2,1)} %copy.112), channel_id=1, source_target_pairs={{0,3},{1,2},{2,1},{3,0},{4,7},{5,6},{6,5},{7,4},{8,11},{9,10},{10,... | collective-permute-start | bytes 1179656 | tf_op jit(solution)/shard_map/ppermute | solution.py:30
  (158 other events, 3368.7 us)
Sparse Core Ops, SparseCore 0:
  21.3 42.7 all-gather.4
  65.7 27.9 all-gather.6
  95.9 116.2 all-gather.8
  214.3 114.9 all-gather.10
  857.0 65.9 reduce-scatter.3
  925.1 127.5 reduce-scatter.5
  1055.0 127.5 reduce-scatter.7

commit v2 on v1

--- a/solution.py
+++ b/solution.py
@@ -25,68 +25,123 @@
     return lax.dot_general(left, right, dims, preferred_element_type=F32).astype(out)
 
 
-def swap(block, bits):
-    size = lax.axis_size("ctx")
-    return lax.ppermute(block, "ctx", [(i, i ^ bits) for i in range(size)])
+class Chain:
+    def __init__(self):
+        self.last = ()
+
+    def after(self, values):
+        values = tuple(values)
+        if not self.last:
+            return values
+        return lax.optimization_barrier(values + self.last)[: len(values)]
+
+    def run(self, function, *args):
+        leaves, tree = jax.tree.flatten(args)
+        out = function(*jax.tree.unflatten(tree, self.after(leaves)))
+        self.last = tuple(jax.tree.leaves(out))
+        return out
+
+    def wait(self, *arrays):
+        self.last = self.last + arrays
+
+
+    def send(self, *sends):
+        blocks = self.after(block for block, _ in sends)
+        return [
+            lax.ppermute(block, "ctx", [(i, i ^ bits) for i in range(4)])
+            for block, (_, bits) in zip(blocks, sends)
+        ]
+
+    def gather_near(self, own):
+        return self.send((own, 1), (own, 2)) if square() else []
+
+    def gather_far(self, near):
+        if not square():
+            return []
+        self.wait(*near)
+        half = near[0].shape[0] // 2
+        one, two = self.after(near)
+        return self.send((one[:half], 2), (two[half:], 1))
+
+    def gathered(self, own, near, far):
+        if not square():
+            return lax.all_gather(own, "ctx", axis=0, tiled=True)
+        self.wait(*far)
+        return jnp.concatenate([own, *near, *far], axis=0)
+
+    def scatter_near(self, parts):
+        if not square():
+            return []
+        across = 3 * (parts.shape[0] // 4)
+        half = parts.shape[0] // 8
+        return self.send((parts[across : across + half], 1), (parts[across + half :], 2))
+
+    def scatter_far(self, parts, near):
+        if not square():
+            return []
+        rows = parts.shape[0] // 4
+        half = rows // 2
+
+        def add(parts, low, high):
+            one, two = parts[rows : 2 * rows], parts[2 * rows : 3 * rows]
+            one_high = (one[half:].astype(F32) + high.astype(F32)).astype(BF16)
+            two_low = (two[:half].astype(F32) + low.astype(F32)).astype(BF16)
+            return (
+                jnp.concatenate([one[:half], one_high], axis=0),
+                jnp.concatenate([two_low, two[half:]], axis=0),
+            )
+
+        self.wait(*near)
+        one, two = self.run(add, parts, *near)
+        return self.send((one, 1), (two, 2))
+
+    def scattered(self, parts, far):
+        if not square():
+            return lax.psum_scatter(parts, "ctx", scatter_dimension=0, tiled=True).astype(F32)
+        self.wait(*far)
+        own = parts[: parts.shape[0] // 4]
+        return own.astype(F32) + far[0].astype(F32) + far[1].astype(F32)
+
+    def exchange(self, block_for):
+        size = lax.axis_size("ctx")
+        rank = lax.axis_index("ctx")
+        if not square():
+            stacked = jnp.stack([block_for(t) for t in range(size)])
+            return [lax.all_to_all(stacked, "ctx", 0, 0)]
+        return [block_for(rank)] + self.send(*[(block_for(rank ^ m), m) for m in (1, 2, 3)])
+
+    def exchanged(self, received):
+        if not square():
+            return received[0]
+        rank = lax.axis_index("ctx")
+        self.wait(*received[1:])
+
+        def lay(*received):
+            out = jnp.zeros((4,) + received[0].shape, received[0].dtype)
+            for member, value in enumerate(received):
+                out = lax.dynamic_update_index_in_dim(out, value, rank ^ member, 0)
+            return out
+
+        return self.run(lay, *received)
+
+    def all_rows(self, received):
+        mine = self.exchanged(received)
+        return lax.all_gather(
+            mine.reshape(-1, mine.shape[-1]), "dp", axis=0, tiled=True
+        )
+
+    def own_rows(self, summed):
+        rows = summed.shape[0] // lax.axis_size("ctx")
+        self.wait(summed)
+        return self.exchange(lambda t: lax.dynamic_slice_in_dim(summed, t * rows, rows, axis=0))
 
 
 def square():
     return lax.axis_size("ctx") == 4
 
 
-def gather_rows(own):
-    if not square():
-        return lax.all_gather(own, "ctx", axis=0, tiled=True)
-    half = own.shape[0] // 2
-    from_one, from_two = swap(own, 1), swap(own, 2)
-    across_low = swap(from_one[:half], 2)
-    across_high = swap(from_two[half:], 1)
-    return jnp.concatenate([own, from_one, from_two, across_low, across_high], axis=0)
-
-
-def scatter_rows(parts):
-    if not square():
-        return lax.psum_scatter(parts, "ctx", scatter_dimension=0, tiled=True).astype(F32)
-    rows = parts.shape[0] // 4
-    half = rows // 2
-    block = parts.reshape(4, rows, -1)
-    low = swap(block[3, :half], 1)
-    high = swap(block[3, half:], 2)
-    for_one = jnp.concatenate(
-        [block[1, :half], (block[1, half:].astype(F32) + high.astype(F32)).astype(BF16)], axis=0
-    )
-    for_two = jnp.concatenate(
-        [(block[2, :half].astype(F32) + low.astype(F32)).astype(BF16), block[2, half:]], axis=0
-    )
-    return (
-        block[0].astype(F32) + swap(for_one, 1).astype(F32) + swap(for_two, 2).astype(F32)
-    )
-
-
-def exchange(block_for):
-    size = lax.axis_size("ctx")
-    rank = lax.axis_index("ctx")
-    if not square():
-        stacked = jnp.stack([block_for(t) for t in range(size)])
-        return lax.all_to_all(stacked, "ctx", 0, 0)
-    received = [block_for(rank)] + [swap(block_for(rank ^ m), m) for m in (1, 2, 3)]
-    out = jnp.zeros((4,) + received[0].shape, received[0].dtype)
-    for member, value in enumerate(received):
-        out = lax.dynamic_update_index_in_dim(out, value, rank ^ member, 0)
-    return out
-
-
-def gather_columns(block_for):
-    mine = exchange(block_for)
-    mine = mine.reshape(-1, mine.shape[-1])
-    return lax.all_gather(mine, "dp", axis=0, tiled=True)
-
-
-def scatter_columns(grads):
-    size = lax.axis_size("ctx")
-    summed = lax.psum_scatter(grads, "dp", scatter_dimension=0, tiled=True)
-    rows = summed.shape[0] // size
-    return exchange(lambda t: lax.dynamic_slice_in_dim(summed, t * rows, rows, axis=0))
+def sum_over_dp(grads):
+    return lax.psum_scatter(grads, "dp", scatter_dimension=0, tiled=True)
 
 
 def swap_halves(rows):
@@ -367,14 +422,17 @@
 
 def feed_kernel(feed_ref, down_in_ref, pair_ref, down_ref, activated_ref, grads_ref):
     tile = down_ref.shape[1]
-    both = dot(feed_ref[...], pair_ref[...])
-    grad_act = dot(down_in_ref[...], down_ref[...])
-    gate, up = both[:, :tile], both[:, tile:]
-    sig = jax.nn.sigmoid(gate)
-    silu = gate * sig
-    activated_ref[...] = (silu * up).astype(BF16)
-    grads_ref[:, :tile] = (grad_act * up * sig * (1.0 + gate * (1.0 - sig))).astype(BF16)
-    grads_ref[:, tile:] = (grad_act * silu).astype(BF16)
+    step = min(256, feed_ref.shape[0])
+    for start in range(0, feed_ref.shape[0], step):
+        here = slice(start, start + step)
+        both = dot(feed_ref[here, :], pair_ref[...])
+        grad_act = dot(down_in_ref[here, :], down_ref[...])
+        gate, up = both[:, :tile], both[:, tile:]
+        sig = jax.nn.sigmoid(gate)
+        silu = gate * sig
+        activated_ref[here, :] = (silu * up).astype(BF16)
+        grads_ref[here, :tile] = (grad_act * up * (sig + silu * (1.0 - sig))).astype(BF16)
+        grads_ref[here, tile:] = (grad_act * silu).astype(BF16)
 
 
 def feed_middle(feed_in, down_in, weights, width, tile):
@@ -410,6 +468,72 @@
     )(feed_in, down_in, weights, weights)
 
 
+def spread_kernel(*refs):
+    count = (len(refs) - 1) // 2
+    total = sum(dot(refs[i][...], refs[count + i][...], NT) for i in range(count))
+    refs[-1][...] = total.astype(BF16)
+
+
+def feed_spread(lefts, weights, places, tile):
+    rows = lefts[0].shape[0]
+    depth = weights[0].shape[0]
+    widths = [left.shape[1] for left in lefts]
+    work = rows * depth * sum(widths)
+
+    step = min(512, rows)
+
+    def weight_spec(width, place):
+        return pl.BlockSpec((tile, width), lambda i, j: (j, place))
+
+    return pl.pallas_call(
+        spread_kernel,
+        grid=(rows // step, depth // tile),
+        in_specs=[pl.BlockSpec((step, width), lambda i, j: (i, 0)) for width in widths]
+        + [weight_spec(width, place) for width, place in zip(widths, places)],
+        out_specs=pl.BlockSpec((step, tile), lambda i, j: (i, j)),
+        out_shape=jax.ShapeDtypeStruct((rows, depth), BF16),
+        compiler_params=pltpu.CompilerParams(
+            dimension_semantics=("arbitrary", "arbitrary"), vmem_limit_bytes=56 << 20
+        ),
+        cost_estimate=pl.CostEstimate(
+            flops=2 * work,
+            bytes_accessed=2 * ((rows + depth) * sum(widths) + rows * depth),
+            transcendentals=0,
+        ),
+        name="feed_spread",
+    )(*lefts, *weights)
+
+
+def lay_kernel(place_ref, *refs, plan, inputs):
+    outs = refs[inputs:]
+    for source, member, start, width, target, at in plan:
+        each = outs[target].shape[1] // 4
+        where = pl.ds(pl.multiple_of(place_ref[member] * each + at, LANES), width)
+        outs[target][:, where] = refs[source][:, start : start + width].astype(F32)
+
+
+def lay_out(received, pieces, widths):
+    blocks = [block for group in received for block in group]
+    rows = blocks[0].shape[0]
+    plan = [
+        (4 * group + member, member, start, width, target, at)
+        for group, start, width, target, at in pieces
+        for member in range(4)
+    ]
+    return pl.pallas_call(
+        functools.partial(lay_kernel, plan=plan, inputs=len(blocks)),
+        grid_spec=pltpu.PrefetchScalarGridSpec(
+            num_scalar_prefetch=1,
+            grid=(1,),
+            in_specs=[pl.BlockSpec(block.shape, lambda i, p: (0, 0)) for block in blocks],
+            out_specs=[pl.BlockSpec((rows, 4 * width), lambda i, p: (0, 0)) for width in widths],
+        ),
+        out_shape=[jax.ShapeDtypeStruct((rows, 4 * width), F32) for width in widths],
+        compiler_params=pltpu.CompilerParams(vmem_limit_bytes=48 << 20),
+        name="lay_out",
+    )(lax.axis_index("ctx") ^ jnp.arange(4, dtype=jnp.int32), *blocks)
+
+
 def norm_forward(values):
     inverse_rms = lax.rsqrt(jnp.mean(values * values, axis=-1, keepdims=True) + EPS)
     return (values * inverse_rms, inverse_rms)
@@ -455,9 +579,12 @@
     own_key_width = key_matrix.shape[1] // ctx
     key_width = -(-own_key_width // LANES) * LANES
     feed_width = gate_weight.shape[1] // ctx
-    chunks = 2
-    chunk = feed_width // chunks
-    tile = min(512, chunk)
+    tile = min(512, feed_width)
+    tiles = feed_width // tile
+    first = max(1, 3 * tiles // 4)
+    chunks = [first * tile] + ([(tiles - first) * tile] if tiles > first else [])
+    starts = [0, chunks[0]][: len(chunks)]
+    chain = Chain()
 
     def columns(weight, t, width, at=0):
         return lax.dynamic_slice_in_dim(weight, t * (weight.shape[1] // ctx) + at, width, axis=1)
@@ -478,136 +605,282 @@
     def feed_for(part):
         def of(t):
             pieces = []
-            for start in range(part * chunk, (part + 1) * chunk, tile):
+            for start in range(starts[part], starts[part] + chunks[part], tile):
                 pieces += [
                     columns(gate_weight, t, tile, start),
                     columns(up_weight, t, tile, start),
                 ]
-            pieces.append(columns(down_weight, t, chunk, part * chunk))
+            pieces.append(columns(down_weight, t, chunks[part], starts[part]))
             return jnp.concatenate(pieces, axis=1)
 
         return of
 
-    projections = gather_columns(projections_for)
-    merge = gather_columns(lambda t: columns(merge_weight, t, query_width))
-    feeds = [gather_columns(feed_for(part)) for part in range(chunks)]
-
+    assert seqs == 2 and len(chunks) <= 2
+    many = len(chunks) > 1
+    last_part = len(chunks) - 1
     qkv_width = query_width + 2 * key_width
-    qkv_weight = projections[:, :qkv_width]
-    gains = projections[:, qkv_width : qkv_width + 2].astype(F32)
-    gain_one, gain_two = gains[:, 0], gains[:, 1]
 
     slots = jnp.argsort(span_order, axis=1).astype(jnp.int32)
     if square():
         slots = ((slots // 2) ^ rank) * 2 + slots % 2
     cos_lanes, sin_lanes = rope_lanes(length)
 
-    inputs = [tokens[s].astype(F32) for s in range(seqs)]
-    normed_one, inverse_one, attn_in = [], [], []
-    for s in range(seqs):
-        normed, inverse = norm_forward(inputs[s])
-        normed_one.append(normed)
-        inverse_one.append(inverse)
-        attn_in.append(gather_rows((normed * gain_one).astype(BF16)))
-    down_in = [gather_rows(out_grad[s]) for s in range(seqs)]
-    attn_out, kept, hidden_one = [], [], []
-    for s in range(seqs):
-        qkv = dot(attn_in[s], qkv_weight)
-        attended, *rest = attention_forward(
-            qkv, slots[s], cos_lanes, sin_lanes, query_width, key_width, group_size
+    def project(rows, weight, gain):
+        normed, _ = norm_forward(rows.astype(F32))
+        rows = (normed * gain).astype(BF16)
+        return rows, dot(rows, weight)
+
+    def attend(qkv, slots):
+        return attention_forward(
+            qkv, slots, cos_lanes, sin_lanes, query_width, key_width, group_size
         )
-        attn_out.append(attended)
-        kept.append(rest)
-        hidden_one.append(inputs[s] + scatter_rows(dot(attended, merge, NT, BF16)))
-
-    normed_two, inverse_two, feed_in = [], [], []
-    for s in range(seqs):
-        normed, inverse = norm_forward(hidden_one[s])
-        normed_two.append(normed)
-        inverse_two.append(inverse)
-        feed_in.append(gather_rows((normed * gain_two).astype(BF16)))
-    middle = [
-        [feed_middle(feed_in[s], down_in[s], feeds[part], chunk, tile) for part in range(chunks)]
-        for s in range(seqs)
-    ]
-    blocks, grad_hidden, merge_in, gain_two_sum = [], [], [], 0.0
-    for s in range(seqs):
-        grad_feed_in = sum(
-            dot(middle[s][part][1], feeds[part][:, : 2 * chunk], NT) for part in range(chunks)
+
+    def merge_back(rows, weight):
+        return dot(rows, weight, NT, BF16)
+
+    def feed_norm(hidden, gain):
+        normed, _ = norm_forward(hidden)
+        return hidden, (normed * gain).astype(BF16)
+
+    def middle_of(feed_in, down_in, weights, part):
+        return feed_middle(feed_in, down_in, weights, chunks[part], tile)
+
+    def feed_back(grads, weights):
+        return feed_spread(grads, weights, [0] * len(grads), tile)
+
+    def feed_out(activated, weights):
+        return feed_spread(activated, weights, [2] * len(activated), tile)
+
+    def token_grads(left, right):
+        return dot(jnp.concatenate(left, axis=0), jnp.concatenate(right, axis=0), TN, BF16)
+
+    def last_grads(feed_in, grads, down_in, activated):
+        activated = [jnp.concatenate(parts, axis=1) for parts in activated]
+        down = token_grads(down_in, activated)
+        if not many:
+            return down
+        return jnp.concatenate([token_grads(feed_in, grads), down], axis=1)
+
+    def feed_norm_back(hidden, summed, cot, gain):
+        normed, inverse = norm_forward(hidden)
+        grad_middle, gain_part = norm_backward(summed, normed, inverse, gain)
+        grad_hidden = cot.astype(F32) + grad_middle
+        return grad_hidden, grad_hidden.astype(BF16), gain_part
+
+    def attend_back(merge_in, weight, kept, slots):
+        grad_attn = dot(merge_in, weight, NN, BF16)
+        parts = attention_backward(kept, grad_attn, slots, cos_lanes, sin_lanes, group_size)
+        return jnp.concatenate(parts, axis=1)
+
+    def project_back(grads, weight):
+        return dot(grads, weight, NT, BF16)
+
+    def gain_part_of(rows, lower):
+        normed, _ = norm_forward(rows.astype(F32))
+        return jnp.sum(normed * lower.astype(F32), axis=0)
+
+    def attention_grads_of(attn_in, grad_qkv, merge_in, attn_out, rows, lower, gain_two_parts):
+        gain_one_sum = sum(gain_part_of(r, l) for r, l in zip(rows, lower))
+        gains = jnp.stack([gain_one_sum, sum(gain_two_parts)], axis=1)
+        return jnp.concatenate(
+            [
+                token_grads(attn_in, grad_qkv),
+                token_grads(merge_in, attn_out),
+                pad_columns(gains.astype(BF16), LANES),
+            ],
+            axis=1,
         )
-        grad_middle, gain_part = norm_backward(
-            scatter_rows(grad_feed_in.astype(BF16)), normed_two[s], inverse_two[s], gain_two
+
+    def project_norm_back(rows, summed, grad_hidden, gain):
+        normed, inverse = norm_forward(rows.astype(F32))
+        grad_lower, _ = norm_backward(summed, normed, inverse, gain)
+        return grad_hidden + grad_lower
+
+    moved = chain.exchange(projections_for)
+    a_near = chain.gather_near(tokens[0])
+    projections = chain.all_rows(moved)
+    moved = chain.exchange(lambda t: columns(merge_weight, t, query_width))
+    merge = chain.all_rows(moved)
+    a_far = chain.gather_far(a_near)
+    moved = chain.exchange(feed_for(0))
+    rows_a = chain.gathered(tokens[0], a_near, a_far)
+    b_near = chain.gather_near(tokens[1])
+
+    qkv_weight = projections[:, :qkv_width]
+    gains = projections[:, qkv_width : qkv_width + 2].astype(F32)
+    gain_one, gain_two = gains[:, 0], gains[:, 1]
+    attn_in_a, qkv = chain.run(project, rows_a, qkv_weight, gain_one)
+    feeds = [chain.all_rows(moved)]
+    attn_out_a, *kept_a = chain.run(attend, qkv, slots[0])
+    branch_a = chain.run(merge_back, attn_out_a, merge)
+    near_a = chain.scatter_near(branch_a)
+    b_far = chain.gather_far(b_near)
+    far_a = chain.scatter_far(branch_a, near_a)
+    rows_b = chain.gathered(tokens[1], b_near, b_far)
+    cot_a_near = chain.gather_near(out_grad[0])
+    attn_in_b, qkv = chain.run(project, rows_b, qkv_weight, gain_one)
+    hidden_a, feed_a = chain.run(
+        feed_norm, tokens[0].astype(F32) + chain.scattered(branch_a, far_a), gain_two
+    )
+    feed_a_near = chain.gather_near(feed_a)
+    attn_out_b, *kept_b = chain.run(attend, qkv, slots[1])
+    cot_a_far = chain.gather_far(cot_a_near)
+    branch_b = chain.run(merge_back, attn_out_b, merge)
+    near_b = chain.scatter_near(branch_b)
+    feed_a_far = chain.gather_far(feed_a_near)
+    down_in_a = chain.gathered(out_grad[0], cot_a_near, cot_a_far)
+    if many:
+        moved = chain.exchange(feed_for(1))
+    far_b = chain.scatter_far(branch_b, near_b)
+    feed_in_a = chain.gathered(feed_a, feed_a_near, feed_a_far)
+    cot_b_near = chain.gather_near(out_grad[1])
+    if many:
+        feeds.append(chain.all_rows(moved))
+    hidden_b, feed_b = chain.run(
+        feed_norm, tokens[1].astype(F32) + chain.scattered(branch_b, far_b), gain_two
+    )
+    feed_b_near = chain.gather_near(feed_b)
+    middle_a = [chain.run(lambda f, d, w: middle_of(f, d, w, 0), feed_in_a, down_in_a, feeds[0])]
+    cot_b_far = chain.gather_far(cot_b_near)
+    feed_b_far = chain.gather_far(feed_b_near)
+    down_in_b = chain.gathered(out_grad[1], cot_b_near, cot_b_far)
+    feed_in_b = chain.gathered(feed_b, feed_b_near, feed_b_far)
+    if many:
+        middle_a.append(
+            chain.run(lambda f, d, w: middle_of(f, d, w, 1), feed_in_a, down_in_a, feeds[1])
         )
-        gain_two_sum = gain_two_sum + gain_part
-        grad_hidden.append(out_grad[s].astype(F32) + grad_middle)
-        merge_in.append(gather_rows(grad_hidden[s].astype(BF16)))
-    feed_tokens = jnp.concatenate(feed_in, axis=0)
-    down_tokens = jnp.concatenate(down_in, axis=0)
-    feed_sums = []
-    for part in range(chunks):
-        activated = jnp.concatenate([middle[s][part][0] for s in range(seqs)], axis=0)
-        grads = jnp.concatenate([middle[s][part][1] for s in range(seqs)], axis=0)
-        grads = jnp.concatenate(
-            [dot(feed_tokens, grads, TN, BF16), dot(down_tokens, activated, TN, BF16)], axis=1
+    back_a = chain.run(feed_back, [m[1] for m in middle_a], feeds)
+    near_a = chain.scatter_near(back_a)
+    middle_b = [chain.run(lambda f, d, w: middle_of(f, d, w, 0), feed_in_b, down_in_b, feeds[0])]
+    far_a = chain.scatter_far(back_a, near_a)
+    grads_first = chain.run(
+        token_grads, [feed_in_a, feed_in_b], [middle_a[0][1], middle_b[0][1]]
+    )
+    sums_first = sum_over_dp(grads_first)
+    grad_hidden_a, merge_a, gain_two_a = chain.run(
+        feed_norm_back, hidden_a, chain.scattered(back_a, far_a), out_grad[0], gain_two
+    )
+    merge_a_near = chain.gather_near(merge_a)
+    if many:
+        middle_b.append(
+            chain.run(lambda f, d, w: middle_of(f, d, w, 1), feed_in_b, down_in_b, feeds[1])
         )
-        feed_sums.append(scatter_columns(grads))
-    for s in range(seqs):
-        branch = sum(
-            dot(middle[s][part][0], feeds[part][:, 2 * chunk :], NT) for part in range(chunks)
-        )
-        blocks.append((hidden_one[s] + scatter_rows(branch.astype(BF16))).astype(BF16))
-
-    grad_qkv, input_grad, gain_one_sum = [], [], 0.0
-    for s in range(seqs):
-        grad_attn = dot(merge_in[s], merge, NN, BF16)
-        parts = attention_backward(
-            kept[s], grad_attn, slots[s], cos_lanes, sin_lanes, group_size
-        )
-        grad_qkv.append(jnp.concatenate(parts, axis=1))
-        grad_lower, gain_part = norm_backward(
-            scatter_rows(dot(grad_qkv[s], qkv_weight, NT, BF16)),
-            normed_one[s],
-            inverse_one[s],
-            gain_one,
-        )
-        gain_one_sum = gain_one_sum + gain_part
-        input_grad.append(grad_hidden[s] + grad_lower)
-    attention_grads = jnp.concatenate(
-        [
-            dot(jnp.concatenate(attn_in, axis=0), jnp.concatenate(grad_qkv, axis=0), TN, BF16),
-            dot(jnp.concatenate(merge_in, axis=0), jnp.concatenate(attn_out, axis=0), TN, BF16),
-            pad_columns(jnp.stack([gain_one_sum, gain_two_sum], axis=1).astype(BF16), LANES),
-        ],
-        axis=1,
-    )
-    attention_sums = scatter_columns(attention_grads)
-
-    def spread(pieces):
-        return pieces.astype(F32).transpose(1, 0, 2).reshape(pieces.shape[1], -1)
-
-    def of_feed(kind):
-        pieces = []
-        for part in range(chunks):
-            for at in range(chunk // tile):
-                start = 2 * chunk + at * tile if kind == 2 else (2 * at + kind) * tile
-                pieces.append(feed_sums[part][:, :, start : start + tile])
-        return spread(jnp.concatenate(pieces, axis=2))
+    back_b = chain.run(feed_back, [m[1] for m in middle_b], feeds)
+    near_b = chain.scatter_near(back_b)
+    merge_a_far = chain.gather_far(merge_a_near)
+    out_a = chain.run(feed_out, [m[0] for m in middle_a], feeds)
+    out_a_near = chain.scatter_near(out_a)
+    far_b = chain.scatter_far(back_b, near_b)
+    merge_in_a = chain.gathered(merge_a, merge_a_near, merge_a_far)
+    grads_last = chain.run(
+        last_grads,
+        [feed_in_a, feed_in_b],
+        [middle_a[last_part][1], middle_b[last_part][1]],
+        [down_in_a, down_in_b],
+        [[m[0] for m in middle_a], [m[0] for m in middle_b]],
+    )
+    out_a_far = chain.scatter_far(out_a, out_a_near)
+    grad_hidden_b, merge_b, gain_two_b = chain.run(
+        feed_norm_back, hidden_b, chain.scattered(back_b, far_b), out_grad[1], gain_two
+    )
+    merge_b_near = chain.gather_near(merge_b)
+    grad_qkv_a = chain.run(attend_back, merge_in_a, merge, kept_a, slots[0])
+    chain.wait(sums_first)
+    sums_last = sum_over_dp(chain.run(lambda g: g, grads_last))
+    merge_b_far = chain.gather_far(merge_b_near)
+    lower_a = chain.run(project_back, grad_qkv_a, qkv_weight)
+    lower_a_near = chain.scatter_near(lower_a)
+    out_b = chain.run(feed_out, [m[0] for m in middle_b], feeds)
+    lower_a_far = chain.scatter_far(lower_a, lower_a_near)
+    merge_in_b = chain.gathered(merge_b, merge_b_near, merge_b_far)
+    out_b_near = chain.scatter_near(out_b)
+    grad_qkv_b = chain.run(attend_back, merge_in_b, merge, kept_b, slots[1])
+    lower_b = chain.run(project_back, grad_qkv_b, qkv_weight)
+    lower_b_near = chain.scatter_near(lower_b)
+    out_b_far = chain.scatter_far(out_b, out_b_near)
+    attention_grads = chain.run(
+        attention_grads_of,
+        [attn_in_a, attn_in_b],
+        [grad_qkv_a, grad_qkv_b],
+        [merge_in_a, merge_in_b],
+        [attn_out_a, attn_out_b],
+        [rows_a, rows_b],
+        [lower_a, lower_b],
+        [gain_two_a, gain_two_b],
+    )
+    lower_b_far = chain.scatter_far(lower_b, lower_b_near)
+    moved_first = chain.own_rows(sums_first)
+    input_grad_a = chain.run(
+        project_norm_back, tokens[0], chain.scattered(lower_a, lower_a_far), grad_hidden_a, gain_one
+    )
+    block_a = chain.run(lambda h, o: (h + o).astype(BF16), hidden_a, chain.scattered(out_a, out_a_far))
+    block_b = chain.run(lambda h, o: (h + o).astype(BF16), hidden_b, chain.scattered(out_b, out_b_far))
+    input_grad_b = chain.run(
+        project_norm_back, tokens[1], chain.scattered(lower_b, lower_b_far), grad_hidden_b, gain_one
+    )
+    chain.wait(sums_last)
+    attention_sums = sum_over_dp(chain.run(lambda g: g, attention_grads))
+    moved_last = chain.own_rows(sums_last)
+    chain.wait(*moved_last[1:])
+    blocks = [block_a, block_b]
+    input_grad = [input_grad_a, input_grad_b]
 
     key_at, value_at = query_width, query_width + key_width
     merge_at, gain_at = qkv_width, qkv_width + query_width
-    gain_totals = jnp.sum(attention_sums[:, :, gain_at : gain_at + 2].astype(F32), axis=0)
+    feed_pieces = [
+        (part, (2 * at + kind) * tile, tile, kind, starts[part] + at * tile)
+        for part, width in enumerate(chunks)
+        for at in range(width // tile)
+        for kind in range(2)
+    ] + [(len(chunks) - 1, 2 * chunks[1] if many else 0, feed_width, 2, 0)]
+    attention_pieces = [
+        (0, 0, query_width, 0, 0),
+        (0, key_at, own_key_width, 1, 0),
+        (0, value_at, own_key_width, 2, 0),
+        (0, merge_at, query_width, 3, 0),
+    ]
+
+    def results(received, pieces, widths):
+        if square():
+            return lay_out(received, pieces, widths)
+        columns_of = [[] for _ in widths]
+        for group, start, width, target, at in sorted(pieces, key=lambda piece: piece[4]):
+            columns_of[target].append(received[group][0][:, :, start : start + width])
+        return [
+            jnp.concatenate(parts, axis=2)
+            .astype(F32)
+            .transpose(1, 0, 2)
+            .reshape(weight_rows, -1)
+            for parts in columns_of
+        ]
+
+    gate_total, up_total, down_total = chain.run(
+        lambda *received: results(received, feed_pieces, [feed_width] * 3),
+        *([moved_first, moved_last] if many else [moved_last]),
+    )
+    moved = chain.own_rows(attention_sums)
+    chain.wait(*moved[1:])
+    query_total, key_total, value_total, merge_total = chain.run(
+        lambda received: results(
+            [received], attention_pieces, [query_width, own_key_width, own_key_width, query_width]
+        ),
+        moved,
+    )
+    gain_totals = sum(block[..., gain_at : gain_at + 2].astype(F32) for block in moved)
+    if not square():
+        gain_totals = jnp.sum(gain_totals, axis=0)
     return (
         jnp.stack(blocks),
         jnp.stack(input_grad),
         gain_totals[:, 0],
-        spread(attention_sums[:, :, :query_width]),
-        spread(attention_sums[:, :, key_at : key_at + own_key_width]),
-        spread(attention_sums[:, :, value_at : value_at + own_key_width]),
-        spread(attention_sums[:, :, merge_at : merge_at + query_width]),
+        query_total,
+        key_total,
+        value_total,
+        merge_total,
         gain_totals[:, 1],
-        of_feed(0),
-        of_feed(1),
-        of_feed(2),
+        gate_total,
+        up_total,
+        down_total,
     )
 
 

time: 1230 us -> 947 us (0.77)
  waiting for transfers between devices: 539 us -> 244 us
  Pallas kernels: 158 us -> 245 us
  matrix products: 202 us -> 122 us
  local copies, waits for them, and re-layouts: 132 us -> 119 us
    ppermute x85, waiting for transfers between devices: 354 us -> 202 us  [send(): lax.ppermute(block, 'ctx', [(i, i ^ bits) for i in range(4)])]
    reduce_scatter x3, waiting for transfers between devices: 185 us -> 42.3 us  [sum_over_dp(): return lax.psum_scatter(grads, 'dp', scatter_dimension=0, tiled=True)]
    pallas_call x0 -> x6, Pallas kernels: none -> 87 us  [the longest x4 81.8 us: feed_spread(): pl.pallas_call(spread_kernel, grid=(rows // step, depth // tile), in_spec...]
    dot_general x22 -> x13, matrix products: 202 us -> 122 us  [dot(): lax.dot_general(left, right, dims, preferred_element_type=F32).astype(out)]
    add x0 -> x11, other arithmetic: none -> 21.9 us  [the longest x6 14.9 us: scattered(): return own.astype(F32) + far[0].astype(F32) + far[1].astype(F32)]
    slice x22 -> x35, local copies, waits for them, and re-layouts: 10.6 us -> 30.5 us  [the longest x16 16.6 us: gather_far(): return self.send((one[:half], 2), (two[half:], 1))]
    dynamic_update_slice x28 -> x16, local copies, waits for them, and re-layouts: 17.8 us -> 3.12 us  [lay(): out = lax.dynamic_update_index_in_dim(out, value, rank ^ member, 0)]
    concatenate x19 -> x22, other arithmetic: 38.4 us -> 27.9 us  [the longest x1 10.8 us: last_grads(): return jnp.concatenate([token_grads(feed_in, grads), down], axis=1)]
  transfers between devices with their start and end apart: 92 -> 92, of which waited for: 51 -> 37; matrix products, arithmetic and copies ran while one was open for 28% -> 28% of each run, Pallas kernels for 9% -> 22%
where the time goes in v2:
time: 947 us; the launch traced here: 938 us
  Pallas kernels  245 us (26%)
  waiting for transfers between devices  244 us (26%)
  matrix products  122 us (13%)
  local copies, waits for them, and re-layouts  119 us (13%)
  other arithmetic  96.5 us (10%)
  starting transfers between devices  94.8 us (10%)
  between operations  16.7 us (2%)
    ppermute x85, waiting for transfers between devices, send(): lax.ppermute(block, 'ctx', [(i, i ^ bits) for i in range(4)])  202 us
    dot_general x13, matrix products, dot(): lax.dot_general(left, right, dims, preferred_element_type=F32).astype(out)  122 us
    ppermute x85, starting transfers between devices, send(): lax.ppermute(block, 'ctx', [(i, i ^ bits) for i in range(4)])  93.9 us
    pallas_call x4, Pallas kernels, feed_middle(): pl.pallas_call(feed_kernel, grid=(tiles,), in_specs=[pl.BlockSpec((rows,...  83.7 us
    pallas_call x4, Pallas kernels, feed_spread(): pl.pallas_call(spread_kernel, grid=(rows // step, depth // tile), in_spec...  81.8 us
    unnamed x272, local copies, waits for them, and re-layouts  62.8 us
    pallas_call x2, Pallas kernels, attention_backward(): pl.pallas_call(functools.partial(attention_backward_kernel, span=length /...  42.6 us
    reduce_scatter x3, waiting for transfers between devices, sum_over_dp(): return lax.psum_scatter(grads, 'dp', scatter_dimension=0, tiled=True)  42.3 us
  transfers between devices with their start and end apart: 92, of which 37 were waited for; matrix products, arithmetic and copies ran while one was open for 28% of the time, Pallas kernels for 22%

profile of v2, /device:TPU:0, one launch (start us, length us, event | category | flops | bytes accessed | tf_op | source)
XLA Modules:
  0.0 937.9 jit_solution(3235139969859841841)
XLA Ops:
  35.8 14.7 %collective-permute-done.5 = bf16[64,512]{1,0:T(8,128)(2,1)S(1)} collective-permute-done((bf16[64,512]{1,0:T(8,128)(2,1)S(1)}, bf16[64,512]{1,0:T(8,128)(2,1)S(1)}, u32[]{:S(2)}, u32[]{:S(2)}) %collective-permute-start.5) | collective-permute-done | bytes 65568 | tf_op jit(solution)/shard_map/ppermute | solution.py:51
  108.3 16.0 %attention_forward.2 = (bf16[1024,512]{1,0:T(8,128)(2,1)S(1)}, bf16[1024,512]{1,0:T(8,128)(2,1)S(1)}, bf16[1024,128]{1,0:T(8,128)(2,1)S(1)}, bf16[1024,128]{1,0:T(8,128)(2,1)S(1)}, f32[4,4,512]{2,1,0:T(4,128)S(1)}) custom-call(s32[8]{0:T(128)S(1)} %get-tuple-element.488.slot_ref, f32[1024,768]{1,0:T(8,128)} %fusion.120.q_ref.k_ref.v_ref, ...), custom_call_target="tpu_custom_call" | custom-call | flops 8589934592 | bytes 8388608 | tf_op jit(solution)/shard_map/attention_forward/pallas_call | solution.py:329
  166.4 13.4 %collective-permute-done.17 = bf16[256,2048]{1,0:T(8,128)(2,1)S(1)} collective-permute-done((bf16[256,2048]{1,0:T(8,128)(2,1)S(1)}, bf16[256,2048]{1,0:T(8,128)(2,1)S(1)}, u32[]{:S(2)}, u32[]{:S(2)}) %collective-permute-start.17) | collective-permute-done | bytes 1048608 | tf_op jit(solution)/shard_map/ppermute | solution.py:51
  182.4 15.9 %attention_forward.3 = (bf16[1024,512]{1,0:T(8,128)(2,1)S(1)}, bf16[1024,512]{1,0:T(8,128)(2,1)S(1)}, bf16[1024,128]{1,0:T(8,128)(2,1)S(1)}, bf16[1024,128]{1,0:T(8,128)(2,1)S(1)}, f32[4,4,512]{2,1,0:T(4,128)S(1)}) custom-call(s32[8]{0:T(128)S(1)} %get-tuple-element.518.slot_ref, f32[1024,768]{1,0:T(8,128)} %fusion.121.q_ref.k_ref.v_ref, ...), custom_call_target="tpu_custom_call" | custom-call | flops 8589934592 | bytes 8388608 | tf_op jit(solution)/shard_map/attention_forward/pallas_call | solution.py:329
  215.0 22.3 %collective-permute-done.21 = bf16[256,2048]{1,0:T(8,128)(2,1)S(1)} collective-permute-done((bf16[256,2048]{1,0:T(8,128)(2,1)S(1)}, bf16[256,2048]{1,0:T(8,128)(2,1)S(1)}, u32[]{:S(2)}, u32[]{:S(2)}) %collective-permute-start.21) | collective-permute-done | bytes 1048608 | tf_op jit(solution)/shard_map/ppermute | solution.py:51
  278.4 17.6 %collective-permute-done.31 = bf16[256,2048]{1,0:T(8,128)(2,1)S(1)} collective-permute-done((bf16[256,2048]{1,0:T(8,128)(2,1)S(1)}, bf16[256,2048]{1,0:T(8,128)(2,1)S(1)}, u32[]{:S(2)}, u32[]{:S(2)}) %collective-permute-start.31) | collective-permute-done | bytes 1048608 | tf_op jit(solution)/shard_map/ppermute | solution.py:51
  303.1 15.3 %collective-permute-done.36 = bf16[256,2048]{1,0:T(8,128)(2,1)S(1)} collective-permute-done((bf16[256,2048]{1,0:T(8,128)(2,1)}, bf16[256,2048]{1,0:T(8,128)(2,1)S(1)}, u32[]{:S(2)}, u32[]{:S(2)}) %collective-permute-start.36) | collective-permute-done | bytes 1048608 | tf_op jit(solution)/shard_map/ppermute | solution.py:51
  320.4 28.4 %feed_middle.4 = (bf16[1024,1536]{1,0:T(8,128)(2,1)}, bf16[1024,3072]{1,0:T(8,128)(2,1)}) custom-call(bf16[1024,2048]{1,0:T(8,128)(2,1)} %constant_dynamic-update-slice_fusion.34.feed_ref, bf16[1024,2048]{1,0:T(8,128)(2,1)} %copy-done.108, bf16[2048,4608]{1,0:T(8,128)(2,1)} %all-gather.9.cloned.1.call-done.pair_ref.down_ref.refs_2_, ...), custom_call_target="tpu_custom_call" | custom-call | flops 19327352832 | bytes 36700160 | tf_op jit(solution)/shard_map/feed_middle/pallas_call | solution.py:442
  370.7 13.6 %feed_middle.5 = (bf16[1024,512]{1,0:T(8,128)(2,1)}, bf16[1024,1024]{1,0:T(8,128)(2,1)}) custom-call(bf16[1024,2048]{1,0:T(8,128)(2,1)} %constant_dynamic-update-slice_fusion.34.feed_ref, bf16[1024,2048]{1,0:T(8,128)(2,1)} %copy-done.108, bf16[2048,1536]{1,0:T(8,128)(2,1)} %all-gather.11.cloned.1.call-done.pair_ref.down_ref.refs_3_, ...), custom_call_target="tpu_custom_call" | custom-call | flops 6442450944 | bytes 17825792 | tf_op jit(solution)/shard_map/feed_middle/pallas_call | solution.py:442
  384.4 24.9 %feed_spread.4 = bf16[1024,2048]{1,0:T(8,128)(2,1)} custom-call(bf16[1024,3072]{1,0:T(8,128)(2,1)} %get-tuple-element.435.refs_0_, bf16[1024,1024]{1,0:T(8,128)(2,1)} %get-tuple-element.469.refs_1_, bf16[2048,4608]{1,0:T(8,128)(2,1)} %all-gather.9.cloned.1.call-done.pair_ref.down_ref.refs_2_, ...), custom_call_target="tpu_custom_call" | custom-call | flops 17179869184 | bytes 29360128 | tf_op jit(solution)/shard_map/feed_spread/pallas_call | solution.py:488
  421.3 27.9 %feed_middle.6 = (bf16[1024,1536]{1,0:T(8,128)(2,1)}, bf16[1024,3072]{1,0:T(8,128)(2,1)}) custom-call(bf16[1024,2048]{1,0:T(8,128)(2,1)} %constant_dynamic-update-slice_fusion.44.feed_ref, bf16[1024,2048]{1,0:T(8,128)(2,1)} %constant_dynamic-update-slice_fusion.49.down_in_ref, bf16[2048,4608]{1,0:T(8,128)(2,1)} %all-gather.9.cloned.1.call-done.pair_ref.down_ref.refs_2_, ...), custom_call_target="tpu_custom_call" | custom-call | flops 19327352832 | bytes 36700160 | tf_op jit(solution)/shard_map/feed_middle/pallas_call | solution.py:442
  453.9 33.4 %fusion.5 = bf16[2048,3072]{1,0:T(8,128)(2,1)} fusion(bf16[1024,3072]{1,0:T(8,128)(2,1)} %get-tuple-element.446.refs_0_, bf16[1024,3072]{1,0:T(8,128)(2,1)} %get-tuple-element.435.refs_0_, bf16[1024,2048]{1,0:T(8,128)(2,1)} %constant_dynamic-update-slice_fusion.44.feed_ref, bf16[1024,2048]{1,0:T(8,128)(2,1)S(1)} %copy-done.88), kind=kOutput, calls=%fused_computation.7 | convolution fusion | flops 25818038272 | bytes 33554432 | tf_op jit(solution)/shard_map/dot_general | solution.py:25
  489.7 19.1 %collective-permute-done.46 = bf16[256,2048]{1,0:T(8,128)(2,1)S(1)} collective-permute-done((bf16[256,2048]{1,0:T(8,128)(2,1)}, bf16[256,2048]{1,0:T(8,128)(2,1)S(1)}, u32[]{:S(2)}, u32[]{:S(2)}) %collective-permute-start.46) | collective-permute-done | bytes 1048608 | tf_op jit(solution)/shard_map/ppermute | solution.py:51
  517.8 13.8 %feed_middle.7 = (bf16[1024,512]{1,0:T(8,128)(2,1)}, bf16[1024,1024]{1,0:T(8,128)(2,1)}) custom-call(bf16[1024,2048]{1,0:T(8,128)(2,1)} %constant_dynamic-update-slice_fusion.44.feed_ref, bf16[1024,2048]{1,0:T(8,128)(2,1)} %constant_dynamic-update-slice_fusion.49.down_in_ref, bf16[2048,1536]{1,0:T(8,128)(2,1)} %all-gather.11.cloned.1.call-done.pair_ref.down_ref.refs_3_, ...), custom_call_target="tpu_custom_call" | custom-call | flops 6442450944 | bytes 17825792 | tf_op jit(solution)/shard_map/feed_middle/pallas_call | solution.py:442
  531.5 25.1 %feed_spread.5 = bf16[1024,2048]{1,0:T(8,128)(2,1)} custom-call(bf16[1024,3072]{1,0:T(8,128)(2,1)} %get-tuple-element.446.refs_0_, bf16[1024,1024]{1,0:T(8,128)(2,1)} %get-tuple-element.470.refs_1_, bf16[2048,4608]{1,0:T(8,128)(2,1)} %all-gather.9.cloned.1.call-done.pair_ref.down_ref.refs_2_, ...), custom_call_target="tpu_custom_call" | custom-call | flops 17179869184 | bytes 29360128 | tf_op jit(solution)/shard_map/feed_spread/pallas_call | solution.py:488
  565.4 16.3 %feed_spread.6 = bf16[1024,2048]{1,0:T(8,128)(2,1)} custom-call(bf16[1024,1536]{1,0:T(8,128)(2,1)} %get-tuple-element.473.refs_0_, bf16[1024,512]{1,0:T(8,128)(2,1)} %get-tuple-element.474.refs_1_, bf16[2048,4608]{1,0:T(8,128)(2,1)} %all-gather.9.cloned.1.call-done.pair_ref.down_ref.refs_2_, ...), custom_call_target="tpu_custom_call" | custom-call | flops 8589934592 | bytes 16777216 | tf_op jit(solution)/shard_map/feed_spread/pallas_call | solution.py:488
  595.2 12.3 %fusion.55 = bf16[2048,1024]{1,0:T(8,128)(2,1)} fusion(bf16[1024,1024]{1,0:T(8,128)(2,1)S(1)} %copy-done.117, bf16[1024,1024]{1,0:T(8,128)(2,1)S(1)} %copy-done.116, bf16[1024,2048]{1,0:T(8,128)(2,1)} %constant_dynamic-update-slice_fusion.44.feed_ref, bf16[1024,2048]{1,0:T(8,128)(2,1)S(1)} %copy-done.89), kind=kOutput, calls=%fused_computation.60 | convolution fusion | flops 8617197568 | bytes 16777216 | tf_op jit(solution)/shard_map/dot_general | solution.py:25
  607.5 27.9 %fusion.46 = bf16[2048,2048]{1,0:T(8,128)(2,1)} fusion(bf16[1024,512]{1,0:T(8,128)(2,1)} %get-tuple-element.506.refs_1_, bf16[1024,1536]{1,0:T(8,128)(2,1)} %get-tuple-element.505.refs_0_, bf16[1024,512]{1,0:T(8,128)(2,1)} %get-tuple-element.474.refs_1_, bf16[1024,1536]{1,0:T(8,128)(2,1)} %get-tuple-element.473.refs_0_, ...), kind=kOutput, calls=%fused_computation.54 | convolution fusion | flops 17234395136 | bytes 25165824 | tf_op jit(solution)/shard_map/dot_general | solution.py:25
  635.4 10.8 %pad_maximum_fusion = bf16[2048,3072]{1,0:T(8,128)(2,1)} fusion(bf16[2048,2048]{1,0:T(8,128)(2,1)} %fusion.46, bf16[2048,1024]{1,0:T(8,128)(2,1)} %fusion.55), kind=kLoop, calls=%fused_computation.4 | loop fusion | flops 25165824 | bytes 25165824 | tf_op jit(solution)/shard_map/concatenate | solution.py:662
  669.4 21.3 %attention_backward.2 = (bf16[1024,512]{1,0:T(8,128)(2,1)S(1)}, bf16[1024,128]{1,0:T(8,128)(2,1)S(1)}, bf16[1024,128]{1,0:T(8,128)(2,1)S(1)}) custom-call(s32[8]{0:T(128)S(1)} %copy-done.1, bf16[1024,512]{1,0:T(8,128)(2,1)S(1)} %get-tuple-element.489.queries_ref, bf16[1024,128]{1,0:T(8,128)(2,1)S(1)} %copy-done.9, bf16[1024,128]{1,0:T(8,128)(2,1)S(1)} %copy-done.11, ...), custom_call_target="tpu_custom_call" | custom-call | flops 21474836480 | bytes 8388608 | tf_op jit(solution)/shard_map/attention_backward/pallas_call | solution.py:383
  715.4 15.5 %feed_spread.7 = bf16[1024,2048]{1,0:T(8,128)(2,1)} custom-call(bf16[1024,1536]{1,0:T(8,128)(2,1)} %get-tuple-element.505.refs_0_, bf16[1024,512]{1,0:T(8,128)(2,1)} %get-tuple-element.506.refs_1_, bf16[2048,4608]{1,0:T(8,128)(2,1)} %all-gather.9.cloned.1.call-done.pair_ref.down_ref.refs_2_, ...), custom_call_target="tpu_custom_call" | custom-call | flops 8589934592 | bytes 16777216 | tf_op jit(solution)/shard_map/feed_spread/pallas_call | solution.py:488
  743.7 21.3 %attention_backward.3 = (bf16[1024,512]{1,0:T(8,128)(2,1)S(1)}, bf16[1024,128]{1,0:T(8,128)(2,1)S(1)}, bf16[1024,128]{1,0:T(8,128)(2,1)S(1)}) custom-call(s32[8]{0:T(128)S(1)} %get-tuple-element.518.slot_ref, bf16[1024,512]{1,0:T(8,128)(2,1)S(1)} %get-tuple-element.519.queries_ref, bf16[1024,128]{1,0:T(8,128)(2,1)S(1)} %get-tuple-element.520.keys_ref, ...), custom_call_target="tpu_custom_call" | custom-call | flops 21474836480 | bytes 8388608 | tf_op jit(solution)/shard_map/attention_backward/pallas_call | solution.py:383
  783.3 10.7 %fusion.60 = bf16[2048,768]{1,0:T(8,128)(2,1)S(1)} fusion(bf16[1024,2048]{1,0:T(8,128)(2,1)} %copy-done.40, bf16[1024,2048]{1,0:T(8,128)(2,1)} %copy-done.39, bf16[1024,768]{1,0:T(8,128)(2,1)} %copy-done.74, bf16[1024,768]{1,0:T(8,128)(2,1)} %constant_dynamic-update-slice_fusion.59), kind=kOutput, calls=%fused_computation.65 | convolution fusion | flops 6467092480 | bytes 14680064 | tf_op jit(solution)/shard_map/dot_general | solution.py:25
  874.3 42.3 %reduce-scatter.8.cloned.1.call-done = bf16[256,1408]{1,0:T(8,128)(2,1)} async-done(((bf16[2048,1408]{1,0:T(8,128)(2,1)}), bf16[256,1408]{1,0:T(8,128)(2,1)}) %reduce-scatter.8.cloned.1.call-update) | async-done | bytes 720912 | tf_op jit(solution)/shard_map/reduce_scatter | solution.py:144
  (640 shorter events, 441.3 us)
Async XLA Ops:
  7.2 67.1 %all-gather.5.cloned.1.call-start = ((), (), s32[]{:S(2)}) async-start(), calls=%async_computation.3 | async-start | bytes 4128768 | tf_op jit(solution)/shard_map/all_gather | solution.py:129
  21.0 104.7 %all-gather.7.cloned.1.call-start = ((), (), s32[]{:S(2)}) async-start(), calls=%async_computation.4 | async-start | bytes 2359296 | tf_op jit(solution)/shard_map/all_gather | solution.py:129
  58.4 262.0 %all-gather.9.cloned.1.call-start = ((), (), s32[]{:S(2)}) async-start(), calls=%async_computation.5 | async-start | bytes 21233664 | tf_op jit(solution)/shard_map/all_gather | solution.py:129
  99.3 267.0 %all-gather.11.cloned.1.call-start = ((), (), s32[]{:S(2)}) async-start(), calls=%async_computation.6 | async-start | bytes 7077888 | tf_op jit(solution)/shard_map/all_gather | solution.py:129
  155.1 43.3 %collective-permute-start.23 = (bf16[256,2048]{1,0:T(8,128)(2,1)S(1)}, bf16[256,2048]{1,0:T(8,128)(2,1)S(1)}, u32[]{:S(2)}, u32[]{:S(2)}) collective-permute-start(bf16[256,2048]{1,0:T(8,128)(2,1)S(1)} %copy-done.42), channel_id=1, source_target_pairs={{0,1},{1,0},{2,3},{3,2},{4,5},{5,4},{6,7},{7,6},{8,9},{9,8},{10,11... | collective-permute-start | bytes 3145736 | tf_op jit(solution)/shard_map/ppermute | solution.py:51
  155.8 43.5 %collective-permute-start.24 = (bf16[256,2048]{1,0:T(8,128)(2,1)S(1)}, bf16[256,2048]{1,0:T(8,128)(2,1)S(1)}, u32[]{:S(2)}, u32[]{:S(2)}) collective-permute-start(bf16[256,2048]{1,0:T(8,128)(2,1)S(1)} %copy-done.42), channel_id=1, source_target_pairs={{0,2},{1,3},{2,0},{3,1},{4,6},{5,7},{6,4},{7,5},{8,10},{9,11},{10,... | collective-permute-start | bytes 3145736 | tf_op jit(solution)/shard_map/ppermute | solution.py:51
  201.5 35.9 %collective-permute-start.21 = (bf16[256,2048]{1,0:T(8,128)(2,1)S(1)}, bf16[256,2048]{1,0:T(8,128)(2,1)S(1)}, u32[]{:S(2)}, u32[]{:S(2)}) collective-permute-start(bf16[256,2048]{1,0:T(8,128)(2,1)S(1)} %get-tuple-element.359), channel_id=1, source_target_pairs={{0,1},{1,0},{2,3},{3,2},{4,5},{5,4},{6,7},{7,6},{8,9},{9,8},{10,11... | collective-permute-start | bytes 3145736 | tf_op jit(solution)/shard_map/ppermute | solution.py:51
  207.9 40.7 %collective-permute-start.29 = (bf16[128,2048]{1,0:T(8,128)(2,1)S(1)}, bf16[128,2048]{1,0:T(8,128)(2,1)S(1)}, u32[]{:S(2)}, u32[]{:S(2)}) collective-permute-start(bf16[128,2048]{1,0:T(8,128)(2,1)S(1)} %get-tuple-element.379), channel_id=1, source_target_pairs={{0,1},{1,0},{2,3},{3,2},{4,5},{5,4},{6,7},{7,6},{8,9},{9,8},{10,11... | collective-permute-start | bytes 1572872 | tf_op jit(solution)/shard_map/ppermute | solution.py:51
  266.5 426.8 %reduce-scatter.4.cloned.1.call-start = ((), (), s32[]{:S(2)}) async-start(), calls=%async_computation.7 | async-start | bytes 14155776 | tf_op jit(solution)/shard_map/reduce_scatter | solution.py:144
  274.0 44.4 %collective-permute-start.36 = (bf16[256,2048]{1,0:T(8,128)(2,1)}, bf16[256,2048]{1,0:T(8,128)(2,1)S(1)}, u32[]{:S(2)}, u32[]{:S(2)}) collective-permute-start(bf16[256,2048]{1,0:T(8,128)(2,1)} %get-tuple-element.484), channel_id=1, source_target_pairs={{0,1},{1,0},{2,3},{3,2},{4,5},{5,4},{6,7},{7,6},{8,9},{9,8},{10,11... | collective-permute-start | bytes 3145736 | tf_op jit(solution)/shard_map/ppermute | solution.py:51
  274.9 73.9 %collective-permute-start.37 = (bf16[256,2048]{1,0:T(8,128)(2,1)}, bf16[256,2048]{1,0:T(8,128)(2,1)}, u32[]{:S(2)}, u32[]{:S(2)}) collective-permute-start(bf16[256,2048]{1,0:T(8,128)(2,1)} %get-tuple-element.484), channel_id=1, source_target_pairs={{0,2},{1,3},{2,0},{3,1},{4,6},{5,7},{6,4},{7,5},{8,10},{9,11},{10,... | collective-permute-start | bytes 3145736 | tf_op jit(solution)/shard_map/ppermute | solution.py:51
  301.4 47.4 %collective-permute-start.38 = (bf16[256,2048]{1,0:T(8,128)(2,1)}, bf16[256,2048]{1,0:T(8,128)(2,1)}, u32[]{:S(2)}, u32[]{:S(2)}) collective-permute-start(bf16[256,2048]{1,0:T(8,128)(2,1)} %get-tuple-element.403), channel_id=1, source_target_pairs={{0,1},{1,0},{2,3},{3,2},{4,5},{5,4},{6,7},{7,6},{8,9},{9,8},{10,11... | collective-permute-start | bytes 3145736 | tf_op jit(solution)/shard_map/ppermute | solution.py:51
  302.8 46.0 %collective-permute-start.39 = (bf16[256,2048]{1,0:T(8,128)(2,1)}, bf16[256,2048]{1,0:T(8,128)(2,1)}, u32[]{:S(2)}, u32[]{:S(2)}) collective-permute-start(bf16[256,2048]{1,0:T(8,128)(2,1)} %get-tuple-element.403), channel_id=1, source_target_pairs={{0,2},{1,3},{2,0},{3,1},{4,6},{5,7},{6,4},{7,5},{8,10},{9,11},{10,... | collective-permute-start | bytes 3145736 | tf_op jit(solution)/shard_map/ppermute | solution.py:51
  487.3 357.5 %reduce-scatter.6.cloned.1.call-start = ((), (), s32[]{:S(2)}) async-start(), calls=%async_computation.8 | async-start | bytes 14155776 | tf_op jit(solution)/shard_map/reduce_scatter | solution.py:144
  516.9 45.2 %collective-permute-start.48 = (bf16[256,2048]{1,0:T(8,128)(2,1)S(1)}, bf16[256,2048]{1,0:T(8,128)(2,1)S(1)}, u32[]{:S(2)}, u32[]{:S(2)}) collective-permute-start(bf16[256,2048]{1,0:T(8,128)(2,1)S(1)} %get-tuple-element.451), channel_id=1, source_target_pairs={{0,1},{1,0},{2,3},{3,2},{4,5},{5,4},{6,7},{7,6},{8,9},{9,8},{10,11... | collective-permute-start | bytes 3145736 | tf_op jit(solution)/shard_map/ppermute | solution.py:51
  516.9 45.2 %collective-permute-start.49 = (bf16[256,2048]{1,0:T(8,128)(2,1)S(1)}, bf16[256,2048]{1,0:T(8,128)(2,1)S(1)}, u32[]{:S(2)}, u32[]{:S(2)}) collective-permute-start(bf16[256,2048]{1,0:T(8,128)(2,1)S(1)} %get-tuple-element.451), channel_id=1, source_target_pairs={{0,2},{1,3},{2,0},{3,1},{4,6},{5,7},{6,4},{7,5},{8,10},{9,11},{10,... | collective-permute-start | bytes 3145736 | tf_op jit(solution)/shard_map/ppermute | solution.py:51
  588.9 57.3 %collective-permute-start.50 = (bf16[128,2048]{1,0:T(8,128)(2,1)}, bf16[128,2048]{1,0:T(8,128)(2,1)}, u32[]{:S(2)}, u32[]{:S(2)}) collective-permute-start(bf16[128,2048]{1,0:T(8,128)(2,1)} %get-tuple-element.456), channel_id=1, source_target_pairs={{0,1},{1,0},{2,3},{3,2},{4,5},{5,4},{6,7},{7,6},{8,9},{9,8},{10,11... | collective-permute-start | bytes 1572872 | tf_op jit(solution)/shard_map/ppermute | solution.py:51
  589.9 56.4 %collective-permute-start.51 = (bf16[128,2048]{1,0:T(8,128)(2,1)}, bf16[128,2048]{1,0:T(8,128)(2,1)}, u32[]{:S(2)}, u32[]{:S(2)}) collective-permute-start(bf16[128,2048]{1,0:T(8,128)(2,1)} %get-tuple-element.457), channel_id=1, source_target_pairs={{0,2},{1,3},{2,0},{3,1},{4,6},{5,7},{6,4},{7,5},{8,10},{9,11},{10,... | collective-permute-start | bytes 1572872 | tf_op jit(solution)/shard_map/ppermute | solution.py:51
  591.7 65.1 %collective-permute-start.58 = (bf16[256,2048]{1,0:T(8,128)(2,1)}, bf16[256,2048]{1,0:T(8,128)(2,1)}, u32[]{:S(2)}, u32[]{:S(2)}) collective-permute-start(bf16[256,2048]{1,0:T(8,128)(2,1)} %pad_maximum_fusion.9), channel_id=1, source_target_pairs={{0,1},{1,0},{2,3},{3,2},{4,5},{5,4},{6,7},{7,6},{8,9},{9,8},{10,11... | collective-permute-start | bytes 3145736 | tf_op jit(solution)/shard_map/ppermute | solution.py:51
  593.9 62.9 %collective-permute-start.59 = (bf16[256,2048]{1,0:T(8,128)(2,1)}, bf16[256,2048]{1,0:T(8,128)(2,1)}, u32[]{:S(2)}, u32[]{:S(2)}) collective-permute-start(bf16[256,2048]{1,0:T(8,128)(2,1)} %pad_maximum_fusion.10), channel_id=1, source_target_pairs={{0,2},{1,3},{2,0},{3,1},{4,6},{5,7},{6,4},{7,5},{8,10},{9,11},{10,... | collective-permute-start | bytes 3145736 | tf_op jit(solution)/shard_map/ppermute | solution.py:51
  651.8 41.5 %collective-permute-start.56 = (bf16[256,2048]{1,0:T(8,128)(2,1)}, bf16[256,2048]{1,0:T(8,128)(2,1)}, u32[]{:S(2)}, u32[]{:S(2)}) collective-permute-start(bf16[256,2048]{1,0:T(8,128)(2,1)} %pad_maximum_fusion.11), channel_id=1, source_target_pairs={{0,1},{1,0},{2,3},{3,2},{4,5},{5,4},{6,7},{7,6},{8,9},{9,8},{10,11... | collective-permute-start | bytes 3145736 | tf_op jit(solution)/shard_map/ppermute | solution.py:51
  652.9 40.5 %collective-permute-start.57 = (bf16[256,2048]{1,0:T(8,128)(2,1)}, bf16[256,2048]{1,0:T(8,128)(2,1)}, u32[]{:S(2)}, u32[]{:S(2)}) collective-permute-start(bf16[256,2048]{1,0:T(8,128)(2,1)} %pad_maximum_fusion.12), channel_id=1, source_target_pairs={{0,2},{1,3},{2,0},{3,1},{4,6},{5,7},{6,4},{7,5},{8,10},{9,11},{10,... | collective-permute-start | bytes 3145736 | tf_op jit(solution)/shard_map/ppermute | solution.py:51
  693.3 223.3 %reduce-scatter.8.cloned.1.call-start = ((), (), s32[]{:S(2)}) async-start(), calls=%async_computation.9 | async-start | bytes 6488064 | tf_op jit(solution)/shard_map/reduce_scatter | solution.py:144
  772.5 37.2 %collective-permute-start.65 = (bf16[256,2048]{1,0:T(8,128)(2,1)}, bf16[256,2048]{1,0:T(8,128)(2,1)S(1)}, u32[]{:S(2)}, u32[]{:S(2)}) collective-permute-start(bf16[256,2048]{1,0:T(8,128)(2,1)} %pad_maximum_fusion.14), channel_id=1, source_target_pairs={{0,2},{1,3},{2,0},{3,1},{4,6},{5,7},{6,4},{7,5},{8,10},{9,11},{10,... | collective-permute-start | bytes 3145736 | tf_op jit(solution)/shard_map/ppermute | solution.py:51
  (186 other events, 2742.1 us)
Sparse Core Ops, SparseCore 0:
  21.2 43.7 all-gather.4
  67.2 27.9 all-gather.6
  99.4 169.1 all-gather.8
  270.1 62.9 all-gather.10
  487.5 128.8 reduce-scatter.3
  693.4 129.8 reduce-scatter.5
  844.9 71.6 reduce-scatter.7

commit v3 on v2

--- a/solution.py
+++ b/solution.py
@@ -63,44 +63,22 @@
         one, two = self.after(near)
         return self.send((one[:half], 2), (two[half:], 1))
 
-    def gathered(self, own, near, far):
-        if not square():
-            return lax.all_gather(own, "ctx", axis=0, tiled=True)
-        self.wait(*far)
-        return jnp.concatenate([own, *near, *far], axis=0)
-
     def scatter_near(self, parts):
-        if not square():
-            return []
-        across = 3 * (parts.shape[0] // 4)
-        half = parts.shape[0] // 8
-        return self.send((parts[across : across + half], 1), (parts[across + half :], 2))
+        return self.send((parts[1], 1), (parts[2], 2)) if square() else []
 
     def scatter_far(self, parts, near):
         if not square():
             return []
-        rows = parts.shape[0] // 4
-        half = rows // 2
-
-        def add(parts, low, high):
-            one, two = parts[rows : 2 * rows], parts[2 * rows : 3 * rows]
-            one_high = (one[half:].astype(F32) + high.astype(F32)).astype(BF16)
-            two_low = (two[:half].astype(F32) + low.astype(F32)).astype(BF16)
-            return (
-                jnp.concatenate([one[:half], one_high], axis=0),
-                jnp.concatenate([two_low, two[half:]], axis=0),
-            )
+
+        def add(own, one, two):
+            half = one.shape[0] // 2
+            for_one = own[2 * half : 3 * half].astype(F32) + two[half:].astype(F32)
+            for_two = own[3 * half :].astype(F32) + one[half:].astype(F32)
+            return for_one.astype(BF16), for_two.astype(BF16)
 
         self.wait(*near)
-        one, two = self.run(add, parts, *near)
-        return self.send((one, 1), (two, 2))
-
-    def scattered(self, parts, far):
-        if not square():
-            return lax.psum_scatter(parts, "ctx", scatter_dimension=0, tiled=True).astype(F32)
-        self.wait(*far)
-        own = parts[: parts.shape[0] // 4]
-        return own.astype(F32) + far[0].astype(F32) + far[1].astype(F32)
+        for_one, for_two = self.run(add, parts[0], *near)
+        return self.send((for_one, 1), (for_two, 2))
 
     def exchange(self, block_for):
         size = lax.axis_size("ctx")
@@ -138,6 +116,29 @@
 
 def square():
     return lax.axis_size("ctx") == 4
+
+
+HALVES = ((0, 0), (0, 1), (1, 1), (2, 0), (1, 0), (3, 0), (2, 1), (3, 1))
+
+
+def gathered(own, near, far):
+    if not square():
+        return lax.all_gather(own, "ctx", axis=0, tiled=True)
+    half = own.shape[0] // 2
+    one, two = near
+    low, high = far
+    return jnp.concatenate(
+        [own, one[half:], two[:half], one[:half], low, two[half:], high], axis=0
+    )
+
+
+def scattered(parts, near, far):
+    if not square():
+        return lax.psum_scatter(parts[0], "ctx", scatter_dimension=0, tiled=True).astype(F32)
+    half = near[0].shape[0] // 2
+    low = parts[0][:half].astype(F32) + near[0][:half].astype(F32) + far[1].astype(F32)
+    high = parts[0][half : 2 * half].astype(F32) + near[1][:half].astype(F32) + far[0].astype(F32)
+    return jnp.concatenate([low, high], axis=0)
 
 
 def sum_over_dp(grads):
@@ -468,40 +469,89 @@
     )(feed_in, down_in, weights, weights)
 
 
-def spread_kernel(*refs):
-    count = (len(refs) - 1) // 2
+def spread_kernel(*refs, count):
     total = sum(dot(refs[i][...], refs[count + i][...], NT) for i in range(count))
-    refs[-1][...] = total.astype(BF16)
-
-
-def feed_spread(lefts, weights, places, tile):
+    total = total.astype(BF16)
+    start = 0
+    for out in refs[2 * count :]:
+        out[...] = total[start : start + out.shape[0]]
+        start += out.shape[0]
+
+
+def spread_rows(lefts, weights, places, tile):
     rows = lefts[0].shape[0]
     depth = weights[0].shape[0]
     widths = [left.shape[1] for left in lefts]
     work = rows * depth * sum(widths)
-
-    step = min(512, rows)
+    outs = [rows // 2, rows // 4, rows // 4] if square() else [rows]
 
     def weight_spec(width, place):
-        return pl.BlockSpec((tile, width), lambda i, j: (j, place))
+        return pl.BlockSpec((tile, width), lambda j: (j, place))
 
     return pl.pallas_call(
-        spread_kernel,
-        grid=(rows // step, depth // tile),
-        in_specs=[pl.BlockSpec((step, width), lambda i, j: (i, 0)) for width in widths]
+        functools.partial(spread_kernel, count=len(lefts)),
+        grid=(depth // tile,),
+        in_specs=[
+            pl.BlockSpec((rows, width), lambda j: (0, 0), pipeline_mode=pl.Buffered(1))
+            for width in widths
+        ]
         + [weight_spec(width, place) for width, place in zip(widths, places)],
-        out_specs=pl.BlockSpec((step, tile), lambda i, j: (i, j)),
-        out_shape=jax.ShapeDtypeStruct((rows, depth), BF16),
+        out_specs=[pl.BlockSpec((each, tile), lambda j: (0, j)) for each in outs],
+        out_shape=[jax.ShapeDtypeStruct((each, depth), BF16) for each in outs],
         compiler_params=pltpu.CompilerParams(
-            dimension_semantics=("arbitrary", "arbitrary"), vmem_limit_bytes=56 << 20
+            dimension_semantics=("arbitrary",), vmem_limit_bytes=56 << 20
         ),
         cost_estimate=pl.CostEstimate(
             flops=2 * work,
             bytes_accessed=2 * ((rows + depth) * sum(widths) + rows * depth),
             transcendentals=0,
         ),
-        name="feed_spread",
+        name="spread_rows",
     )(*lefts, *weights)
+
+
+def token_kernel(*refs, seqs, pair_tiles):
+    feeds, downs, pairs, acts = (refs[at * seqs : (at + 1) * seqs] for at in range(4))
+    column = pl.program_id(0)
+
+    @pl.when(column < pair_tiles)
+    def _():
+        total = sum(dot(left[...], right[...], TN) for left, right in zip(feeds, pairs))
+        refs[-1][...] = total.astype(BF16)
+
+    @pl.when(column >= pair_tiles)
+    def _():
+        total = sum(dot(left[...], right[...], TN) for left, right in zip(downs, acts))
+        refs[-1][...] = total.astype(BF16)
+
+
+def feed_grads(feeds, downs, pairs, acts, tile):
+    seqs = len(feeds)
+    rows, depth = feeds[0].shape
+    pair_tiles, act_tiles = pairs[0].shape[1] // tile, acts[0].shape[1] // tile
+    step = min(512, depth)
+    columns = (pair_tiles + act_tiles) * tile
+    left_pair = pl.BlockSpec((rows, step), lambda j, i: (0, jnp.where(j < pair_tiles, i, 0)))
+    left_act = pl.BlockSpec((rows, step), lambda j, i: (0, jnp.where(j < pair_tiles, 0, i)))
+    pair = pl.BlockSpec((rows, tile), lambda j, i: (0, jnp.minimum(j, pair_tiles - 1)))
+    act = pl.BlockSpec((rows, tile), lambda j, i: (0, jnp.maximum(j - pair_tiles, 0)))
+    work = seqs * rows * depth * columns
+    return pl.pallas_call(
+        functools.partial(token_kernel, seqs=seqs, pair_tiles=pair_tiles),
+        grid=(pair_tiles + act_tiles, depth // step),
+        in_specs=[left_pair] * seqs + [left_act] * seqs + [pair] * seqs + [act] * seqs,
+        out_specs=pl.BlockSpec((step, tile), lambda j, i: (i, j)),
+        out_shape=jax.ShapeDtypeStruct((depth, columns), BF16),
+        compiler_params=pltpu.CompilerParams(
+            dimension_semantics=("arbitrary", "arbitrary"), vmem_limit_bytes=56 << 20
+        ),
+        cost_estimate=pl.CostEstimate(
+            flops=2 * work,
+            bytes_accessed=2 * (2 * seqs * rows * depth + (seqs * rows + depth) * columns),
+            transcendentals=0,
+        ),
+        name="feed_grads",
+    )(*feeds, *downs, *pairs, *acts)
 
 
 def lay_kernel(place_ref, *refs, plan, inputs):
@@ -617,18 +667,19 @@
 
     assert seqs == 2 and len(chunks) <= 2
     many = len(chunks) > 1
-    last_part = len(chunks) - 1
     qkv_width = query_width + 2 * key_width
 
     slots = jnp.argsort(span_order, axis=1).astype(jnp.int32)
     if square():
-        slots = ((slots // 2) ^ rank) * 2 + slots % 2
+        places = [HALVES.index((member, half)) for member in range(4) for half in range(2)]
+        slots = jnp.array(places, jnp.int32)[((slots // 2) ^ rank) * 2 + slots % 2]
     cos_lanes, sin_lanes = rope_lanes(length)
 
-    def project(rows, weight, gain):
+    def project(own, near, far, weight, gain):
+        rows = gathered(own, near, far)
         normed, _ = norm_forward(rows.astype(F32))
-        rows = (normed * gain).astype(BF16)
-        return rows, dot(rows, weight)
+        attn_in = (normed * gain).astype(BF16)
+        return rows, attn_in, dot(attn_in, weight)
 
     def attend(qkv, slots):
         return attention_forward(
@@ -636,9 +687,10 @@
         )
 
     def merge_back(rows, weight):
-        return dot(rows, weight, NT, BF16)
-
-    def feed_norm(hidden, gain):
+        return spread_rows([rows], [weight], [0], tile)
+
+    def feed_norm(rows, branch, near, far, gain):
+        hidden = rows.astype(F32) + scattered(branch, near, far)
         normed, _ = norm_forward(hidden)
         return hidden, (normed * gain).astype(BF16)
 
@@ -646,38 +698,44 @@
         return feed_middle(feed_in, down_in, weights, chunks[part], tile)
 
     def feed_back(grads, weights):
-        return feed_spread(grads, weights, [0] * len(grads), tile)
+        return spread_rows(grads, weights, [0] * len(grads), tile)
 
     def feed_out(activated, weights):
-        return feed_spread(activated, weights, [2] * len(activated), tile)
+        return spread_rows(activated, weights, [2] * len(activated), tile)
 
     def token_grads(left, right):
         return dot(jnp.concatenate(left, axis=0), jnp.concatenate(right, axis=0), TN, BF16)
 
-    def last_grads(feed_in, grads, down_in, activated):
-        activated = [jnp.concatenate(parts, axis=1) for parts in activated]
-        down = token_grads(down_in, activated)
-        if not many:
-            return down
-        return jnp.concatenate([token_grads(feed_in, grads), down], axis=1)
-
-    def feed_norm_back(hidden, summed, cot, gain):
+    def feed_grads_of(feed_in, down_in, middle, part):
+        return feed_grads(
+            feed_in, down_in, [m[1] for m in middle], [m[0] for m in middle], chunks[part]
+        )
+
+    def feed_norm_back(hidden, parts, near, far, cot, gain):
         normed, inverse = norm_forward(hidden)
-        grad_middle, gain_part = norm_backward(summed, normed, inverse, gain)
+        grad_middle, gain_part = norm_backward(
+            scattered(parts, near, far), normed, inverse, gain
+        )
         grad_hidden = cot.astype(F32) + grad_middle
         return grad_hidden, grad_hidden.astype(BF16), gain_part
 
-    def attend_back(merge_in, weight, kept, slots):
+    def attend_back(own, near, far, weight, kept, slots):
+        merge_in = gathered(own, near, far)
         grad_attn = dot(merge_in, weight, NN, BF16)
         parts = attention_backward(kept, grad_attn, slots, cos_lanes, sin_lanes, group_size)
-        return jnp.concatenate(parts, axis=1)
+        return merge_in, jnp.concatenate(parts, axis=1)
 
     def project_back(grads, weight):
-        return dot(grads, weight, NT, BF16)
+        return spread_rows([grads], [weight], [0], tile)
 
     def gain_part_of(rows, lower):
         normed, _ = norm_forward(rows.astype(F32))
-        return jnp.sum(normed * lower.astype(F32), axis=0)
+        total, start = 0.0, 0
+        for part in lower:
+            here = slice(start, start + part.shape[0])
+            total = total + jnp.sum(normed[here] * part.astype(F32), axis=0)
+            start += part.shape[0]
+        return total
 
     def attention_grads_of(attn_in, grad_qkv, merge_in, attn_out, rows, lower, gain_two_parts):
         gain_one_sum = sum(gain_part_of(r, l) for r, l in zip(rows, lower))
@@ -691,10 +749,16 @@
             axis=1,
         )
 
-    def project_norm_back(rows, summed, grad_hidden, gain):
+    def project_norm_back(rows, parts, near, far, grad_hidden, gain):
         normed, inverse = norm_forward(rows.astype(F32))
-        grad_lower, _ = norm_backward(summed, normed, inverse, gain)
+        grad_lower, _ = norm_backward(scattered(parts, near, far), normed, inverse, gain)
         return grad_hidden + grad_lower
+
+    def block_of(hidden, parts, near, far):
+        return (hidden + scattered(parts, near, far)).astype(BF16)
+
+    def only(*values):
+        return values
 
     moved = chain.exchange(projections_for)
     a_near = chain.gather_near(tokens[0])
@@ -703,100 +767,116 @@
     merge = chain.all_rows(moved)
     a_far = chain.gather_far(a_near)
     moved = chain.exchange(feed_for(0))
-    rows_a = chain.gathered(tokens[0], a_near, a_far)
+    chain.wait(*a_far)
     b_near = chain.gather_near(tokens[1])
-
-    qkv_weight = projections[:, :qkv_width]
     gains = projections[:, qkv_width : qkv_width + 2].astype(F32)
     gain_one, gain_two = gains[:, 0], gains[:, 1]
-    attn_in_a, qkv = chain.run(project, rows_a, qkv_weight, gain_one)
+    rows_a, attn_in_a, qkv = chain.run(
+        project, tokens[0], a_near, a_far, projections[:, :qkv_width], gain_one
+    )
     feeds = [chain.all_rows(moved)]
     attn_out_a, *kept_a = chain.run(attend, qkv, slots[0])
+    b_far = chain.gather_far(b_near)
     branch_a = chain.run(merge_back, attn_out_a, merge)
     near_a = chain.scatter_near(branch_a)
-    b_far = chain.gather_far(b_near)
+    chain.wait(*b_far)
+    rows_b, attn_in_b, qkv = chain.run(
+        project, tokens[1], b_near, b_far, projections[:, :qkv_width], gain_one
+    )
     far_a = chain.scatter_far(branch_a, near_a)
-    rows_b = chain.gathered(tokens[1], b_near, b_far)
     cot_a_near = chain.gather_near(out_grad[0])
-    attn_in_b, qkv = chain.run(project, rows_b, qkv_weight, gain_one)
-    hidden_a, feed_a = chain.run(
-        feed_norm, tokens[0].astype(F32) + chain.scattered(branch_a, far_a), gain_two
-    )
+    attn_out_b, *kept_b = chain.run(attend, qkv, slots[1])
+    chain.wait(*far_a)
+    hidden_a, feed_a = chain.run(feed_norm, tokens[0], branch_a, near_a, far_a, gain_two)
     feed_a_near = chain.gather_near(feed_a)
-    attn_out_b, *kept_b = chain.run(attend, qkv, slots[1])
+    branch_b = chain.run(merge_back, attn_out_b, merge)
+    chain.wait(*cot_a_near)
+    if many:
+        moved = chain.exchange(feed_for(1))
     cot_a_far = chain.gather_far(cot_a_near)
-    branch_b = chain.run(merge_back, attn_out_b, merge)
     near_b = chain.scatter_near(branch_b)
     feed_a_far = chain.gather_far(feed_a_near)
-    down_in_a = chain.gathered(out_grad[0], cot_a_near, cot_a_far)
-    if many:
-        moved = chain.exchange(feed_for(1))
-    far_b = chain.scatter_far(branch_b, near_b)
-    feed_in_a = chain.gathered(feed_a, feed_a_near, feed_a_far)
-    cot_b_near = chain.gather_near(out_grad[1])
+    chain.wait(*cot_a_far)
+    down_in_a = chain.run(gathered, out_grad[0], cot_a_near, cot_a_far)
     if many:
         feeds.append(chain.all_rows(moved))
-    hidden_b, feed_b = chain.run(
-        feed_norm, tokens[1].astype(F32) + chain.scattered(branch_b, far_b), gain_two
-    )
+    far_b = chain.scatter_far(branch_b, near_b)
+    chain.wait(*feed_a_far)
+    cot_b_near = chain.gather_near(out_grad[1])
+    feed_in_a = chain.run(gathered, feed_a, feed_a_near, feed_a_far)
+    middle_a = [chain.run(lambda f, d, w: middle_of(f, d, w, 0), feed_in_a, down_in_a, feeds[0])]
+    chain.wait(*far_b)
+    hidden_b, feed_b = chain.run(feed_norm, tokens[1], branch_b, near_b, far_b, gain_two)
     feed_b_near = chain.gather_near(feed_b)
-    middle_a = [chain.run(lambda f, d, w: middle_of(f, d, w, 0), feed_in_a, down_in_a, feeds[0])]
     cot_b_far = chain.gather_far(cot_b_near)
-    feed_b_far = chain.gather_far(feed_b_near)
-    down_in_b = chain.gathered(out_grad[1], cot_b_near, cot_b_far)
-    feed_in_b = chain.gathered(feed_b, feed_b_near, feed_b_far)
     if many:
         middle_a.append(
             chain.run(lambda f, d, w: middle_of(f, d, w, 1), feed_in_a, down_in_a, feeds[1])
         )
+    feed_b_far = chain.gather_far(feed_b_near)
     back_a = chain.run(feed_back, [m[1] for m in middle_a], feeds)
     near_a = chain.scatter_near(back_a)
+    chain.wait(*cot_b_far, *feed_b_far)
+    down_in_b = chain.run(gathered, out_grad[1], cot_b_near, cot_b_far)
+    feed_in_b = chain.run(gathered, feed_b, feed_b_near, feed_b_far)
     middle_b = [chain.run(lambda f, d, w: middle_of(f, d, w, 0), feed_in_b, down_in_b, feeds[0])]
     far_a = chain.scatter_far(back_a, near_a)
     grads_first = chain.run(
-        token_grads, [feed_in_a, feed_in_b], [middle_a[0][1], middle_b[0][1]]
-    )
-    sums_first = sum_over_dp(grads_first)
+        lambda f, d, m: feed_grads_of(f, d, m, 0),
+        [feed_in_a, feed_in_b], [down_in_a, down_in_b], [middle_a[0], middle_b[0]],
+    )
+    chain.wait(*far_a)
+    sums = [sum_over_dp(*chain.run(only, grads_first))]
     grad_hidden_a, merge_a, gain_two_a = chain.run(
-        feed_norm_back, hidden_a, chain.scattered(back_a, far_a), out_grad[0], gain_two
+        feed_norm_back, hidden_a, back_a, near_a, far_a, out_grad[0], gain_two
     )
     merge_a_near = chain.gather_near(merge_a)
     if many:
         middle_b.append(
             chain.run(lambda f, d, w: middle_of(f, d, w, 1), feed_in_b, down_in_b, feeds[1])
         )
+    merge_a_far = chain.gather_far(merge_a_near)
     back_b = chain.run(feed_back, [m[1] for m in middle_b], feeds)
     near_b = chain.scatter_near(back_b)
-    merge_a_far = chain.gather_far(merge_a_near)
+    chain.wait(*merge_a_far)
+    merge_in_a, grad_qkv_a = chain.run(
+        attend_back, merge_a, merge_a_near, merge_a_far, merge, kept_a, slots[0]
+    )
+    far_b = chain.scatter_far(back_b, near_b)
+    lower_a = chain.run(project_back, grad_qkv_a, projections)
+    lower_a_near = chain.scatter_near(lower_a)
     out_a = chain.run(feed_out, [m[0] for m in middle_a], feeds)
+    chain.wait(*far_b)
+    grad_hidden_b, merge_b, gain_two_b = chain.run(
+        feed_norm_back, hidden_b, back_b, near_b, far_b, out_grad[1], gain_two
+    )
+    merge_b_near = chain.gather_near(merge_b)
+    lower_a_far = chain.scatter_far(lower_a, lower_a_near)
+    if many:
+        grads_last = chain.run(
+            lambda f, d, m: feed_grads_of(f, d, m, 1),
+            [feed_in_a, feed_in_b], [down_in_a, down_in_b], [middle_a[1], middle_b[1]],
+        )
+    merge_b_far = chain.gather_far(merge_b_near)
     out_a_near = chain.scatter_near(out_a)
-    far_b = chain.scatter_far(back_b, near_b)
-    merge_in_a = chain.gathered(merge_a, merge_a_near, merge_a_far)
-    grads_last = chain.run(
-        last_grads,
-        [feed_in_a, feed_in_b],
-        [middle_a[last_part][1], middle_b[last_part][1]],
-        [down_in_a, down_in_b],
-        [[m[0] for m in middle_a], [m[0] for m in middle_b]],
-    )
+    chain.wait(*lower_a_far)
+    input_grad_a = chain.run(
+        project_norm_back, tokens[0], lower_a, lower_a_near, lower_a_far, grad_hidden_a, gain_one
+    )
+    out_b = chain.run(feed_out, [m[0] for m in middle_b], feeds)
+    chain.wait(*merge_b_far)
+    if many:
+        chain.wait(sums[0])
+        sums.append(sum_over_dp(*chain.run(only, grads_last)))
     out_a_far = chain.scatter_far(out_a, out_a_near)
-    grad_hidden_b, merge_b, gain_two_b = chain.run(
-        feed_norm_back, hidden_b, chain.scattered(back_b, far_b), out_grad[1], gain_two
-    )
-    merge_b_near = chain.gather_near(merge_b)
-    grad_qkv_a = chain.run(attend_back, merge_in_a, merge, kept_a, slots[0])
-    chain.wait(sums_first)
-    sums_last = sum_over_dp(chain.run(lambda g: g, grads_last))
-    merge_b_far = chain.gather_far(merge_b_near)
-    lower_a = chain.run(project_back, grad_qkv_a, qkv_weight)
-    lower_a_near = chain.scatter_near(lower_a)
-    out_b = chain.run(feed_out, [m[0] for m in middle_b], feeds)
-    lower_a_far = chain.scatter_far(lower_a, lower_a_near)
-    merge_in_b = chain.gathered(merge_b, merge_b_near, merge_b_far)
     out_b_near = chain.scatter_near(out_b)
-    grad_qkv_b = chain.run(attend_back, merge_in_b, merge, kept_b, slots[1])
-    lower_b = chain.run(project_back, grad_qkv_b, qkv_weight)
+    merge_in_b, grad_qkv_b = chain.run(
+        attend_back, merge_b, merge_b_near, merge_b_far, merge, kept_b, slots[1]
+    )
+    lower_b = chain.run(project_back, grad_qkv_b, projections)
     lower_b_near = chain.scatter_near(lower_b)
+    chain.wait(*out_a_far)
+    block_a = chain.run(block_of, hidden_a, out_a, out_a_near, out_a_far)
     out_b_far = chain.scatter_far(out_b, out_b_near)
     attention_grads = chain.run(
         attention_grads_of,
@@ -808,31 +888,31 @@
         [lower_a, lower_b],
         [gain_two_a, gain_two_b],
     )
+    chain.wait(sums[-1])
+    attention_sums = sum_over_dp(*chain.run(only, attention_grads))
     lower_b_far = chain.scatter_far(lower_b, lower_b_near)
-    moved_first = chain.own_rows(sums_first)
-    input_grad_a = chain.run(
-        project_norm_back, tokens[0], chain.scattered(lower_a, lower_a_far), grad_hidden_a, gain_one
-    )
-    block_a = chain.run(lambda h, o: (h + o).astype(BF16), hidden_a, chain.scattered(out_a, out_a_far))
-    block_b = chain.run(lambda h, o: (h + o).astype(BF16), hidden_b, chain.scattered(out_b, out_b_far))
+    moved_feed = [chain.own_rows(sums[0])]
+    chain.wait(*out_b_far)
+    block_b = chain.run(block_of, hidden_b, out_b, out_b_near, out_b_far)
+    chain.wait(*lower_b_far)
     input_grad_b = chain.run(
-        project_norm_back, tokens[1], chain.scattered(lower_b, lower_b_far), grad_hidden_b, gain_one
-    )
-    chain.wait(sums_last)
-    attention_sums = sum_over_dp(chain.run(lambda g: g, attention_grads))
-    moved_last = chain.own_rows(sums_last)
-    chain.wait(*moved_last[1:])
+        project_norm_back, tokens[1], lower_b, lower_b_near, lower_b_far, grad_hidden_b, gain_one
+    )
+    chain.wait(*moved_feed[0][1:])
+    moved_feed += [chain.own_rows(part) for part in sums[1:]]
+    chain.wait(*moved_feed[-1][1:])
     blocks = [block_a, block_b]
     input_grad = [input_grad_a, input_grad_b]
 
     key_at, value_at = query_width, query_width + key_width
     merge_at, gain_at = qkv_width, qkv_width + query_width
     feed_pieces = [
-        (part, (2 * at + kind) * tile, tile, kind, starts[part] + at * tile)
+        (part, 2 * width + at * tile if kind == 2 else (2 * at + kind) * tile, tile, kind,
+         starts[part] + at * tile)
         for part, width in enumerate(chunks)
         for at in range(width // tile)
-        for kind in range(2)
-    ] + [(len(chunks) - 1, 2 * chunks[1] if many else 0, feed_width, 2, 0)]
+        for kind in range(3)
+    ]
     attention_pieces = [
         (0, 0, query_width, 0, 0),
         (0, key_at, own_key_width, 1, 0),
@@ -856,7 +936,7 @@
 
     gate_total, up_total, down_total = chain.run(
         lambda *received: results(received, feed_pieces, [feed_width] * 3),
-        *([moved_first, moved_last] if many else [moved_last]),
+        *moved_feed,
     )
     moved = chain.own_rows(attention_sums)
     chain.wait(*moved[1:])

time: 947 us -> 872 us (0.921)
  Pallas kernels: 245 us -> 338 us
  matrix products: 122 us -> 30.2 us
  waiting for transfers between devices: 244 us -> 192 us
  other arithmetic: 96.5 us -> 77.6 us
    pallas_call x4 -> x10, Pallas kernels: 81.8 us -> 175 us  [the longest x8 101 us: spread_rows(): pl.pallas_call(functools.partial(spread_kernel, count=len(lefts)), grid=(...]
    dot_general x13 -> x6, matrix products: 122 us -> 30.2 us  [dot(): lax.dot_general(left, right, dims, preferred_element_type=F32).astype(out)]
    reduce_scatter x3, waiting for transfers between devices: 42.3 us -> 5.79 us  [sum_over_dp(): return lax.psum_scatter(grads, 'dp', scatter_dimension=0, tiled=True)]
    concatenate x17 -> x0, other arithmetic: 24.3 us -> none  [the longest x1 10.8 us: last_grads(): return jnp.concatenate([token_grads(feed_in, grads), down], axis=1)]
    ppermute x85, waiting for transfers between devices: 202 us -> 178 us  [send(): lax.ppermute(block, 'ctx', [(i, i ^ bits) for i in range(4)])]
    slice x17 -> x1, local copies, waits for them, and re-layouts: 12.9 us -> 2.09 us  [body(): projections[:, :qkv_width]]
    convert_element_type x12 -> x16, other arithmetic: 14.4 us -> 25.2 us  [the longest x8 15.3 us: add(): return (for_one.astype(BF16), for_two.astype(BF16))]
  transfers between devices with their start and end apart: 92 -> 92, of which waited for: 37 -> 42; matrix products, arithmetic and copies ran while one was open for 28% -> 23% of each run, Pallas kernels for 22% -> 39%
where the time goes in v3:
time: 872 us; the launch traced here: 862 us
  Pallas kernels  338 us (39%)
  waiting for transfers between devices  192 us (22%)
  local copies, waits for them, and re-layouts  115 us (13%)
  starting transfers between devices  92.3 us (11%)
  other arithmetic  77.6 us (9%)
  matrix products  30.2 us (3%)
  between operations  16.6 us (2%)
    ppermute x85, waiting for transfers between devices, send(): lax.ppermute(block, 'ctx', [(i, i ^ bits) for i in range(4)])  178 us
    pallas_call x8, Pallas kernels, spread_rows(): pl.pallas_call(functools.partial(spread_kernel, count=len(lefts)), grid=(...  101 us
    ppermute x85, starting transfers between devices, send(): lax.ppermute(block, 'ctx', [(i, i ^ bits) for i in range(4)])  91.4 us
    pallas_call x4, Pallas kernels, feed_middle(): pl.pallas_call(feed_kernel, grid=(tiles,), in_specs=[pl.BlockSpec((rows,...  84 us
    pallas_call x2, Pallas kernels, feed_grads(): pl.pallas_call(functools.partial(token_kernel, seqs=seqs, pair_tiles=pair...  73.4 us
    unnamed x272, local copies, waits for them, and re-layouts  65.9 us
    pallas_call x2, Pallas kernels, attention_backward(): pl.pallas_call(functools.partial(attention_backward_kernel, span=length /...  42.6 us
    pallas_call x2, Pallas kernels, attention_forward(): pl.pallas_call(functools.partial(attention_forward_kernel, span=length //...  31.9 us
  transfers between devices with their start and end apart: 92, of which 42 were waited for; matrix products, arithmetic and copies ran while one was open for 23% of the time, Pallas kernels for 39%

profile of v3, /device:TPU:0, one launch (start us, length us, event | category | flops | bytes accessed | tf_op | source)
XLA Modules:
  0.0 862.0 jit_solution(16773177447282141884)
XLA Ops:
  37.4 13.8 %collective-permute-done.5 = bf16[64,512]{1,0:T(8,128)(2,1)S(1)} collective-permute-done((bf16[64,512]{1,0:T(8,128)(2,1)S(1)}, bf16[64,512]{1,0:T(8,128)(2,1)S(1)}, u32[]{:S(2)}, u32[]{:S(2)}) %collective-permute-start.5) | collective-permute-done | bytes 65568 | tf_op jit(solution)/shard_map/ppermute | solution.py:51
  83.8 9.8 %collective-permute-done.12 = bf16[64,4608]{1,0:T(8,128)(2,1)} collective-permute-done((bf16[64,4608]{1,0:T(8,128)(2,1)}, bf16[64,4608]{1,0:T(8,128)(2,1)}, u32[]{:S(2)}, u32[]{:S(2)}) %collective-permute-start.12) | collective-permute-done | bytes 589856 | tf_op jit(solution)/shard_map/ppermute | solution.py:51
  106.1 16.0 %attention_forward.2 = (bf16[1024,512]{1,0:T(8,128)(2,1)S(1)}, bf16[1024,512]{1,0:T(8,128)(2,1)S(1)}, bf16[1024,128]{1,0:T(8,128)(2,1)S(1)}, bf16[1024,128]{1,0:T(8,128)(2,1)S(1)}, f32[4,4,512]{2,1,0:T(4,128)S(1)}) custom-call(s32[8]{0:T(128)S(1)} %get-tuple-element.616.slot_ref, f32[1024,768]{1,0:T(8,128)} %fusion.70.q_ref.k_ref.v_ref, ...), custom_call_target="tpu_custom_call" | custom-call | flops 8589934592 | bytes 8388608 | tf_op jit(solution)/shard_map/attention_forward/pallas_call | solution.py:330
  168.5 15.9 %attention_forward.3 = (bf16[1024,512]{1,0:T(8,128)(2,1)S(1)}, bf16[1024,512]{1,0:T(8,128)(2,1)S(1)}, bf16[1024,128]{1,0:T(8,128)(2,1)S(1)}, bf16[1024,128]{1,0:T(8,128)(2,1)S(1)}, f32[4,4,512]{2,1,0:T(4,128)S(1)}) custom-call(s32[8]{0:T(128)S(1)} %get-tuple-element.701.slot_ref, f32[1024,768]{1,0:T(8,128)} %fusion.71.q_ref.k_ref.v_ref, ...), custom_call_target="tpu_custom_call" | custom-call | flops 8589934592 | bytes 8388608 | tf_op jit(solution)/shard_map/attention_forward/pallas_call | solution.py:330
  209.0 15.2 %collective-permute-done.21 = bf16[256,2048]{1,0:T(8,128)(2,1)S(1)} collective-permute-done((bf16[256,2048]{1,0:T(8,128)(2,1)S(1)}, bf16[256,2048]{1,0:T(8,128)(2,1)S(1)}, u32[]{:S(2)}, u32[]{:S(2)}) %collective-permute-start.21) | collective-permute-done | bytes 1048608 | tf_op jit(solution)/shard_map/ppermute | solution.py:51
  227.3 9.3 %collective-permute-done.32 = bf16[128,2048]{1,0:T(8,128)(2,1)S(1)} collective-permute-done((bf16[128,2048]{1,0:T(8,128)(2,1)S(1)}, bf16[128,2048]{1,0:T(8,128)(2,1)S(1)}, u32[]{:S(2)}, u32[]{:S(2)}) %collective-permute-start.32) | collective-permute-done | bytes 524320 | tf_op jit(solution)/shard_map/ppermute | solution.py:51
  252.1 20.0 %collective-permute-done.27 = bf16[256,2048]{1,0:T(8,128)(2,1)S(1)} collective-permute-done((bf16[256,2048]{1,0:T(8,128)(2,1)}, bf16[256,2048]{1,0:T(8,128)(2,1)S(1)}, u32[]{:S(2)}, u32[]{:S(2)}) %collective-permute-start.27) | collective-permute-done | bytes 1048608 | tf_op jit(solution)/shard_map/ppermute | solution.py:51
  277.1 7.6 collective-permute-done.25
  291.6 28.4 %feed_middle.4 = (bf16[1024,1536]{1,0:T(8,128)(2,1)}, bf16[1024,3072]{1,0:T(8,128)(2,1)}) custom-call(bf16[1024,2048]{1,0:T(8,128)(2,1)} %constant_dynamic-update-slice_fusion.33.feed_ref.refs_0_, bf16[1024,2048]{1,0:T(8,128)(2,1)} %copy-done.86, bf16[2048,4608]{1,0:T(8,128)(2,1)} %all-gather.9.cloned.1.call-done.pair_ref.down_ref.refs_2_, ...), custom_call_target="tpu_custom_call" | custom-call | flops 19327352832 | bytes 36700160 | tf_op jit(solution)/shard_map/feed_middle/pallas_call | solution.py:443
  337.7 13.6 %feed_middle.5 = (bf16[1024,512]{1,0:T(8,128)(2,1)}, bf16[1024,1024]{1,0:T(8,128)(2,1)}) custom-call(bf16[1024,2048]{1,0:T(8,128)(2,1)} %constant_dynamic-update-slice_fusion.33.feed_ref.refs_0_, bf16[1024,2048]{1,0:T(8,128)(2,1)} %copy-done.86, bf16[2048,1536]{1,0:T(8,128)(2,1)} %all-gather.11.cloned.1.call-done.pair_ref.down_ref.refs_3_, ...), custom_call_target="tpu_custom_call" | custom-call | flops 6442450944 | bytes 17825792 | tf_op jit(solution)/shard_map/feed_middle/pallas_call | solution.py:443
  356.2 23.7 %spread_rows.10 = (bf16[512,2048]{1,0:T(8,128)(2,1)}, bf16[256,2048]{1,0:T(8,128)(2,1)}, bf16[256,2048]{1,0:T(8,128)(2,1)}) custom-call(bf16[1024,3072]{1,0:T(8,128)(2,1)} %get-tuple-element.585.refs_0_.refs_4_, bf16[1024,1024]{1,0:T(8,128)(2,1)} %get-tuple-element.666.refs_1_.refs_4_, ...), custom_call_target="tpu_custom_call" | custom-call | flops 17179869184 | bytes 29360128 | tf_op jit(solution)/shard_map/spread_rows/pallas_call | solution.py:491
  400.9 28.3 %feed_middle.6 = (bf16[1024,1536]{1,0:T(8,128)(2,1)}, bf16[1024,3072]{1,0:T(8,128)(2,1)}) custom-call(bf16[1024,2048]{1,0:T(8,128)(2,1)} %constant_dynamic-update-slice_fusion.39.feed_ref.refs_1_, bf16[1024,2048]{1,0:T(8,128)(2,1)} %copy-done.87, bf16[2048,4608]{1,0:T(8,128)(2,1)} %all-gather.9.cloned.1.call-done.pair_ref.down_ref.refs_2_, ...), custom_call_target="tpu_custom_call" | custom-call | flops 19327352832 | bytes 36700160 | tf_op jit(solution)/shard_map/feed_middle/pallas_call | solution.py:443
  431.9 50.0 %feed_grads.2 = bf16[2048,4608]{1,0:T(8,128)(2,1)} custom-call(bf16[1024,2048]{1,0:T(8,128)(2,1)} %constant_dynamic-update-slice_fusion.33.feed_ref.refs_0_, bf16[1024,2048]{1,0:T(8,128)(2,1)} %constant_dynamic-update-slice_fusion.39.feed_ref.refs_1_, bf16[1024,2048]{1,0:T(8,128)(2,1)} %copy-done.86, bf16[1024,2048]{1,0:T(8,128)(2,1)} %copy-done.87, ...), custom_call_target="tpu_custom_call" | custom-call | flops 38654705664 | bytes 54525952 | tf_op jit(solution)/shard_map/feed_grads/pallas_call | solution.py:539
  492.5 13.7 %feed_middle.7 = (bf16[1024,512]{1,0:T(8,128)(2,1)}, bf16[1024,1024]{1,0:T(8,128)(2,1)}) custom-call(bf16[1024,2048]{1,0:T(8,128)(2,1)} %constant_dynamic-update-slice_fusion.39.feed_ref.refs_1_, bf16[1024,2048]{1,0:T(8,128)(2,1)} %copy-done.87, bf16[2048,1536]{1,0:T(8,128)(2,1)} %all-gather.11.cloned.1.call-done.pair_ref.down_ref.refs_3_, ...), custom_call_target="tpu_custom_call" | custom-call | flops 6442450944 | bytes 17825792 | tf_op jit(solution)/shard_map/feed_middle/pallas_call | solution.py:443
  516.8 24.0 %spread_rows.11 = (bf16[512,2048]{1,0:T(8,128)(2,1)}, bf16[256,2048]{1,0:T(8,128)(2,1)}, bf16[256,2048]{1,0:T(8,128)(2,1)}) custom-call(bf16[1024,3072]{1,0:T(8,128)(2,1)} %get-tuple-element.609.refs_5_.refs_0_, bf16[1024,1024]{1,0:T(8,128)(2,1)} %get-tuple-element.667.refs_1_.refs_5_, ...), custom_call_target="tpu_custom_call" | custom-call | flops 17179869184 | bytes 29360128 | tf_op jit(solution)/shard_map/spread_rows/pallas_call | solution.py:491
  547.7 21.2 %attention_backward.2 = (bf16[1024,512]{1,0:T(8,128)(2,1)S(1)}, bf16[1024,128]{1,0:T(8,128)(2,1)S(1)}, bf16[1024,128]{1,0:T(8,128)(2,1)S(1)}) custom-call(s32[8]{0:T(128)S(1)} %copy-done.1, bf16[1024,512]{1,0:T(8,128)(2,1)S(1)} %get-tuple-element.617.queries_ref, bf16[1024,128]{1,0:T(8,128)(2,1)S(1)} %copy-done.9, bf16[1024,128]{1,0:T(8,128)(2,1)S(1)} %copy-done.11, ...), custom_call_target="tpu_custom_call" | custom-call | flops 21474836480 | bytes 8388608 | tf_op jit(solution)/shard_map/attention_backward/pallas_call | solution.py:384
  583.0 13.6 %spread_rows.13 = (bf16[512,2048]{1,0:T(8,128)(2,1)}, bf16[256,2048]{1,0:T(8,128)(2,1)}, bf16[256,2048]{1,0:T(8,128)(2,1)}) custom-call(bf16[1024,1536]{1,0:T(8,128)(2,1)} %get-tuple-element.640.refs_6_.refs_0_, bf16[1024,512]{1,0:T(8,128)(2,1)} %get-tuple-element.668.refs_1_.refs_6_, ...), custom_call_target="tpu_custom_call" | custom-call | flops 8589934592 | bytes 16777216 | tf_op jit(solution)/shard_map/spread_rows/pallas_call | solution.py:491
  612.5 23.4 %feed_grads.3 = bf16[2048,1536]{1,0:T(8,128)(2,1)} custom-call(bf16[1024,2048]{1,0:T(8,128)(2,1)} %constant_dynamic-update-slice_fusion.33.feed_ref.refs_0_, bf16[1024,2048]{1,0:T(8,128)(2,1)} %constant_dynamic-update-slice_fusion.39.feed_ref.refs_1_, bf16[1024,2048]{1,0:T(8,128)(2,1)} %copy-done.86, bf16[1024,2048]{1,0:T(8,128)(2,1)} %copy-done.87, ...), custom_call_target="tpu_custom_call" | custom-call | flops 12884901888 | bytes 29360128 | tf_op jit(solution)/shard_map/feed_grads/pallas_call | solution.py:539
  649.7 13.2 %spread_rows.14 = (bf16[512,2048]{1,0:T(8,128)(2,1)}, bf16[256,2048]{1,0:T(8,128)(2,1)}, bf16[256,2048]{1,0:T(8,128)(2,1)}) custom-call(bf16[1024,1536]{1,0:T(8,128)(2,1)} %get-tuple-element.684.refs_7_.refs_0_, bf16[1024,512]{1,0:T(8,128)(2,1)} %get-tuple-element.685.refs_7_.refs_1_, ...), custom_call_target="tpu_custom_call" | custom-call | flops 8589934592 | bytes 16777216 | tf_op jit(solution)/shard_map/spread_rows/pallas_call | solution.py:491
  692.1 21.4 %attention_backward.3 = (bf16[1024,512]{1,0:T(8,128)(2,1)S(1)}, bf16[1024,128]{1,0:T(8,128)(2,1)S(1)}, bf16[1024,128]{1,0:T(8,128)(2,1)S(1)}) custom-call(s32[8]{0:T(128)S(1)} %get-tuple-element.701.slot_ref, bf16[1024,512]{1,0:T(8,128)(2,1)S(1)} %get-tuple-element.702.queries_ref, bf16[1024,128]{1,0:T(8,128)(2,1)S(1)} %get-tuple-element.703.keys_ref, ...), custom_call_target="tpu_custom_call" | custom-call | flops 21474836480 | bytes 8388608 | tf_op jit(solution)/shard_map/attention_backward/pallas_call | solution.py:384
  714.8 7.4 spread_rows.15
  738.6 10.6 %fusion.20 = bf16[2048,768]{1,0:T(8,128)(2,1)S(1)} fusion(bf16[1024,2048]{1,0:T(8,128)(2,1)} %copy-done.36, bf16[1024,2048]{1,0:T(8,128)(2,1)} %copy-done.35, bf16[1024,768]{1,0:T(8,128)(2,1)} %copy-done.79, bf16[1024,768]{1,0:T(8,128)(2,1)} %copy-done.78), kind=kOutput, calls=%fused_computation.33 | convolution fusion | flops 6467092480 | bytes 14680064 | tf_op jit(solution)/shard_map/dot_general | solution.py:25
  763.0 19.0 %collective-permute-done.72 = bf16[256,2048]{1,0:T(8,128)(2,1)} collective-permute-done((bf16[256,2048]{1,0:T(8,128)(2,1)}, bf16[256,2048]{1,0:T(8,128)(2,1)}, u32[]{:S(2)}, u32[]{:S(2)}) %collective-permute-start.72) | collective-permute-done | bytes 1048608 | tf_op jit(solution)/shard_map/ppermute | solution.py:51
  797.9 9.8 %collective-permute-done.74 = bf16[128,2048]{1,0:T(8,128)(2,1)S(1)} collective-permute-done((bf16[128,2048]{1,0:T(8,128)(2,1)S(1)}, bf16[128,2048]{1,0:T(8,128)(2,1)S(1)}, u32[]{:S(2)}, u32[]{:S(2)}) %collective-permute-start.74) | collective-permute-done | bytes 524320 | tf_op jit(solution)/shard_map/ppermute | solution.py:51
  (614 shorter events, 416.4 us)
Async XLA Ops:
  7.2 58.4 %all-gather.5.cloned.1.call-start = ((), (), s32[]{:S(2)}) async-start(), calls=%async_computation.3 | async-start | bytes 4128768 | tf_op jit(solution)/shard_map/all_gather | solution.py:107
  21.7 112.7 %all-gather.7.cloned.1.call-start = ((), (), s32[]{:S(2)}) async-start(), calls=%async_computation.4 | async-start | bytes 2359296 | tf_op jit(solution)/shard_map/all_gather | solution.py:107
  52.5 239.2 %all-gather.9.cloned.1.call-start = ((), (), s32[]{:S(2)}) async-start(), calls=%async_computation.5 | async-start | bytes 21233664 | tf_op jit(solution)/shard_map/all_gather | solution.py:107
  98.6 233.9 %all-gather.11.cloned.1.call-start = ((), (), s32[]{:S(2)}) async-start(), calls=%async_computation.6 | async-start | bytes 7077888 | tf_op jit(solution)/shard_map/all_gather | solution.py:107
  166.8 36.7 %collective-permute-start.24 = (bf16[256,2048]{1,0:T(8,128)(2,1)S(1)}, bf16[256,2048]{1,0:T(8,128)(2,1)}, u32[]{:S(2)}, u32[]{:S(2)}) collective-permute-start(bf16[256,2048]{1,0:T(8,128)(2,1)S(1)} %copy-done.27), channel_id=1, source_target_pairs={{0,2},{1,3},{2,0},{3,1},{4,6},{5,7},{6,4},{7,5},{8,10},{9,11},{10,... | collective-permute-start | bytes 3145736 | tf_op jit(solution)/shard_map/ppermute | solution.py:51
  188.1 36.1 %collective-permute-start.21 = (bf16[256,2048]{1,0:T(8,128)(2,1)S(1)}, bf16[256,2048]{1,0:T(8,128)(2,1)S(1)}, u32[]{:S(2)}, u32[]{:S(2)}) collective-permute-start(bf16[256,2048]{1,0:T(8,128)(2,1)S(1)} %multiply_convert_fusion.1), channel_id=1, source_target_pairs={{0,1},{1,0},{2,3},{3,2},{4,5},{5,4},{6,7},{7,6},{8,9},{9,8},{10,11... | collective-permute-start | bytes 3145736 | tf_op jit(solution)/shard_map/ppermute | solution.py:51
  189.8 36.0 %collective-permute-start.22 = (bf16[256,2048]{1,0:T(8,128)(2,1)S(1)}, bf16[256,2048]{1,0:T(8,128)(2,1)S(1)}, u32[]{:S(2)}, u32[]{:S(2)}) collective-permute-start(bf16[256,2048]{1,0:T(8,128)(2,1)S(1)} %multiply_convert_fusion.1), channel_id=1, source_target_pairs={{0,2},{1,3},{2,0},{3,1},{4,6},{5,7},{6,4},{7,5},{8,10},{9,11},{10,... | collective-permute-start | bytes 3145736 | tf_op jit(solution)/shard_map/ppermute | solution.py:51
  245.7 423.0 %reduce-scatter.4.cloned.1.call-start = ((), (), s32[]{:S(2)}) async-start(), calls=%async_computation.7 | async-start | bytes 21233664 | tf_op jit(solution)/shard_map/reduce_scatter | solution.py:145
  276.5 43.6 %collective-permute-start.34 = (bf16[128,2048]{1,0:T(8,128)(2,1)}, bf16[128,2048]{1,0:T(8,128)(2,1)}, u32[]{:S(2)}, u32[]{:S(2)}) collective-permute-start(bf16[128,2048]{1,0:T(8,128)(2,1)} %get-tuple-element.525), channel_id=1, source_target_pairs={{0,1},{1,0},{2,3},{3,2},{4,5},{5,4},{6,7},{7,6},{8,9},{9,8},{10,11... | collective-permute-start | bytes 1572872 | tf_op jit(solution)/shard_map/ppermute | solution.py:51
  277.1 42.9 %collective-permute-start.35 = (bf16[128,2048]{1,0:T(8,128)(2,1)}, bf16[128,2048]{1,0:T(8,128)(2,1)}, u32[]{:S(2)}, u32[]{:S(2)}) collective-permute-start(bf16[128,2048]{1,0:T(8,128)(2,1)} %get-tuple-element.526), channel_id=1, source_target_pairs={{0,2},{1,3},{2,0},{3,1},{4,6},{5,7},{6,4},{7,5},{8,10},{9,11},{10,... | collective-permute-start | bytes 1572872 | tf_op jit(solution)/shard_map/ppermute | solution.py:51
  284.7 44.6 %collective-permute-start.36 = (bf16[256,2048]{1,0:T(8,128)(2,1)}, bf16[256,2048]{1,0:T(8,128)(2,1)}, u32[]{:S(2)}, u32[]{:S(2)}) collective-permute-start(bf16[256,2048]{1,0:T(8,128)(2,1)} %get-tuple-element.651), channel_id=1, source_target_pairs={{0,1},{1,0},{2,3},{3,2},{4,5},{5,4},{6,7},{7,6},{8,9},{9,8},{10,11... | collective-permute-start | bytes 3145736 | tf_op jit(solution)/shard_map/ppermute | solution.py:51
  285.4 43.9 %collective-permute-start.37 = (bf16[256,2048]{1,0:T(8,128)(2,1)}, bf16[256,2048]{1,0:T(8,128)(2,1)}, u32[]{:S(2)}, u32[]{:S(2)}) collective-permute-start(bf16[256,2048]{1,0:T(8,128)(2,1)} %get-tuple-element.651), channel_id=1, source_target_pairs={{0,2},{1,3},{2,0},{3,1},{4,6},{5,7},{6,4},{7,5},{8,10},{9,11},{10,... | collective-permute-start | bytes 3145736 | tf_op jit(solution)/shard_map/ppermute | solution.py:51
  334.7 46.7 %collective-permute-start.44 = (bf16[128,2048]{1,0:T(8,128)(2,1)S(1)}, bf16[128,2048]{1,0:T(8,128)(2,1)S(1)}, u32[]{:S(2)}, u32[]{:S(2)}) collective-permute-start(bf16[128,2048]{1,0:T(8,128)(2,1)S(1)} %slice.467), channel_id=1, source_target_pairs={{0,2},{1,3},{2,0},{3,1},{4,6},{5,7},{6,4},{7,5},{8,10},{9,11},{10,... | collective-permute-start | bytes 1572872 | tf_op jit(solution)/shard_map/ppermute | solution.py:51
  336.2 46.6 %collective-permute-start.45 = (bf16[128,2048]{1,0:T(8,128)(2,1)S(1)}, bf16[128,2048]{1,0:T(8,128)(2,1)S(1)}, u32[]{:S(2)}, u32[]{:S(2)}) collective-permute-start(bf16[128,2048]{1,0:T(8,128)(2,1)S(1)} %slice.468), channel_id=1, source_target_pairs={{0,1},{1,0},{2,3},{3,2},{4,5},{5,4},{6,7},{7,6},{8,9},{9,8},{10,11... | collective-permute-start | bytes 1572872 | tf_op jit(solution)/shard_map/ppermute | solution.py:51
  379.9 49.2 %collective-permute-start.40 = (bf16[256,2048]{1,0:T(8,128)(2,1)}, bf16[256,2048]{1,0:T(8,128)(2,1)S(1)}, u32[]{:S(2)}, u32[]{:S(2)}) collective-permute-start(bf16[256,2048]{1,0:T(8,128)(2,1)} %get-tuple-element.551), channel_id=1, source_target_pairs={{0,1},{1,0},{2,3},{3,2},{4,5},{5,4},{6,7},{7,6},{8,9},{9,8},{10,11... | collective-permute-start | bytes 3145736 | tf_op jit(solution)/shard_map/ppermute | solution.py:51
  381.4 47.8 %collective-permute-start.41 = (bf16[256,2048]{1,0:T(8,128)(2,1)}, bf16[256,2048]{1,0:T(8,128)(2,1)S(1)}, u32[]{:S(2)}, u32[]{:S(2)}) collective-permute-start(bf16[256,2048]{1,0:T(8,128)(2,1)} %get-tuple-element.552), channel_id=1, source_target_pairs={{0,2},{1,3},{2,0},{3,1},{4,6},{5,7},{6,4},{7,5},{8,10},{9,11},{10,... | collective-permute-start | bytes 3145736 | tf_op jit(solution)/shard_map/ppermute | solution.py:51
  430.8 51.1 %collective-permute-start.46 = (bf16[128,2048]{1,0:T(8,128)(2,1)}, bf16[128,2048]{1,0:T(8,128)(2,1)}, u32[]{:S(2)}, u32[]{:S(2)}) collective-permute-start(bf16[128,2048]{1,0:T(8,128)(2,1)} %get-tuple-element.579), channel_id=1, source_target_pairs={{0,1},{1,0},{2,3},{3,2},{4,5},{5,4},{6,7},{7,6},{8,9},{9,8},{10,11... | collective-permute-start | bytes 1572872 | tf_op jit(solution)/shard_map/ppermute | solution.py:51
  431.4 50.6 %collective-permute-start.47 = (bf16[128,2048]{1,0:T(8,128)(2,1)}, bf16[128,2048]{1,0:T(8,128)(2,1)}, u32[]{:S(2)}, u32[]{:S(2)}) collective-permute-start(bf16[128,2048]{1,0:T(8,128)(2,1)} %get-tuple-element.580), channel_id=1, source_target_pairs={{0,2},{1,3},{2,0},{3,1},{4,6},{5,7},{6,4},{7,5},{8,10},{9,11},{10,... | collective-permute-start | bytes 1572872 | tf_op jit(solution)/shard_map/ppermute | solution.py:51
  482.0 275.1 %reduce-scatter.6.cloned.1.call-start = ((), (), s32[]{:S(2)}) async-start(), calls=%async_computation.8 | async-start | bytes 7077888 | tf_op jit(solution)/shard_map/reduce_scatter | solution.py:145
  668.8 173.3 %reduce-scatter.8.cloned.1.call-start = ((), (), s32[]{:S(2)}) async-start(), calls=%async_computation.9 | async-start | bytes 6488064 | tf_op jit(solution)/shard_map/reduce_scatter | solution.py:145
  677.7 44.5 %collective-permute-start.66 = (bf16[128,2048]{1,0:T(8,128)(2,1)}, bf16[128,2048]{1,0:T(8,128)(2,1)S(1)}, u32[]{:S(2)}, u32[]{:S(2)}) collective-permute-start(bf16[128,2048]{1,0:T(8,128)(2,1)} %get-tuple-element.699), channel_id=1, source_target_pairs={{0,1},{1,0},{2,3},{3,2},{4,5},{5,4},{6,7},{7,6},{8,9},{9,8},{10,11... | collective-permute-start | bytes 1572872 | tf_op jit(solution)/shard_map/ppermute | solution.py:51
  678.9 43.3 %collective-permute-start.67 = (bf16[128,2048]{1,0:T(8,128)(2,1)}, bf16[128,2048]{1,0:T(8,128)(2,1)S(1)}, u32[]{:S(2)}, u32[]{:S(2)}) collective-permute-start(bf16[128,2048]{1,0:T(8,128)(2,1)} %get-tuple-element.700), channel_id=1, source_target_pairs={{0,2},{1,3},{2,0},{3,1},{4,6},{5,7},{6,4},{7,5},{8,10},{9,11},{10,... | collective-permute-start | bytes 1572872 | tf_op jit(solution)/shard_map/ppermute | solution.py:51
  679.2 45.2 %collective-permute-start.68 = (bf16[256,2048]{1,0:T(8,128)(2,1)}, bf16[256,2048]{1,0:T(8,128)(2,1)S(1)}, u32[]{:S(2)}, u32[]{:S(2)}) collective-permute-start(bf16[256,2048]{1,0:T(8,128)(2,1)} %get-tuple-element.726), channel_id=1, source_target_pairs={{0,1},{1,0},{2,3},{3,2},{4,5},{5,4},{6,7},{7,6},{8,9},{9,8},{10,11... | collective-permute-start | bytes 3145736 | tf_op jit(solution)/shard_map/ppermute | solution.py:51
  679.8 44.7 %collective-permute-start.69 = (bf16[256,2048]{1,0:T(8,128)(2,1)}, bf16[256,2048]{1,0:T(8,128)(2,1)S(1)}, u32[]{:S(2)}, u32[]{:S(2)}) collective-permute-start(bf16[256,2048]{1,0:T(8,128)(2,1)} %get-tuple-element.727), channel_id=1, source_target_pairs={{0,2},{1,3},{2,0},{3,1},{4,6},{5,7},{6,4},{7,5},{8,10},{9,11},{10,... | collective-permute-start | bytes 3145736 | tf_op jit(solution)/shard_map/ppermute | solution.py:51
  (175 other events, 2842.1 us)
Sparse Core Ops, SparseCore 0:
  21.8 43.7 all-gather.4
  67.2 27.9 all-gather.6
  98.7 169.2 all-gather.8
  269.5 62.9 all-gather.10
  482.1 186.5 reduce-scatter.3
  670.9 68.1 reduce-scatter.5
  757.2 62.2 reduce-scatter.7

commit v4 on v3

--- a/solution.py
+++ b/solution.py
@@ -119,6 +119,22 @@
 
 
 HALVES = ((0, 0), (0, 1), (1, 1), (2, 0), (1, 0), (3, 0), (2, 1), (3, 1))
+
+
+def pieces_of(own, near, far):
+    rows = own.shape[0]
+    if not square():
+        whole = gathered(own, near, far)
+        return [whole], [(0, 0, whole.shape[0], 0)]
+    half = rows // 2
+    sources = [own, *near, *far]
+    plan = []
+    for at, (member, part) in enumerate(HALVES):
+        if member == 3:
+            plan.append((3 + part, 0, half, at * half))
+        else:
+            plan.append((member, part * half, half, at * half))
+    return sources, plan
 
 
 def gathered(own, near, far):
@@ -421,83 +437,193 @@
     )(slots, queries, keys, values, totals, grad, cos_lanes, sin_lanes)
 
 
-def feed_kernel(feed_ref, down_in_ref, pair_ref, down_ref, activated_ref, grads_ref):
+def put_together(sources, plan, target, whole_ref, sems):
+    copies = [
+        pltpu.make_async_copy(
+            sources[source].at[pl.ds(row, rows)], target.at[pl.ds(to, rows)], sems.at[at]
+        )
+        for at, (source, row, rows, to) in enumerate(plan)
+    ]
+    return copies, pltpu.make_async_copy(target, whole_ref, sems.at[len(plan)])
+
+
+def gather_in(calls):
+    for copies, _ in calls:
+        for copy in copies:
+            copy.start()
+    for copies, out in calls:
+        for copy in copies:
+            copy.wait()
+        out.start()
+
+
+def feed_tile(feed_ref, down_in_ref, pair_ref, down_ref, activated_ref, grads_ref):
     tile = down_ref.shape[1]
-    step = min(256, feed_ref.shape[0])
-    for start in range(0, feed_ref.shape[0], step):
-        here = slice(start, start + step)
-        both = dot(feed_ref[here, :], pair_ref[...])
-        grad_act = dot(down_in_ref[here, :], down_ref[...])
-        gate, up = both[:, :tile], both[:, tile:]
-        sig = jax.nn.sigmoid(gate)
-        silu = gate * sig
-        activated_ref[here, :] = (silu * up).astype(BF16)
-        grads_ref[here, :tile] = (grad_act * up * (sig + silu * (1.0 - sig))).astype(BF16)
-        grads_ref[here, tile:] = (grad_act * silu).astype(BF16)
-
-
-def feed_middle(feed_in, down_in, weights, width, tile):
-    rows, depth = feed_in.shape
+    both = dot(feed_ref[...], pair_ref[...])
+    grad_act = dot(down_in_ref[...], down_ref[...])
+    gate, up = both[:, :tile], both[:, tile:]
+    sig = jax.nn.sigmoid(gate)
+    silu = gate * sig
+    activated_ref[...] = (silu * up).astype(BF16)
+    grads_ref[:, :tile] = (grad_act * up * (sig + silu * (1.0 - sig))).astype(BF16)
+    grads_ref[:, tile:] = (grad_act * silu).astype(BF16)
+
+
+def feed_kernel(*refs, plan, count):
+    step = pl.program_id(0)
+    feeds, downs, refs = refs[:count], refs[count : 2 * count], refs[2 * count :]
+    pair_ref, down_ref, activated_ref, grads_ref, feed_out, down_out = refs[:6]
+    feed_all, down_all, feed_sems, down_sems = refs[6:]
+    calls = [
+        put_together(feeds, plan, feed_all, feed_out, feed_sems),
+        put_together(downs, plan, down_all, down_out, down_sems),
+    ]
+
+    @pl.when(step == 0)
+    def _():
+        gather_in(calls)
+
+    feed_tile(feed_all, down_all, pair_ref, down_ref, activated_ref, grads_ref)
+
+    @pl.when(step == pl.num_programs(0) - 1)
+    def _():
+        for _, out in calls:
+            out.wait()
+
+
+def feed_specs(rows, depth, width, tile):
     tiles = width // tile
+    weights = [
+        pl.BlockSpec((depth, 2 * tile), lambda j: (0, j)),
+        pl.BlockSpec((depth, tile), lambda j: (0, 2 * tiles + j)),
+    ]
+    outs = [
+        pl.BlockSpec((rows, tile), lambda j: (0, j)),
+        pl.BlockSpec((rows, 2 * tile), lambda j: (0, j)),
+    ]
+    shapes = [
+        jax.ShapeDtypeStruct((rows, width), BF16),
+        jax.ShapeDtypeStruct((rows, 2 * width), BF16),
+    ]
     work = rows * depth * width
-    return pl.pallas_call(
-        feed_kernel,
-        grid=(tiles,),
-        in_specs=[
-            pl.BlockSpec((rows, depth), lambda j: (0, 0), pipeline_mode=pl.Buffered(1)),
-            pl.BlockSpec((rows, depth), lambda j: (0, 0), pipeline_mode=pl.Buffered(1)),
-            pl.BlockSpec((depth, 2 * tile), lambda j: (0, j)),
-            pl.BlockSpec((depth, tile), lambda j: (0, 2 * tiles + j)),
-        ],
-        out_specs=[
-            pl.BlockSpec((rows, tile), lambda j: (0, j)),
-            pl.BlockSpec((rows, 2 * tile), lambda j: (0, j)),
-        ],
-        out_shape=[
-            jax.ShapeDtypeStruct((rows, width), BF16),
-            jax.ShapeDtypeStruct((rows, 2 * width), BF16),
-        ],
-        compiler_params=pltpu.CompilerParams(
+    settings = {
+        "compiler_params": pltpu.CompilerParams(
             dimension_semantics=("arbitrary",), vmem_limit_bytes=56 << 20
         ),
-        cost_estimate=pl.CostEstimate(
+        "cost_estimate": pl.CostEstimate(
             flops=6 * work,
             bytes_accessed=2 * (2 * rows * depth + 3 * depth * width + 3 * rows * width),
             transcendentals=rows * width,
         ),
+    }
+    return weights, outs, shapes, settings
+
+
+def feed_first(feed, down, weights, width, tile):
+    feeds, plan = pieces_of(*feed)
+    downs, _ = pieces_of(*down)
+    rows, depth = sum(entry[2] for entry in plan), weights.shape[0]
+    weight_specs, outs, shapes, settings = feed_specs(rows, depth, width, tile)
+    anywhere = pl.BlockSpec(memory_space=pl.ANY)
+    whole = jax.ShapeDtypeStruct((rows, depth), BF16)
+    return pl.pallas_call(
+        functools.partial(feed_kernel, plan=plan, count=len(feeds)),
+        grid=(width // tile,),
+        in_specs=[anywhere] * (2 * len(feeds)) + weight_specs,
+        out_specs=outs + [anywhere] * 2,
+        out_shape=shapes + [whole] * 2,
+        scratch_shapes=[
+            pltpu.VMEM((rows, depth), BF16),
+            pltpu.VMEM((rows, depth), BF16),
+            pltpu.SemaphoreType.DMA((len(plan) + 1,)),
+            pltpu.SemaphoreType.DMA((len(plan) + 1,)),
+        ],
+        name="feed_first",
+        **settings,
+    )(*feeds, *downs, weights, weights)
+
+
+def feed_middle(feed_in, down_in, weights, width, tile):
+    rows, depth = feed_in.shape
+    weight_specs, outs, shapes, settings = feed_specs(rows, depth, width, tile)
+    resident = pl.BlockSpec((rows, depth), lambda j: (0, 0), pipeline_mode=pl.Buffered(1))
+    return pl.pallas_call(
+        feed_tile,
+        grid=(width // tile,),
+        in_specs=[resident] * 2 + weight_specs,
+        out_specs=outs,
+        out_shape=shapes,
         name="feed_middle",
+        **settings,
     )(feed_in, down_in, weights, weights)
 
 
-def spread_kernel(*refs, count):
+def rows_kernel(*refs, plan, count):
+    sources, (weight_ref, out_ref, whole_ref, target, sems) = refs[:count], refs[count:]
+    call = put_together(sources, plan, target, whole_ref, sems)
+    gather_in([call])
+    out_ref[...] = dot(target[...], weight_ref[...]).astype(BF16)
+    call[1].wait()
+
+
+def rows_times(own, near, far, weight):
+    sources, plan = pieces_of(own, near, far)
+    rows, depth = sum(entry[2] for entry in plan), weight.shape[0]
+    anywhere = pl.BlockSpec(memory_space=pl.ANY)
+    return pl.pallas_call(
+        functools.partial(rows_kernel, plan=plan, count=len(sources)),
+        in_specs=[anywhere] * len(sources) + [pl.BlockSpec(memory_space=pltpu.VMEM)],
+        out_specs=[pl.BlockSpec(memory_space=pltpu.VMEM), anywhere],
+        out_shape=[
+            jax.ShapeDtypeStruct((rows, weight.shape[1]), BF16),
+            jax.ShapeDtypeStruct((rows, depth), BF16),
+        ],
+        scratch_shapes=[
+            pltpu.VMEM((rows, depth), BF16),
+            pltpu.SemaphoreType.DMA((len(plan) + 1,)),
+        ],
+        compiler_params=pltpu.CompilerParams(vmem_limit_bytes=48 << 20),
+        cost_estimate=pl.CostEstimate(
+            flops=2 * rows * depth * weight.shape[1],
+            bytes_accessed=2 * (2 * rows * depth + (rows + depth) * weight.shape[1]),
+            transcendentals=0,
+        ),
+        name="rows_times",
+    )(*sources, weight)
+
+
+def spread_kernel(*refs, count, begun):
     total = sum(dot(refs[i][...], refs[count + i][...], NT) for i in range(count))
-    total = total.astype(BF16)
+    if begun:
+        total = total + refs[2 * count][...]
     start = 0
-    for out in refs[2 * count :]:
-        out[...] = total[start : start + out.shape[0]]
+    for out in refs[2 * count + begun :]:
+        out[...] = total[start : start + out.shape[0]].astype(out.dtype)
         start += out.shape[0]
 
 
-def spread_rows(lefts, weights, places, tile):
+def spread_rows(lefts, weights, places, tile, begun=None, whole=False):
     rows = lefts[0].shape[0]
     depth = weights[0].shape[0]
     widths = [left.shape[1] for left in lefts]
     work = rows * depth * sum(widths)
-    outs = [rows // 2, rows // 4, rows // 4] if square() else [rows]
+    outs = [rows // 2, rows // 4, rows // 4] if square() and not whole else [rows]
+    begun = [] if begun is None else [begun]
 
     def weight_spec(width, place):
         return pl.BlockSpec((tile, width), lambda j: (j, place))
 
     return pl.pallas_call(
-        functools.partial(spread_kernel, count=len(lefts)),
+        functools.partial(spread_kernel, count=len(lefts), begun=len(begun)),
         grid=(depth // tile,),
         in_specs=[
             pl.BlockSpec((rows, width), lambda j: (0, 0), pipeline_mode=pl.Buffered(1))
             for width in widths
         ]
-        + [weight_spec(width, place) for width, place in zip(widths, places)],
+        + [weight_spec(width, place) for width, place in zip(widths, places)]
+        + [pl.BlockSpec((rows, tile), lambda j: (0, j)) for _ in begun],
         out_specs=[pl.BlockSpec((each, tile), lambda j: (0, j)) for each in outs],
-        out_shape=[jax.ShapeDtypeStruct((each, depth), BF16) for each in outs],
+        out_shape=[jax.ShapeDtypeStruct((each, depth), F32 if whole else BF16) for each in outs],
         compiler_params=pltpu.CompilerParams(
             dimension_semantics=("arbitrary",), vmem_limit_bytes=56 << 20
         ),
@@ -507,7 +633,7 @@
             transcendentals=0,
         ),
         name="spread_rows",
-    )(*lefts, *weights)
+    )(*lefts, *weights, *begun)
 
 
 def token_kernel(*refs, seqs, pair_tiles):
@@ -552,6 +678,51 @@
         ),
         name="feed_grads",
     )(*feeds, *downs, *pairs, *acts)
+
+
+def two_grads_kernel(*refs, seqs):
+    lefts, rights, others, more = (refs[at * seqs : (at + 1) * seqs] for at in range(4))
+    gains_ref, out_ref = refs[4 * seqs :]
+    width = rights[0].shape[1]
+    end = width + more[0].shape[1]
+    first = sum(dot(left[...], right[...], TN) for left, right in zip(lefts, rights))
+    out_ref[:, :width] = first.astype(BF16)
+    second = sum(dot(left[...], right[...], TN) for left, right in zip(others, more))
+    out_ref[:, width:end] = second.astype(BF16)
+    out_ref[:, end:] = gains_ref[...]
+
+
+def two_grads(lefts, rights, others, more, gains):
+    seqs = len(lefts)
+    rows, depth = lefts[0].shape
+    widths = [rights[0].shape[1], more[0].shape[1], gains.shape[1]]
+    step = min(512, depth)
+    work = seqs * rows * depth * (widths[0] + widths[1])
+
+    def resident(array):
+        return pl.BlockSpec(array.shape, lambda i: (0, 0), pipeline_mode=pl.Buffered(1))
+
+    left = pl.BlockSpec((rows, step), lambda i: (0, i))
+    return pl.pallas_call(
+        functools.partial(two_grads_kernel, seqs=seqs),
+        grid=(depth // step,),
+        in_specs=[left] * seqs
+        + [resident(array) for array in rights]
+        + [left] * seqs
+        + [resident(array) for array in more]
+        + [pl.BlockSpec((step, widths[2]), lambda i: (i, 0))],
+        out_specs=pl.BlockSpec((step, sum(widths)), lambda i: (i, 0)),
+        out_shape=jax.ShapeDtypeStruct((depth, sum(widths)), BF16),
+        compiler_params=pltpu.CompilerParams(
+            dimension_semantics=("arbitrary",), vmem_limit_bytes=56 << 20
+        ),
+        cost_estimate=pl.CostEstimate(
+            flops=2 * work,
+            bytes_accessed=2 * (2 * seqs * rows * depth + (seqs * rows + depth) * sum(widths)),
+            transcendentals=0,
+        ),
+        name="two_grads",
+    )(*lefts, *rights, *others, *more, gains)
 
 
 def lay_kernel(place_ref, *refs, plan, inputs):
@@ -694,17 +865,17 @@
         normed, _ = norm_forward(hidden)
         return hidden, (normed * gain).astype(BF16)
 
-    def middle_of(feed_in, down_in, weights, part):
-        return feed_middle(feed_in, down_in, weights, chunks[part], tile)
-
-    def feed_back(grads, weights):
-        return spread_rows(grads, weights, [0] * len(grads), tile)
-
-    def feed_out(activated, weights):
-        return spread_rows(activated, weights, [2] * len(activated), tile)
-
-    def token_grads(left, right):
-        return dot(jnp.concatenate(left, axis=0), jnp.concatenate(right, axis=0), TN, BF16)
+    def middle_first(feed, down, weights):
+        return feed_first(feed, down, weights, chunks[0], tile)
+
+    def middle_last(feed_in, down_in, weights):
+        return feed_middle(feed_in, down_in, weights, chunks[1], tile)
+
+    def feed_back(grads, weights, begun=None, whole=False):
+        return spread_rows(grads, weights, [0] * len(grads), tile, begun, whole)
+
+    def feed_out(activated, weights, begun=None, whole=False):
+        return spread_rows(activated, weights, [2] * len(activated), tile, begun, whole)
 
     def feed_grads_of(feed_in, down_in, middle, part):
         return feed_grads(
@@ -720,8 +891,7 @@
         return grad_hidden, grad_hidden.astype(BF16), gain_part
 
     def attend_back(own, near, far, weight, kept, slots):
-        merge_in = gathered(own, near, far)
-        grad_attn = dot(merge_in, weight, NN, BF16)
+        grad_attn, merge_in = rows_times(own, near, far, weight)
         parts = attention_backward(kept, grad_attn, slots, cos_lanes, sin_lanes, group_size)
         return merge_in, jnp.concatenate(parts, axis=1)
 
@@ -740,14 +910,8 @@
     def attention_grads_of(attn_in, grad_qkv, merge_in, attn_out, rows, lower, gain_two_parts):
         gain_one_sum = sum(gain_part_of(r, l) for r, l in zip(rows, lower))
         gains = jnp.stack([gain_one_sum, sum(gain_two_parts)], axis=1)
-        return jnp.concatenate(
-            [
-                token_grads(attn_in, grad_qkv),
-                token_grads(merge_in, attn_out),
-                pad_columns(gains.astype(BF16), LANES),
-            ],
-            axis=1,
-        )
+        gains = pad_columns(gains.astype(BF16), LANES)
+        return two_grads(attn_in, grad_qkv, merge_in, attn_out, gains)
 
     def project_norm_back(rows, parts, near, far, grad_hidden, gain):
         normed, inverse = norm_forward(rows.astype(F32))
@@ -790,36 +954,44 @@
     hidden_a, feed_a = chain.run(feed_norm, tokens[0], branch_a, near_a, far_a, gain_two)
     feed_a_near = chain.gather_near(feed_a)
     branch_b = chain.run(merge_back, attn_out_b, merge)
-    chain.wait(*cot_a_near)
+    cot_a_far = chain.gather_far(cot_a_near)
+    feed_a_far = chain.gather_far(feed_a_near)
     if many:
         moved = chain.exchange(feed_for(1))
-    cot_a_far = chain.gather_far(cot_a_near)
+    chain.wait(*cot_a_far)
+    chain.wait(*feed_a_far)
     near_b = chain.scatter_near(branch_b)
-    feed_a_far = chain.gather_far(feed_a_near)
-    chain.wait(*cot_a_far)
-    down_in_a = chain.run(gathered, out_grad[0], cot_a_near, cot_a_far)
     if many:
         feeds.append(chain.all_rows(moved))
+    cot_b_near = chain.gather_near(out_grad[1])
+    *first, feed_in_a, down_in_a = chain.run(
+        middle_first,
+        (feed_a, feed_a_near, feed_a_far), (out_grad[0], cot_a_near, cot_a_far), feeds[0],
+    )
+    middle_a = [first]
     far_b = chain.scatter_far(branch_b, near_b)
-    chain.wait(*feed_a_far)
-    cot_b_near = chain.gather_near(out_grad[1])
-    feed_in_a = chain.run(gathered, feed_a, feed_a_near, feed_a_far)
-    middle_a = [chain.run(lambda f, d, w: middle_of(f, d, w, 0), feed_in_a, down_in_a, feeds[0])]
+    cot_b_far = chain.gather_far(cot_b_near)
+    begun_back = None
+    if many:
+        (begun_back,) = chain.run(
+            lambda m, w: feed_back([m], [w], None, True), middle_a[0][1], feeds[0]
+        )
     chain.wait(*far_b)
     hidden_b, feed_b = chain.run(feed_norm, tokens[1], branch_b, near_b, far_b, gain_two)
     feed_b_near = chain.gather_near(feed_b)
-    cot_b_far = chain.gather_far(cot_b_near)
     if many:
-        middle_a.append(
-            chain.run(lambda f, d, w: middle_of(f, d, w, 1), feed_in_a, down_in_a, feeds[1])
-        )
+        middle_a.append(chain.run(middle_last, feed_in_a, down_in_a, feeds[1]))
     feed_b_far = chain.gather_far(feed_b_near)
-    back_a = chain.run(feed_back, [m[1] for m in middle_a], feeds)
+    ends_a = slice(1 if many else 0, None)
+    back_a = chain.run(feed_back, [m[1] for m in middle_a[ends_a]], feeds[ends_a], begun_back)
     near_a = chain.scatter_near(back_a)
-    chain.wait(*cot_b_far, *feed_b_far)
-    down_in_b = chain.run(gathered, out_grad[1], cot_b_near, cot_b_far)
-    feed_in_b = chain.run(gathered, feed_b, feed_b_near, feed_b_far)
-    middle_b = [chain.run(lambda f, d, w: middle_of(f, d, w, 0), feed_in_b, down_in_b, feeds[0])]
+    chain.wait(*cot_b_far)
+    chain.wait(*feed_b_far)
+    *first, feed_in_b, down_in_b = chain.run(
+        middle_first,
+        (feed_b, feed_b_near, feed_b_far), (out_grad[1], cot_b_near, cot_b_far), feeds[0],
+    )
+    middle_b = [first]
     far_a = chain.scatter_far(back_a, near_a)
     grads_first = chain.run(
         lambda f, d, m: feed_grads_of(f, d, m, 0),
@@ -832,9 +1004,7 @@
     )
     merge_a_near = chain.gather_near(merge_a)
     if many:
-        middle_b.append(
-            chain.run(lambda f, d, w: middle_of(f, d, w, 1), feed_in_b, down_in_b, feeds[1])
-        )
+        middle_b.append(chain.run(middle_last, feed_in_b, down_in_b, feeds[1]))
     merge_a_far = chain.gather_far(merge_a_near)
     back_b = chain.run(feed_back, [m[1] for m in middle_b], feeds)
     near_b = chain.scatter_near(back_b)
@@ -858,26 +1028,25 @@
             [feed_in_a, feed_in_b], [down_in_a, down_in_b], [middle_a[1], middle_b[1]],
         )
     merge_b_far = chain.gather_far(merge_b_near)
-    out_a_near = chain.scatter_near(out_a)
     chain.wait(*lower_a_far)
     input_grad_a = chain.run(
         project_norm_back, tokens[0], lower_a, lower_a_near, lower_a_far, grad_hidden_a, gain_one
     )
-    out_b = chain.run(feed_out, [m[0] for m in middle_b], feeds)
     chain.wait(*merge_b_far)
+    out_a_near = chain.scatter_near(out_a)
+    merge_in_b, grad_qkv_b = chain.run(
+        attend_back, merge_b, merge_b_near, merge_b_far, merge, kept_b, slots[1]
+    )
+    chain.wait(*out_a_near)
+    chain.wait(sums[0])
     if many:
-        chain.wait(sums[0])
         sums.append(sum_over_dp(*chain.run(only, grads_last)))
     out_a_far = chain.scatter_far(out_a, out_a_near)
-    out_b_near = chain.scatter_near(out_b)
-    merge_in_b, grad_qkv_b = chain.run(
-        attend_back, merge_b, merge_b_near, merge_b_far, merge, kept_b, slots[1]
-    )
     lower_b = chain.run(project_back, grad_qkv_b, projections)
     lower_b_near = chain.scatter_near(lower_b)
     chain.wait(*out_a_far)
     block_a = chain.run(block_of, hidden_a, out_a, out_a_near, out_a_far)
-    out_b_far = chain.scatter_far(out_b, out_b_near)
+    moved_feed = [chain.own_rows(sums[0])]
     attention_grads = chain.run(
         attention_grads_of,
         [attn_in_a, attn_in_b],
@@ -888,19 +1057,22 @@
         [lower_a, lower_b],
         [gain_two_a, gain_two_b],
     )
+    chain.wait(*lower_b_near)
+    chain.wait(*moved_feed[0][1:])
     chain.wait(sums[-1])
     attention_sums = sum_over_dp(*chain.run(only, attention_grads))
     lower_b_far = chain.scatter_far(lower_b, lower_b_near)
-    moved_feed = [chain.own_rows(sums[0])]
-    chain.wait(*out_b_far)
-    block_b = chain.run(block_of, hidden_b, out_b, out_b_near, out_b_far)
+    out_b = chain.run(feed_out, [m[0] for m in middle_b], feeds)
+    out_b_near = chain.scatter_near(out_b)
     chain.wait(*lower_b_far)
     input_grad_b = chain.run(
         project_norm_back, tokens[1], lower_b, lower_b_near, lower_b_far, grad_hidden_b, gain_one
     )
-    chain.wait(*moved_feed[0][1:])
     moved_feed += [chain.own_rows(part) for part in sums[1:]]
+    out_b_far = chain.scatter_far(out_b, out_b_near)
     chain.wait(*moved_feed[-1][1:])
+    chain.wait(*out_b_far)
+    block_b = chain.run(block_of, hidden_b, out_b, out_b_near, out_b_far)
     blocks = [block_a, block_b]
     input_grad = [input_grad_a, input_grad_b]
 

time: 872 us -> 830 us (0.952)
  Pallas kernels: 338 us -> 374 us
  local copies, waits for them, and re-layouts: 115 us -> 79.3 us
  matrix products: 30.2 us -> 10.1 us
  other arithmetic: 77.6 us -> 62.5 us
  waiting for transfers between devices: 192 us -> 182 us
    pallas_call x12 -> x16, Pallas kernels: 185 us -> 222 us  [the longest x9 107 us: spread_rows(): pl.pallas_call(functools.partial(spread_kernel, count=len(lefts), begun=l...]
    unnamed x272 -> x226, local copies, waits for them, and re-layouts: 65.9 us -> 38.6 us
    dot_general x6 -> x2, matrix products: 30.2 us -> 10.1 us  [dot(): lax.dot_general(left, right, dims, preferred_element_type=F32).astype(out)]
    ppermute x85, waiting for transfers between devices: 178 us -> 164 us  [send(): lax.ppermute(block, 'ctx', [(i, i ^ bits) for i in range(4)])]
  transfers between devices with their start and end apart: 92 -> 92, of which waited for: 42 -> 41; matrix products, arithmetic and copies ran while one was open for 23% -> 15% of each run, Pallas kernels for 39% -> 46%
where the time goes in v4:
time: 830 us; the launch traced here: 818 us
  Pallas kernels  374 us (45%)
  waiting for transfers between devices  182 us (22%)
  starting transfers between devices  93.4 us (11%)
  local copies, waits for them, and re-layouts  79.3 us (10%)
  other arithmetic  62.5 us (8%)
  between operations  16.4 us (2%)
  matrix products  10.1 us (1%)
    ppermute x85, waiting for transfers between devices, send(): lax.ppermute(block, 'ctx', [(i, i ^ bits) for i in range(4)])  164 us
    pallas_call x9, Pallas kernels, spread_rows(): pl.pallas_call(functools.partial(spread_kernel, count=len(lefts), begun=l...  107 us
    ppermute x85, starting transfers between devices, send(): lax.ppermute(block, 'ctx', [(i, i ^ bits) for i in range(4)])  92.9 us
    pallas_call x2, Pallas kernels, feed_grads(): pl.pallas_call(functools.partial(token_kernel, seqs=seqs, pair_tiles=pair...  73.3 us
    pallas_call x2, Pallas kernels, feed_first(): pl.pallas_call(functools.partial(feed_kernel, plan=plan, count=len(feeds)...  61.3 us
    pallas_call x2, Pallas kernels, attention_backward(): pl.pallas_call(functools.partial(attention_backward_kernel, span=length /...  42.4 us
    unnamed x226, local copies, waits for them, and re-layouts  38.6 us
    pallas_call x2, Pallas kernels, attention_forward(): pl.pallas_call(functools.partial(attention_forward_kernel, span=length //...  31.3 us
  transfers between devices with their start and end apart: 92, of which 41 were waited for; matrix products, arithmetic and copies ran while one was open for 15% of the time, Pallas kernels for 46%

profile of v4, /device:TPU:0, one launch (start us, length us, event | category | flops | bytes accessed | tf_op | source)
XLA Modules:
  0.0 817.6 jit_solution(13374764369891099178)
XLA Ops:
  38.5 12.6 %collective-permute-done.5 = bf16[64,512]{1,0:T(8,128)(2,1)S(1)} collective-permute-done((bf16[64,512]{1,0:T(8,128)(2,1)S(1)}, bf16[64,512]{1,0:T(8,128)(2,1)S(1)}, u32[]{:S(2)}, u32[]{:S(2)}) %collective-permute-start.5) | collective-permute-done | bytes 65568 | tf_op jit(solution)/shard_map/ppermute | solution.py:51
  83.7 9.8 %collective-permute-done.12 = bf16[64,4608]{1,0:T(8,128)(2,1)} collective-permute-done((bf16[64,4608]{1,0:T(8,128)(2,1)}, bf16[64,4608]{1,0:T(8,128)(2,1)}, u32[]{:S(2)}, u32[]{:S(2)}) %collective-permute-start.12) | collective-permute-done | bytes 589856 | tf_op jit(solution)/shard_map/ppermute | solution.py:51
  106.1 15.6 %attention_forward.2 = (bf16[1024,512]{1,0:T(8,128)(2,1)S(1)}, bf16[1024,512]{1,0:T(8,128)(2,1)S(1)}, bf16[1024,128]{1,0:T(8,128)(2,1)S(1)}, bf16[1024,128]{1,0:T(8,128)(2,1)S(1)}, f32[4,4,512]{2,1,0:T(4,128)S(1)}) custom-call(s32[8]{0:T(128)S(1)} %get-tuple-element.622.slot_ref, f32[1024,768]{1,0:T(8,128)} %fusion.46.q_ref.k_ref.v_ref, ...), custom_call_target="tpu_custom_call" | custom-call | flops 8589934592 | bytes 8388608 | tf_op jit(solution)/shard_map/attention_forward/pallas_call | solution.py:346
  168.5 15.7 %attention_forward.3 = (bf16[1024,512]{1,0:T(8,128)(2,1)S(1)}, bf16[1024,512]{1,0:T(8,128)(2,1)S(1)}, bf16[1024,128]{1,0:T(8,128)(2,1)S(1)}, bf16[1024,128]{1,0:T(8,128)(2,1)S(1)}, f32[4,4,512]{2,1,0:T(4,128)S(1)}) custom-call(s32[8]{0:T(128)S(1)} %get-tuple-element.703.slot_ref, f32[1024,768]{1,0:T(8,128)} %fusion.47.q_ref.k_ref.v_ref, ...), custom_call_target="tpu_custom_call" | custom-call | flops 8589934592 | bytes 8388608 | tf_op jit(solution)/shard_map/attention_forward/pallas_call | solution.py:346
  206.7 17.6 %collective-permute-done.21.refs_1_ = bf16[256,2048]{1,0:T(8,128)(2,1)S(1)} collective-permute-done((bf16[256,2048]{1,0:T(8,128)(2,1)S(1)}, bf16[256,2048]{1,0:T(8,128)(2,1)S(1)}, u32[]{:S(2)}, u32[]{:S(2)}) %collective-permute-start.21) | collective-permute-done | bytes 1048608 | tf_op jit(solution)/shard_map/ppermute | solution.py:51
  228.4 8.7 %collective-permute-done.27.refs_8_ = bf16[128,2048]{1,0:T(8,128)(2,1)S(1)} collective-permute-done((bf16[128,2048]{1,0:T(8,128)(2,1)S(1)}, bf16[128,2048]{1,0:T(8,128)(2,1)S(1)}, u32[]{:S(2)}, u32[]{:S(2)}) %collective-permute-start.27) | collective-permute-done | bytes 524320 | tf_op jit(solution)/shard_map/ppermute | solution.py:51
  239.1 10.6 %collective-permute-done.29 = bf16[64,1536]{1,0:T(8,128)(2,1)S(1)} collective-permute-done((bf16[64,1536]{1,0:T(8,128)(2,1)S(1)}, bf16[64,1536]{1,0:T(8,128)(2,1)S(1)}, u32[]{:S(2)}, u32[]{:S(2)}) %collective-permute-start.29) | collective-permute-done | bytes 196640 | tf_op jit(solution)/shard_map/ppermute | solution.py:51
  268.0 31.1 %feed_first.2 = (bf16[1024,1536]{1,0:T(8,128)(2,1)}, bf16[1024,3072]{1,0:T(8,128)(2,1)}, bf16[1024,2048]{1,0:T(8,128)(2,1)}, bf16[1024,2048]{1,0:T(8,128)(2,1)}) custom-call(bf16[256,2048]{1,0:T(8,128)(2,1)} %copy-done.60, bf16[256,2048]{1,0:T(8,128)(2,1)} %copy-done.80, bf16[256,2048]{1,0:T(8,128)(2,1)} %copy-done.81, bf16[128,2048]{1,0:T(8,128)(2,1)} %copy-done.101, ...), custom_call_target="tpu_custom_call" | custom-call | flops 19327352832 | bytes 36700160 | tf_op jit(solution)/shard_map/feed_first/pallas_call | solution.py:529
  305.2 19.2 %spread_rows.11.refs_2_ = f32[1024,2048]{1,0:T(8,128)} custom-call(bf16[1024,3072]{1,0:T(8,128)(2,1)} %get-tuple-element.591.refs_0_.refs_4_, bf16[2048,4608]{1,0:T(8,128)(2,1)} %all-gather.9.cloned.1.call-done.refs_10_.refs_11_.refs_1_.refs_2_), custom_call_target="tpu_custom_call" | custom-call | flops 12884901888 | bytes 23068672 | tf_op jit(solution)/shard_map/spread_rows/pallas_call | solution.py:616
  336.4 13.5 %feed_middle.2 = (bf16[1024,512]{1,0:T(8,128)(2,1)}, bf16[1024,1024]{1,0:T(8,128)(2,1)}) custom-call(bf16[1024,2048]{1,0:T(8,128)(2,1)} %get-tuple-element.672.feed_ref.refs_0_, bf16[1024,2048]{1,0:T(8,128)(2,1)} %get-tuple-element.674.down_in_ref.refs_2_, bf16[2048,1536]{1,0:T(8,128)(2,1)} %all-gather.11.cloned.1.call-done.pair_ref.down_ref.refs_1_.refs_3_, ...), custom_call_target="tpu_custom_call" | custom-call | flops 6442450944 | bytes 17825792 | tf_op jit(solution)/shard_map/feed_middle/pallas_call | solution.py:550
  361.2 10.0 %spread_rows.12 = (bf16[512,2048]{1,0:T(8,128)(2,1)}, bf16[256,2048]{1,0:T(8,128)(2,1)}, bf16[256,2048]{1,0:T(8,128)(2,1)}) custom-call(bf16[1024,1024]{1,0:T(8,128)(2,1)} %get-tuple-element.676.refs_0_.refs_4_, bf16[2048,1536]{1,0:T(8,128)(2,1)} %all-gather.11.cloned.1.call-done.pair_ref.down_ref.refs_1_.refs_3_, f32[1024,2048]{1,0:T(8,128)} %spread_rows.11.refs_2_), custom_call_target="tpu_custom_call" | custom-call | flops 4294967296 | bytes 10485760 | tf_op jit(solution)/shard_map/spread_rows/pallas_call | solution.py:616
  378.5 30.2 %feed_first.3 = (bf16[1024,1536]{1,0:T(8,128)(2,1)}, bf16[1024,3072]{1,0:T(8,128)(2,1)}, bf16[1024,2048]{1,0:T(8,128)(2,1)}, bf16[1024,2048]{1,0:T(8,128)(2,1)}) custom-call(bf16[256,2048]{1,0:T(8,128)(2,1)} %multiply_convert_fusion.refs_0_, bf16[256,2048]{1,0:T(8,128)(2,1)} %collective-permute-done.38.refs_1_, ...), custom_call_target="tpu_custom_call" | custom-call | flops 19327352832 | bytes 36700160 | tf_op jit(solution)/shard_map/feed_first/pallas_call | solution.py:529
  412.5 50.1 %feed_grads.2 = bf16[2048,4608]{1,0:T(8,128)(2,1)} custom-call(bf16[1024,2048]{1,0:T(8,128)(2,1)} %get-tuple-element.672.feed_ref.refs_0_, bf16[1024,2048]{1,0:T(8,128)(2,1)} %get-tuple-element.673.refs_1_.feed_ref, bf16[1024,2048]{1,0:T(8,128)(2,1)} %get-tuple-element.674.down_in_ref.refs_2_, bf16[1024,2048]{1,0:T(8,128)(2,1)} %get-tuple-element.675.refs_3_.down_in_ref, ...), custom_call_target="tpu_custom_call" | custom-call | flops 38654705664 | bytes 54525952 | tf_op jit(solution)/shard_map/feed_grads/pallas_call | solution.py:665
  472.1 13.5 %feed_middle.3 = (bf16[1024,512]{1,0:T(8,128)(2,1)}, bf16[1024,1024]{1,0:T(8,128)(2,1)}) custom-call(bf16[1024,2048]{1,0:T(8,128)(2,1)} %get-tuple-element.673.refs_1_.feed_ref, bf16[1024,2048]{1,0:T(8,128)(2,1)} %get-tuple-element.675.refs_3_.down_in_ref, bf16[2048,1536]{1,0:T(8,128)(2,1)} %all-gather.11.cloned.1.call-done.pair_ref.down_ref.refs_1_.refs_3_, ...), custom_call_target="tpu_custom_call" | custom-call | flops 6442450944 | bytes 17825792 | tf_op jit(solution)/shard_map/feed_middle/pallas_call | solution.py:550
  497.0 24.4 %spread_rows.13 = (bf16[512,2048]{1,0:T(8,128)(2,1)}, bf16[256,2048]{1,0:T(8,128)(2,1)}, bf16[256,2048]{1,0:T(8,128)(2,1)}) custom-call(bf16[1024,3072]{1,0:T(8,128)(2,1)} %get-tuple-element.615.refs_5_.refs_0_, bf16[1024,1024]{1,0:T(8,128)(2,1)} %get-tuple-element.677.refs_1_.refs_5_, ...), custom_call_target="tpu_custom_call" | custom-call | flops 17179869184 | bytes 29360128 | tf_op jit(solution)/shard_map/spread_rows/pallas_call | solution.py:616
  526.5 21.2 %attention_backward.2 = (bf16[1024,512]{1,0:T(8,128)(2,1)S(1)}, bf16[1024,128]{1,0:T(8,128)(2,1)S(1)}, bf16[1024,128]{1,0:T(8,128)(2,1)S(1)}) custom-call(s32[8]{0:T(128)S(1)} %copy-done.7, bf16[1024,512]{1,0:T(8,128)(2,1)S(1)} %get-tuple-element.623.queries_ref, bf16[1024,128]{1,0:T(8,128)(2,1)S(1)} %get-tuple-element.624.keys_ref, ...), custom_call_target="tpu_custom_call" | custom-call | flops 21474836480 | bytes 8388608 | tf_op jit(solution)/shard_map/attention_backward/pallas_call | solution.py:400
  562.3 13.4 %spread_rows.15 = (bf16[512,2048]{1,0:T(8,128)(2,1)}, bf16[256,2048]{1,0:T(8,128)(2,1)}, bf16[256,2048]{1,0:T(8,128)(2,1)}) custom-call(bf16[1024,1536]{1,0:T(8,128)(2,1)} %get-tuple-element.648.refs_6_.refs_0_, bf16[1024,512]{1,0:T(8,128)(2,1)} %get-tuple-element.678.refs_1_.refs_6_, ...), custom_call_target="tpu_custom_call" | custom-call | flops 8589934592 | bytes 16777216 | tf_op jit(solution)/shard_map/spread_rows/pallas_call | solution.py:616
  591.9 23.3 %feed_grads.3 = bf16[2048,1536]{1,0:T(8,128)(2,1)} custom-call(bf16[1024,2048]{1,0:T(8,128)(2,1)} %get-tuple-element.672.feed_ref.refs_0_, bf16[1024,2048]{1,0:T(8,128)(2,1)} %get-tuple-element.673.refs_1_.feed_ref, bf16[1024,2048]{1,0:T(8,128)(2,1)} %get-tuple-element.674.down_in_ref.refs_2_, bf16[1024,2048]{1,0:T(8,128)(2,1)} %get-tuple-element.675.refs_3_.down_in_ref, ...), custom_call_target="tpu_custom_call" | custom-call | flops 12884901888 | bytes 29360128 | tf_op jit(solution)/shard_map/feed_grads/pallas_call | solution.py:665
  638.9 21.2 %attention_backward.3 = (bf16[1024,512]{1,0:T(8,128)(2,1)S(1)}, bf16[1024,128]{1,0:T(8,128)(2,1)S(1)}, bf16[1024,128]{1,0:T(8,128)(2,1)S(1)}) custom-call(s32[8]{0:T(128)S(1)} %copy-done.5, bf16[1024,512]{1,0:T(8,128)(2,1)S(1)} %copy-done.11, bf16[1024,128]{1,0:T(8,128)(2,1)S(1)} %get-tuple-element.705.keys_ref, bf16[1024,128]{1,0:T(8,128)(2,1)S(1)} %copy-done.13, ...), custom_call_target="tpu_custom_call" | custom-call | flops 21474836480 | bytes 8388608 | tf_op jit(solution)/shard_map/attention_backward/pallas_call | solution.py:400
  678.0 9.1 %collective-permute-done.66 = bf16[128,2048]{1,0:T(8,128)(2,1)S(1)} collective-permute-done((bf16[128,2048]{1,0:T(8,128)(2,1)S(1)}, bf16[128,2048]{1,0:T(8,128)(2,1)S(1)}, u32[]{:S(2)}, u32[]{:S(2)}) %collective-permute-start.66) | collective-permute-done | bytes 524320 | tf_op jit(solution)/shard_map/ppermute | solution.py:51
  707.8 17.4 %two_grads.1 = bf16[2048,1408]{1,0:T(8,128)(2,1)} custom-call(bf16[1024,2048]{1,0:T(8,128)(2,1)} %copy-done.37, bf16[1024,2048]{1,0:T(8,128)(2,1)} %copy-done.38, bf16[1024,768]{1,0:T(8,128)(2,1)} %copy-done.75, bf16[1024,768]{1,0:T(8,128)(2,1)} %copy-done.76, bf16[1024,2048]{1,0:T(8,128)(2,1)} %get-tuple-element.735.refs_4_, ...), custom_call_target="tpu_custom_call" | custom-call | flops 10737418240 | bytes 28311552 | tf_op jit(solution)/shard_map/two_grads/pallas_call | solution.py:706
  735.6 14.0 %spread_rows.17 = (bf16[512,2048]{1,0:T(8,128)(2,1)}, bf16[256,2048]{1,0:T(8,128)(2,1)}, bf16[256,2048]{1,0:T(8,128)(2,1)}) custom-call(bf16[1024,1536]{1,0:T(8,128)(2,1)} %get-tuple-element.756.refs_7_.refs_0_, bf16[1024,512]{1,0:T(8,128)(2,1)} %get-tuple-element.757.refs_7_.refs_1_, ...), custom_call_target="tpu_custom_call" | custom-call | flops 8589934592 | bytes 16777216 | tf_op jit(solution)/shard_map/spread_rows/pallas_call | solution.py:616
  758.3 13.8 %collective-permute-done.73 = bf16[256,2048]{1,0:T(8,128)(2,1)S(1)} collective-permute-done((bf16[256,2048]{1,0:T(8,128)(2,1)}, bf16[256,2048]{1,0:T(8,128)(2,1)S(1)}, u32[]{:S(2)}, u32[]{:S(2)}) %collective-permute-start.73) | collective-permute-done | bytes 1048608 | tf_op jit(solution)/shard_map/ppermute | solution.py:51
  780.9 8.1 collective-permute-done.79.refs_5_
  (562 shorter events, 377.4 us)
Async XLA Ops:
  7.2 58.4 %all-gather.5.cloned.1.call-start = ((), (), s32[]{:S(2)}) async-start(), calls=%async_computation.3 | async-start | bytes 4128768 | tf_op jit(solution)/shard_map/all_gather | solution.py:107
  21.7 112.7 %all-gather.7.cloned.1.call-start = ((), (), s32[]{:S(2)}) async-start(), calls=%async_computation.4 | async-start | bytes 2359296 | tf_op jit(solution)/shard_map/all_gather | solution.py:107
  52.4 215.6 %all-gather.9.cloned.1.call-start = ((), (), s32[]{:S(2)}) async-start(), calls=%async_computation.5 | async-start | bytes 21233664 | tf_op jit(solution)/shard_map/all_gather | solution.py:107
  58.2 35.3 %collective-permute-start.12 = (bf16[64,4608]{1,0:T(8,128)(2,1)}, bf16[64,4608]{1,0:T(8,128)(2,1)}, u32[]{:S(2)}, u32[]{:S(2)}) collective-permute-start(bf16[64,4608]{1,0:T(8,128)(2,1)} %get-tuple-element.436), channel_id=1, source_target_pairs={{0,3},{1,2},{2,1},{3,0},{4,7},{5,6},{6,5},{7,4},{8,11},{9,10},{10,... | collective-permute-start | bytes 1769480 | tf_op jit(solution)/shard_map/ppermute | solution.py:51
  98.6 237.8 %all-gather.11.cloned.1.call-start = ((), (), s32[]{:S(2)}) async-start(), calls=%async_computation.6 | async-start | bytes 7077888 | tf_op jit(solution)/shard_map/all_gather | solution.py:107
  166.3 35.6 %collective-permute-start.23 = (bf16[256,2048]{1,0:T(8,128)(2,1)S(1)}, bf16[256,2048]{1,0:T(8,128)(2,1)}, u32[]{:S(2)}, u32[]{:S(2)}) collective-permute-start(bf16[256,2048]{1,0:T(8,128)(2,1)S(1)} %copy-done.41), channel_id=1, source_target_pairs={{0,1},{1,0},{2,3},{3,2},{4,5},{5,4},{6,7},{7,6},{8,9},{9,8},{10,11... | collective-permute-start | bytes 3145736 | tf_op jit(solution)/shard_map/ppermute | solution.py:51
  166.8 36.8 %collective-permute-start.24 = (bf16[256,2048]{1,0:T(8,128)(2,1)S(1)}, bf16[256,2048]{1,0:T(8,128)(2,1)}, u32[]{:S(2)}, u32[]{:S(2)}) collective-permute-start(bf16[256,2048]{1,0:T(8,128)(2,1)S(1)} %copy-done.41), channel_id=1, source_target_pairs={{0,2},{1,3},{2,0},{3,1},{4,6},{5,7},{6,4},{7,5},{8,10},{9,11},{10,... | collective-permute-start | bytes 3145736 | tf_op jit(solution)/shard_map/ppermute | solution.py:51
  188.3 36.0 %collective-permute-start.21 = (bf16[256,2048]{1,0:T(8,128)(2,1)S(1)}, bf16[256,2048]{1,0:T(8,128)(2,1)S(1)}, u32[]{:S(2)}, u32[]{:S(2)}) collective-permute-start(bf16[256,2048]{1,0:T(8,128)(2,1)S(1)} %multiply_convert_fusion.1.refs_0_), channel_id=1, source_target_pairs={{0,1},{1,0},{2,3},{3,2},{4,5},{5,4},{6,7},{7,6},{8,9},{9,8},{10,11... | collective-permute-start | bytes 3145736 | tf_op jit(solution)/shard_map/ppermute | solution.py:51
  190.0 35.9 %collective-permute-start.22 = (bf16[256,2048]{1,0:T(8,128)(2,1)S(1)}, bf16[256,2048]{1,0:T(8,128)(2,1)S(1)}, u32[]{:S(2)}, u32[]{:S(2)}) collective-permute-start(bf16[256,2048]{1,0:T(8,128)(2,1)S(1)} %multiply_convert_fusion.1.refs_0_), channel_id=1, source_target_pairs={{0,2},{1,3},{2,0},{3,1},{4,6},{5,7},{6,4},{7,5},{8,10},{9,11},{10,... | collective-permute-start | bytes 3145736 | tf_op jit(solution)/shard_map/ppermute | solution.py:51
  255.8 405.7 %reduce-scatter.4.cloned.1.call-start = ((), (), s32[]{:S(2)}) async-start(), calls=%async_computation.7 | async-start | bytes 21233664 | tf_op jit(solution)/shard_map/reduce_scatter | solution.py:161
  255.9 45.9 %collective-permute-start.36 = (bf16[256,2048]{1,0:T(8,128)(2,1)}, bf16[256,2048]{1,0:T(8,128)(2,1)}, u32[]{:S(2)}, u32[]{:S(2)}) collective-permute-start(bf16[256,2048]{1,0:T(8,128)(2,1)} %get-tuple-element.659.refs_5_), channel_id=1, source_target_pairs={{0,1},{1,0},{2,3},{3,2},{4,5},{5,4},{6,7},{7,6},{8,9},{9,8},{10,11... | collective-permute-start | bytes 3145736 | tf_op jit(solution)/shard_map/ppermute | solution.py:51
  257.4 44.4 %collective-permute-start.37 = (bf16[256,2048]{1,0:T(8,128)(2,1)}, bf16[256,2048]{1,0:T(8,128)(2,1)}, u32[]{:S(2)}, u32[]{:S(2)}) collective-permute-start(bf16[256,2048]{1,0:T(8,128)(2,1)} %get-tuple-element.659.refs_5_), channel_id=1, source_target_pairs={{0,2},{1,3},{2,0},{3,1},{4,6},{5,7},{6,4},{7,5},{8,10},{9,11},{10,... | collective-permute-start | bytes 3145736 | tf_op jit(solution)/shard_map/ppermute | solution.py:51
  257.9 42.2 %collective-permute-start.32 = (bf16[256,2048]{1,0:T(8,128)(2,1)}, bf16[256,2048]{1,0:T(8,128)(2,1)}, u32[]{:S(2)}, u32[]{:S(2)}) collective-permute-start(bf16[256,2048]{1,0:T(8,128)(2,1)} %get-tuple-element.525), channel_id=1, source_target_pairs={{0,1},{1,0},{2,3},{3,2},{4,5},{5,4},{6,7},{7,6},{8,9},{9,8},{10,11... | collective-permute-start | bytes 3145736 | tf_op jit(solution)/shard_map/ppermute | solution.py:51
  259.1 41.1 %collective-permute-start.33 = (bf16[256,2048]{1,0:T(8,128)(2,1)}, bf16[256,2048]{1,0:T(8,128)(2,1)}, u32[]{:S(2)}, u32[]{:S(2)}) collective-permute-start(bf16[256,2048]{1,0:T(8,128)(2,1)} %get-tuple-element.526), channel_id=1, source_target_pairs={{0,2},{1,3},{2,0},{3,1},{4,6},{5,7},{6,4},{7,5},{8,10},{9,11},{10,... | collective-permute-start | bytes 3145736 | tf_op jit(solution)/shard_map/ppermute | solution.py:51
  333.0 38.5 %collective-permute-start.44 = (bf16[128,2048]{1,0:T(8,128)(2,1)}, bf16[128,2048]{1,0:T(8,128)(2,1)}, u32[]{:S(2)}, u32[]{:S(2)}) collective-permute-start(bf16[128,2048]{1,0:T(8,128)(2,1)} %slice.387), channel_id=1, source_target_pairs={{0,2},{1,3},{2,0},{3,1},{4,6},{5,7},{6,4},{7,5},{8,10},{9,11},{10,... | collective-permute-start | bytes 1572872 | tf_op jit(solution)/shard_map/ppermute | solution.py:51
  334.7 38.4 %collective-permute-start.45 = (bf16[128,2048]{1,0:T(8,128)(2,1)S(1)}, bf16[128,2048]{1,0:T(8,128)(2,1)}, u32[]{:S(2)}, u32[]{:S(2)}) collective-permute-start(bf16[128,2048]{1,0:T(8,128)(2,1)S(1)} %slice.388), channel_id=1, source_target_pairs={{0,1},{1,0},{2,3},{3,2},{4,5},{5,4},{6,7},{7,6},{8,9},{9,8},{10,11... | collective-permute-start | bytes 1572872 | tf_op jit(solution)/shard_map/ppermute | solution.py:51
  371.1 37.6 %collective-permute-start.40 = (bf16[256,2048]{1,0:T(8,128)(2,1)}, bf16[256,2048]{1,0:T(8,128)(2,1)S(1)}, u32[]{:S(2)}, u32[]{:S(2)}) collective-permute-start(bf16[256,2048]{1,0:T(8,128)(2,1)} %get-tuple-element.557), channel_id=1, source_target_pairs={{0,1},{1,0},{2,3},{3,2},{4,5},{5,4},{6,7},{7,6},{8,9},{9,8},{10,11... | collective-permute-start | bytes 3145736 | tf_op jit(solution)/shard_map/ppermute | solution.py:51
  371.5 37.3 %collective-permute-start.41 = (bf16[256,2048]{1,0:T(8,128)(2,1)}, bf16[256,2048]{1,0:T(8,128)(2,1)S(1)}, u32[]{:S(2)}, u32[]{:S(2)}) collective-permute-start(bf16[256,2048]{1,0:T(8,128)(2,1)} %get-tuple-element.558), channel_id=1, source_target_pairs={{0,2},{1,3},{2,0},{3,1},{4,6},{5,7},{6,4},{7,5},{8,10},{9,11},{10,... | collective-permute-start | bytes 3145736 | tf_op jit(solution)/shard_map/ppermute | solution.py:51
  410.4 52.2 %collective-permute-start.46 = (bf16[128,2048]{1,0:T(8,128)(2,1)}, bf16[128,2048]{1,0:T(8,128)(2,1)S(1)}, u32[]{:S(2)}, u32[]{:S(2)}) collective-permute-start(bf16[128,2048]{1,0:T(8,128)(2,1)} %get-tuple-element.585), channel_id=1, source_target_pairs={{0,1},{1,0},{2,3},{3,2},{4,5},{5,4},{6,7},{7,6},{8,9},{9,8},{10,11... | collective-permute-start | bytes 1572872 | tf_op jit(solution)/shard_map/ppermute | solution.py:51
  412.1 50.5 %collective-permute-start.47 = (bf16[128,2048]{1,0:T(8,128)(2,1)}, bf16[128,2048]{1,0:T(8,128)(2,1)}, u32[]{:S(2)}, u32[]{:S(2)}) collective-permute-start(bf16[128,2048]{1,0:T(8,128)(2,1)} %get-tuple-element.586), channel_id=1, source_target_pairs={{0,2},{1,3},{2,0},{3,1},{4,6},{5,7},{6,4},{7,5},{8,10},{9,11},{10,... | collective-permute-start | bytes 1572872 | tf_op jit(solution)/shard_map/ppermute | solution.py:51
  462.6 268.0 %reduce-scatter.6.cloned.1.call-start = ((), (), s32[]{:S(2)}) async-start(), calls=%async_computation.8 | async-start | bytes 7077888 | tf_op jit(solution)/shard_map/reduce_scatter | solution.py:161
  661.6 135.2 %reduce-scatter.8.cloned.1.call-start = ((), (), s32[]{:S(2)}) async-start(), calls=%async_computation.9 | async-start | bytes 6488064 | tf_op jit(solution)/shard_map/reduce_scatter | solution.py:161
  676.6 48.6 %collective-permute-start.68 = (bf16[256,2048]{1,0:T(8,128)(2,1)}, bf16[256,2048]{1,0:T(8,128)(2,1)}, u32[]{:S(2)}, u32[]{:S(2)}) collective-permute-start(bf16[256,2048]{1,0:T(8,128)(2,1)} %get-tuple-element.745), channel_id=1, source_target_pairs={{0,1},{1,0},{2,3},{3,2},{4,5},{5,4},{6,7},{7,6},{8,9},{9,8},{10,11... | collective-permute-start | bytes 3145736 | tf_op jit(solution)/shard_map/ppermute | solution.py:51
  676.7 48.6 %collective-permute-start.69 = (bf16[256,2048]{1,0:T(8,128)(2,1)}, bf16[256,2048]{1,0:T(8,128)(2,1)}, u32[]{:S(2)}, u32[]{:S(2)}) collective-permute-start(bf16[256,2048]{1,0:T(8,128)(2,1)} %get-tuple-element.746), channel_id=1, source_target_pairs={{0,2},{1,3},{2,0},{3,1},{4,6},{5,7},{6,4},{7,5},{8,10},{9,11},{10,... | collective-permute-start | bytes 3145736 | tf_op jit(solution)/shard_map/ppermute | solution.py:51
  (170 other events, 3389.1 us)
Sparse Core Ops, SparseCore 0:
  21.8 43.7 all-gather.4
  67.2 27.9 all-gather.6
  98.7 169.2 all-gather.8
  269.4 62.9 all-gather.10
  462.7 187.7 reduce-scatter.3
  661.7 68.8 reduce-scatter.5
  732.9 63.2 reduce-scatter.7

commit v5 on v4

--- a/solution.py
+++ b/solution.py
@@ -190,6 +190,11 @@
     return key <= query
 
 
+def hide_later(scores, mask, low):
+    diagonal = jnp.where(mask, scores[low:], -1e30)
+    return jnp.concatenate([scores[:low], diagonal], axis=0) if low else diagonal
+
+
 def attention_forward_kernel(
     slot_ref, q_ref, k_ref, v_ref, cos_ref, sin_ref,
     out_ref, queries_ref, keys_ref, values_ref, total_ref, key_both, value_turned,
@@ -230,18 +235,11 @@
     for index in range(length // block):
         low, high = index * block, (index + 1) * block
         wide = two_heads(queries_ref[low:high, :] * jnp.asarray(HEAD_SIZE**-0.5, BF16))
-        diagonal = jnp.where(mask, dot(key_both[low:high, :], wide, NT), -1e30)
-        top = jnp.max(diagonal, axis=0, keepdims=True)
-        if index:
-            before = dot(key_both[:low, :], wide, NT)
-            top = jnp.maximum(top, jnp.max(before, axis=0, keepdims=True))
-        near = jnp.exp(diagonal - top)
-        total = jnp.sum(near, axis=0, keepdims=True)
-        attended = dot(value_turned[:, low:high], near.astype(BF16))
-        if index:
-            far = jnp.exp(before - top)
-            total = total + jnp.sum(far, axis=0, keepdims=True)
-            attended = attended + dot(value_turned[:, :low], far.astype(BF16))
+        scores = hide_later(dot(key_both[:high, :], wide, NT), mask, low)
+        top = jnp.max(scores, axis=0, keepdims=True)
+        prob = jnp.exp(scores - top)
+        total = jnp.sum(prob, axis=0, keepdims=True)
+        attended = dot(value_turned[:, :high], prob.astype(BF16))
         total_ref[0, index : index + 1, :] = top + jnp.log(total)
         attended = attended / total
         rows = jnp.concatenate([attended[:, :block], attended[:, block:]], axis=0).T.astype(BF16)
@@ -252,7 +250,7 @@
 
 
 def attention_backward_kernel(
-    slot_ref, queries_ref, keys_ref, values_ref, total_ref, grad_ref, cos_ref, sin_ref,
+    slot_ref, queries_ref, keys_ref, values_ref, total_ref, out_ref, grad_ref, cos_ref, sin_ref,
     grad_q_ref, grad_k_ref, grad_v_ref, key_both, value_both, key_turned, key_sum, value_sum,
     *, span, pairs_of_head
 ):
@@ -282,29 +280,26 @@
     for index in range(length // block):
         low, high = index * block, (index + 1) * block
         wide = two_heads(queries_ref[low:high, :] * jnp.asarray(HEAD_SIZE**-0.5, BF16))
-        grad = two_heads(
-            jnp.concatenate(
-                [grad_ref[place(index * each + part), :] for part in range(each)], axis=0
-            )
+        here = [place(index * each + part) for part in range(each)]
+        grad = jnp.concatenate([grad_ref[rows, :] for rows in here], axis=0)
+        out = jnp.concatenate([out_ref[rows, :] for rows in here], axis=0)
+        both = (grad.astype(F32) * out.astype(F32)).T
+        row_dot = jnp.concatenate(
+            [
+                jnp.sum(both[:HEAD_SIZE], axis=0, keepdims=True),
+                jnp.sum(both[HEAD_SIZE:], axis=0, keepdims=True),
+            ],
+            axis=1,
         )
+        grad = two_heads(grad)
         total = total_ref[0, index : index + 1, :]
-        ranges = [(low, high)] + ([(0, low)] if index else [])
-        probs, grad_probs, row_dot = [], [], 0.0
-        for start, stop in ranges:
-            scores = dot(key_both[start:stop, :], wide, NT)
-            if start == low:
-                scores = jnp.where(mask, scores, -1e30)
-            prob = jnp.exp(scores - total)
-            grad_prob = dot(value_both[start:stop, :], grad, NT)
-            row_dot = row_dot + jnp.sum(prob * grad_prob, axis=0, keepdims=True)
-            probs.append(prob)
-            grad_probs.append(grad_prob)
-        turned = 0.0
-        for (start, stop), prob, grad_prob in zip(ranges, probs, grad_probs):
-            grad_score = (prob * (grad_prob - row_dot)).astype(BF16)
-            value_sum[start:stop, :] += dot(prob.astype(BF16), grad)
-            key_sum[start:stop, :] += dot(grad_score, wide)
-            turned = turned + dot(key_turned[:, start:stop], grad_score)
+        scores = hide_later(dot(key_both[:high, :], wide, NT), mask, low)
+        prob = jnp.exp(scores - total)
+        grad_prob = dot(value_both[:high, :], grad, NT)
+        grad_score = (prob * (grad_prob - row_dot)).astype(BF16)
+        value_sum[:high, :] += dot(prob.astype(BF16), grad)
+        key_sum[:high, :] += dot(grad_score, wide)
+        turned = dot(key_turned[:, :high], grad_score)
         turned = turned * HEAD_SIZE**-0.5
         rows = jnp.concatenate([turned[:, :block], turned[:, block:]], axis=0).T
         for part in range(each):
@@ -380,13 +375,13 @@
             dimension_semantics=("arbitrary",), vmem_limit_bytes=48 << 20
         ),
         cost_estimate=pl.CostEstimate(
-            flops=8 * work, bytes_accessed=8 << 20, transcendentals=work // 128
+            flops=24 * work, bytes_accessed=8 << 20, transcendentals=work // 128
         ),
         name="attention_forward",
     )(slots, qkv, qkv, qkv, cos_lanes, sin_lanes)
 
 
-def attention_backward(kept, grad, slots, cos_lanes, sin_lanes, group_size):
+def attention_backward(kept, out, grad, slots, cos_lanes, sin_lanes, group_size):
     queries, keys, values, totals = kept
     length, query_width = queries.shape
     key_width = keys.shape[1]
@@ -410,6 +405,7 @@
                 by_block,
                 pl.BlockSpec((1, blocks, 2 * QUERY_BLOCK), lambda p, s: (p, 0, 0)),
                 by_pair,
+                by_pair,
                 whole,
                 whole,
             ],
@@ -431,10 +427,10 @@
             dimension_semantics=("arbitrary",), vmem_limit_bytes=48 << 20
         ),
         cost_estimate=pl.CostEstimate(
-            flops=20 * work, bytes_accessed=8 << 20, transcendentals=work // 128
+            flops=60 * work, bytes_accessed=8 << 20, transcendentals=work // 128
         ),
         name="attention_backward",
-    )(slots, queries, keys, values, totals, grad, cos_lanes, sin_lanes)
+    )(slots, queries, keys, values, totals, out, grad, cos_lanes, sin_lanes)
 
 
 def put_together(sources, plan, target, whole_ref, sems):
@@ -511,8 +507,8 @@
             dimension_semantics=("arbitrary",), vmem_limit_bytes=56 << 20
         ),
         "cost_estimate": pl.CostEstimate(
-            flops=6 * work,
-            bytes_accessed=2 * (2 * rows * depth + 3 * depth * width + 3 * rows * width),
+            flops=(6 * work) * 3,
+            bytes_accessed=(2 * (2 * rows * depth + 3 * depth * width + 3 * rows * width)) * 3,
             transcendentals=rows * width,
         ),
     }
@@ -584,8 +580,8 @@
         ],
         compiler_params=pltpu.CompilerParams(vmem_limit_bytes=48 << 20),
         cost_estimate=pl.CostEstimate(
-            flops=2 * rows * depth * weight.shape[1],
-            bytes_accessed=2 * (2 * rows * depth + (rows + depth) * weight.shape[1]),
+            flops=(2 * rows * depth * weight.shape[1]) * 3,
+            bytes_accessed=(2 * (2 * rows * depth + (rows + depth) * weight.shape[1])) * 3,
             transcendentals=0,
         ),
         name="rows_times",
@@ -628,8 +624,8 @@
             dimension_semantics=("arbitrary",), vmem_limit_bytes=56 << 20
         ),
         cost_estimate=pl.CostEstimate(
-            flops=2 * work,
-            bytes_accessed=2 * ((rows + depth) * sum(widths) + rows * depth),
+            flops=(2 * work) * 3,
+            bytes_accessed=(2 * ((rows + depth) * sum(widths) + rows * depth)) * 3,
             transcendentals=0,
         ),
         name="spread_rows",
@@ -672,8 +668,8 @@
             dimension_semantics=("arbitrary", "arbitrary"), vmem_limit_bytes=56 << 20
         ),
         cost_estimate=pl.CostEstimate(
-            flops=2 * work,
-            bytes_accessed=2 * (2 * seqs * rows * depth + (seqs * rows + depth) * columns),
+            flops=(2 * work) * 3,
+            bytes_accessed=(2 * (2 * seqs * rows * depth + (seqs * rows + depth) * columns)) * 3,
             transcendentals=0,
         ),
         name="feed_grads",
@@ -717,8 +713,8 @@
             dimension_semantics=("arbitrary",), vmem_limit_bytes=56 << 20
         ),
         cost_estimate=pl.CostEstimate(
-            flops=2 * work,
-            bytes_accessed=2 * (2 * seqs * rows * depth + (seqs * rows + depth) * sum(widths)),
+            flops=(2 * work) * 3,
+            bytes_accessed=(2 * (2 * seqs * rows * depth + (seqs * rows + depth) * sum(widths))) * 3,
             transcendentals=0,
         ),
         name="two_grads",
@@ -890,9 +886,9 @@
         grad_hidden = cot.astype(F32) + grad_middle
         return grad_hidden, grad_hidden.astype(BF16), gain_part
 
-    def attend_back(own, near, far, weight, kept, slots):
+    def attend_back(own, near, far, weight, kept, out, slots):
         grad_attn, merge_in = rows_times(own, near, far, weight)
-        parts = attention_backward(kept, grad_attn, slots, cos_lanes, sin_lanes, group_size)
+        parts = attention_backward(kept, out, grad_attn, slots, cos_lanes, sin_lanes, group_size)
         return merge_in, jnp.concatenate(parts, axis=1)
 
     def project_back(grads, weight):
@@ -907,9 +903,8 @@
             start += part.shape[0]
         return total
 
-    def attention_grads_of(attn_in, grad_qkv, merge_in, attn_out, rows, lower, gain_two_parts):
-        gain_one_sum = sum(gain_part_of(r, l) for r, l in zip(rows, lower))
-        gains = jnp.stack([gain_one_sum, sum(gain_two_parts)], axis=1)
+    def attention_grads_of(attn_in, grad_qkv, merge_in, attn_out, gain_one_parts, gain_two_parts):
+        gains = jnp.stack([sum(gain_one_parts), sum(gain_two_parts)], axis=1)
         gains = pad_columns(gains.astype(BF16), LANES)
         return two_grads(attn_in, grad_qkv, merge_in, attn_out, gains)
 
@@ -1010,7 +1005,7 @@
     near_b = chain.scatter_near(back_b)
     chain.wait(*merge_a_far)
     merge_in_a, grad_qkv_a = chain.run(
-        attend_back, merge_a, merge_a_near, merge_a_far, merge, kept_a, slots[0]
+        attend_back, merge_a, merge_a_near, merge_a_far, merge, kept_a, attn_out_a, slots[0]
     )
     far_b = chain.scatter_far(back_b, near_b)
     lower_a = chain.run(project_back, grad_qkv_a, projections)
@@ -1034,31 +1029,31 @@
     )
     chain.wait(*merge_b_far)
     out_a_near = chain.scatter_near(out_a)
-    merge_in_b, grad_qkv_b = chain.run(
-        attend_back, merge_b, merge_b_near, merge_b_far, merge, kept_b, slots[1]
-    )
+    gain_one_a = chain.run(gain_part_of, rows_a, lower_a)
     chain.wait(*out_a_near)
     chain.wait(sums[0])
     if many:
         sums.append(sum_over_dp(*chain.run(only, grads_last)))
     out_a_far = chain.scatter_far(out_a, out_a_near)
+    moved_feed = [chain.own_rows(sums[0])]
+    merge_in_b, grad_qkv_b = chain.run(
+        attend_back, merge_b, merge_b_near, merge_b_far, merge, kept_b, attn_out_b, slots[1]
+    )
     lower_b = chain.run(project_back, grad_qkv_b, projections)
+    chain.wait(*out_a_far)
     lower_b_near = chain.scatter_near(lower_b)
-    chain.wait(*out_a_far)
-    block_a = chain.run(block_of, hidden_a, out_a, out_a_near, out_a_far)
-    moved_feed = [chain.own_rows(sums[0])]
+    chain.wait(*moved_feed[0][1:])
+    gain_one_b = chain.run(gain_part_of, rows_b, lower_b)
     attention_grads = chain.run(
         attention_grads_of,
         [attn_in_a, attn_in_b],
         [grad_qkv_a, grad_qkv_b],
         [merge_in_a, merge_in_b],
         [attn_out_a, attn_out_b],
-        [rows_a, rows_b],
-        [lower_a, lower_b],
+        [gain_one_a, gain_one_b],
         [gain_two_a, gain_two_b],
     )
     chain.wait(*lower_b_near)
-    chain.wait(*moved_feed[0][1:])
     chain.wait(sums[-1])
     attention_sums = sum_over_dp(*chain.run(only, attention_grads))
     lower_b_far = chain.scatter_far(lower_b, lower_b_near)
@@ -1070,6 +1065,7 @@
     )
     moved_feed += [chain.own_rows(part) for part in sums[1:]]
     out_b_far = chain.scatter_far(out_b, out_b_near)
+    block_a = chain.run(block_of, hidden_a, out_a, out_a_near, out_a_far)
     chain.wait(*moved_feed[-1][1:])
     chain.wait(*out_b_far)
     block_b = chain.run(block_of, hidden_b, out_b, out_b_near, out_b_far)

time: 830 us -> 814 us (0.981)
    unnamed x226 -> x274, local copies, waits for them, and re-layouts: 38.6 us -> 38.2 us
  transfers between devices with their start and end apart: 92 -> 92, of which waited for: 41 -> 42; matrix products, arithmetic and copies ran while one was open for 15% -> 15% of each run, Pallas kernels for 46% -> 46%
where the time goes in v5:
time: 814 us; the launch traced here: 804 us
  Pallas kernels  369 us (45%)
  waiting for transfers between devices  176 us (22%)
  starting transfers between devices  92.1 us (11%)
  local copies, waits for them, and re-layouts  73.3 us (9%)
  other arithmetic  67 us (8%)
  between operations  16.6 us (2%)
  matrix products  10.1 us (1%)
    ppermute x85, waiting for transfers between devices, send(): lax.ppermute(block, 'ctx', [(i, i ^ bits) for i in range(4)])  159 us
    pallas_call x9, Pallas kernels, spread_rows(): pl.pallas_call(functools.partial(spread_kernel, count=len(lefts), begun=l...  107 us
    ppermute x85, starting transfers between devices, send(): lax.ppermute(block, 'ctx', [(i, i ^ bits) for i in range(4)])  91.6 us
    pallas_call x2, Pallas kernels, feed_grads(): pl.pallas_call(functools.partial(token_kernel, seqs=seqs, pair_tiles=pair...  73.5 us
    pallas_call x2, Pallas kernels, feed_first(): pl.pallas_call(functools.partial(feed_kernel, plan=plan, count=len(feeds)...  61.2 us
    unnamed x274, local copies, waits for them, and re-layouts  38.2 us
    pallas_call x2, Pallas kernels, attention_backward(): pl.pallas_call(functools.partial(attention_backward_kernel, span=length /...  37.7 us
    pallas_call x2, Pallas kernels, attention_forward(): pl.pallas_call(functools.partial(attention_forward_kernel, span=length //...  30.6 us
  transfers between devices with their start and end apart: 92, of which 42 were waited for; matrix products, arithmetic and copies ran while one was open for 15% of the time, Pallas kernels for 46%

profile of v5, /device:TPU:0, one launch (start us, length us, event | category | flops | bytes accessed | tf_op | source)
XLA Modules:
  0.0 804.3 jit_solution(13591663020271632081)
XLA Ops:
  38.6 12.6 %collective-permute-done.5 = bf16[64,512]{1,0:T(8,128)(2,1)S(1)} collective-permute-done((bf16[64,512]{1,0:T(8,128)(2,1)S(1)}, bf16[64,512]{1,0:T(8,128)(2,1)S(1)}, u32[]{:S(2)}, u32[]{:S(2)}) %collective-permute-start.5) | collective-permute-done | bytes 65568 | tf_op jit(solution)/shard_map/ppermute | solution.py:51
  83.7 9.8 %collective-permute-done.12 = bf16[64,4608]{1,0:T(8,128)(2,1)} collective-permute-done((bf16[64,4608]{1,0:T(8,128)(2,1)}, bf16[64,4608]{1,0:T(8,128)(2,1)}, u32[]{:S(2)}, u32[]{:S(2)}) %collective-permute-start.12) | collective-permute-done | bytes 589856 | tf_op jit(solution)/shard_map/ppermute | solution.py:51
  107.6 15.3 %attention_forward.2 = (bf16[1024,512]{1,0:T(8,128)(2,1)S(1)}, bf16[1024,512]{1,0:T(8,128)(2,1)S(1)}, bf16[1024,128]{1,0:T(8,128)(2,1)S(1)}, bf16[1024,128]{1,0:T(8,128)(2,1)S(1)}, f32[4,4,512]{2,1,0:T(4,128)S(1)}) custom-call(s32[8]{0:T(128)S(1)} %get-tuple-element.626.slot_ref, f32[1024,768]{1,0:T(8,128)} %fusion.46.q_ref.k_ref.v_ref, ...), custom_call_target="tpu_custom_call" | custom-call | flops 25769803776 | bytes 8388608 | tf_op jit(solution)/shard_map/attention_forward/pallas_call | solution.py:341
  169.8 15.3 %attention_forward.3 = (bf16[1024,512]{1,0:T(8,128)(2,1)S(1)}, bf16[1024,512]{1,0:T(8,128)(2,1)S(1)}, bf16[1024,128]{1,0:T(8,128)(2,1)S(1)}, bf16[1024,128]{1,0:T(8,128)(2,1)S(1)}, f32[4,4,512]{2,1,0:T(4,128)S(1)}) custom-call(s32[8]{0:T(128)S(1)} %get-tuple-element.711.slot_ref, f32[1024,768]{1,0:T(8,128)} %fusion.47.q_ref.k_ref.v_ref, ...), custom_call_target="tpu_custom_call" | custom-call | flops 25769803776 | bytes 8388608 | tf_op jit(solution)/shard_map/attention_forward/pallas_call | solution.py:341
  207.8 17.7 %collective-permute-done.21.refs_1_ = bf16[256,2048]{1,0:T(8,128)(2,1)S(1)} collective-permute-done((bf16[256,2048]{1,0:T(8,128)(2,1)S(1)}, bf16[256,2048]{1,0:T(8,128)(2,1)S(1)}, u32[]{:S(2)}, u32[]{:S(2)}) %collective-permute-start.21) | collective-permute-done | bytes 1048608 | tf_op jit(solution)/shard_map/ppermute | solution.py:51
  256.7 11.3 %all-gather.9.cloned.1.call-done.refs_10_.refs_11_.refs_1_.refs_2_ = bf16[2048,4608]{1,0:T(8,128)(2,1)} async-done(((bf16[256,4608]{1,0:T(8,128)(2,1)}), bf16[2048,4608]{1,0:T(8,128)(2,1)}) %all-gather.9.cloned.1.call-update) | async-done | bytes 18874384 | tf_op jit(solution)/shard_map/all_gather | solution.py:107
  268.0 31.0 %feed_first.2 = (bf16[1024,1536]{1,0:T(8,128)(2,1)}, bf16[1024,3072]{1,0:T(8,128)(2,1)}, bf16[1024,2048]{1,0:T(8,128)(2,1)}, bf16[1024,2048]{1,0:T(8,128)(2,1)}) custom-call(bf16[256,2048]{1,0:T(8,128)(2,1)} %copy-done.71, bf16[256,2048]{1,0:T(8,128)(2,1)} %copy-done.100, bf16[256,2048]{1,0:T(8,128)(2,1)} %collective-permute-done.22.refs_2_, ...), custom_call_target="tpu_custom_call" | custom-call | flops 57982058496 | bytes 110100480 | tf_op jit(solution)/shard_map/feed_first/pallas_call | solution.py:525
  307.7 19.1 %spread_rows.11.refs_2_ = f32[1024,2048]{1,0:T(8,128)} custom-call(bf16[1024,3072]{1,0:T(8,128)(2,1)} %get-tuple-element.595.refs_0_.refs_4_, bf16[2048,4608]{1,0:T(8,128)(2,1)} %all-gather.9.cloned.1.call-done.refs_10_.refs_11_.refs_1_.refs_2_), custom_call_target="tpu_custom_call" | custom-call | flops 38654705664 | bytes 69206016 | tf_op jit(solution)/shard_map/spread_rows/pallas_call | solution.py:612
  338.1 13.5 %feed_middle.2 = (bf16[1024,512]{1,0:T(8,128)(2,1)}, bf16[1024,1024]{1,0:T(8,128)(2,1)}) custom-call(bf16[1024,2048]{1,0:T(8,128)(2,1)} %get-tuple-element.677.feed_ref.refs_0_, bf16[1024,2048]{1,0:T(8,128)(2,1)} %get-tuple-element.679.down_in_ref.refs_2_, bf16[2048,1536]{1,0:T(8,128)(2,1)} %all-gather.11.cloned.1.call-done.pair_ref.down_ref.refs_1_.refs_3_, ...), custom_call_target="tpu_custom_call" | custom-call | flops 19327352832 | bytes 53477376 | tf_op jit(solution)/shard_map/feed_middle/pallas_call | solution.py:546
  351.5 9.0 %collective-permute-done.38.refs_1_ = bf16[256,2048]{1,0:T(8,128)(2,1)S(1)} collective-permute-done((bf16[256,2048]{1,0:T(8,128)(2,1)}, bf16[256,2048]{1,0:T(8,128)(2,1)S(1)}, u32[]{:S(2)}, u32[]{:S(2)}) %collective-permute-start.38) | collective-permute-done | bytes 1048608 | tf_op jit(solution)/shard_map/ppermute | solution.py:51
  364.2 10.0 %spread_rows.12 = (bf16[512,2048]{1,0:T(8,128)(2,1)}, bf16[256,2048]{1,0:T(8,128)(2,1)}, bf16[256,2048]{1,0:T(8,128)(2,1)}) custom-call(bf16[1024,1024]{1,0:T(8,128)(2,1)} %get-tuple-element.681.refs_0_.refs_4_, bf16[2048,1536]{1,0:T(8,128)(2,1)} %all-gather.11.cloned.1.call-done.pair_ref.down_ref.refs_1_.refs_3_, f32[1024,2048]{1,0:T(8,128)} %spread_rows.11.refs_2_), custom_call_target="tpu_custom_call" | custom-call | flops 12884901888 | bytes 31457280 | tf_op jit(solution)/shard_map/spread_rows/pallas_call | solution.py:612
  376.9 30.2 %feed_first.3 = (bf16[1024,1536]{1,0:T(8,128)(2,1)}, bf16[1024,3072]{1,0:T(8,128)(2,1)}, bf16[1024,2048]{1,0:T(8,128)(2,1)}, bf16[1024,2048]{1,0:T(8,128)(2,1)}) custom-call(bf16[256,2048]{1,0:T(8,128)(2,1)} %multiply_convert_fusion.refs_0_, bf16[256,2048]{1,0:T(8,128)(2,1)} %copy-done.101, bf16[256,2048]{1,0:T(8,128)(2,1)} %copy-done.102, ...), custom_call_target="tpu_custom_call" | custom-call | flops 57982058496 | bytes 110100480 | tf_op jit(solution)/shard_map/feed_first/pallas_call | solution.py:525
  410.2 50.0 %feed_grads.2 = bf16[2048,4608]{1,0:T(8,128)(2,1)} custom-call(bf16[1024,2048]{1,0:T(8,128)(2,1)} %get-tuple-element.677.feed_ref.refs_0_, bf16[1024,2048]{1,0:T(8,128)(2,1)} %get-tuple-element.678.refs_1_.feed_ref, bf16[1024,2048]{1,0:T(8,128)(2,1)} %get-tuple-element.679.down_in_ref.refs_2_, bf16[1024,2048]{1,0:T(8,128)(2,1)} %get-tuple-element.680.refs_3_.down_in_ref, ...), custom_call_target="tpu_custom_call" | custom-call | flops 115964116992 | bytes 163577856 | tf_op jit(solution)/shard_map/feed_grads/pallas_call | solution.py:661
  470.8 13.6 %feed_middle.3 = (bf16[1024,512]{1,0:T(8,128)(2,1)}, bf16[1024,1024]{1,0:T(8,128)(2,1)}) custom-call(bf16[1024,2048]{1,0:T(8,128)(2,1)} %get-tuple-element.678.refs_1_.feed_ref, bf16[1024,2048]{1,0:T(8,128)(2,1)} %get-tuple-element.680.refs_3_.down_in_ref, bf16[2048,1536]{1,0:T(8,128)(2,1)} %all-gather.11.cloned.1.call-done.pair_ref.down_ref.refs_1_.refs_3_, ...), custom_call_target="tpu_custom_call" | custom-call | flops 19327352832 | bytes 53477376 | tf_op jit(solution)/shard_map/feed_middle/pallas_call | solution.py:546
  494.6 24.2 %spread_rows.13 = (bf16[512,2048]{1,0:T(8,128)(2,1)}, bf16[256,2048]{1,0:T(8,128)(2,1)}, bf16[256,2048]{1,0:T(8,128)(2,1)}) custom-call(bf16[1024,3072]{1,0:T(8,128)(2,1)} %get-tuple-element.619.refs_5_.refs_0_, bf16[1024,1024]{1,0:T(8,128)(2,1)} %get-tuple-element.682.refs_1_.refs_5_, ...), custom_call_target="tpu_custom_call" | custom-call | flops 51539607552 | bytes 88080384 | tf_op jit(solution)/shard_map/spread_rows/pallas_call | solution.py:612
  526.5 18.9 %attention_backward.2 = (bf16[1024,512]{1,0:T(8,128)(2,1)S(1)}, bf16[1024,128]{1,0:T(8,128)(2,1)S(1)}, bf16[1024,128]{1,0:T(8,128)(2,1)S(1)}) custom-call(s32[8]{0:T(128)S(1)} %copy-done.9, bf16[1024,512]{1,0:T(8,128)(2,1)S(1)} %get-tuple-element.627.queries_ref, bf16[1024,128]{1,0:T(8,128)(2,1)S(1)} %get-tuple-element.628.keys_ref, ...), custom_call_target="tpu_custom_call" | custom-call | flops 64424509440 | bytes 8388608 | tf_op jit(solution)/shard_map/attention_backward/pallas_call | solution.py:395
  550.9 7.5 spread_rows.14
  560.6 13.5 %spread_rows.15 = (bf16[512,2048]{1,0:T(8,128)(2,1)}, bf16[256,2048]{1,0:T(8,128)(2,1)}, bf16[256,2048]{1,0:T(8,128)(2,1)}) custom-call(bf16[1024,1536]{1,0:T(8,128)(2,1)} %get-tuple-element.653.refs_6_.refs_0_, bf16[1024,512]{1,0:T(8,128)(2,1)} %get-tuple-element.683.refs_1_.refs_6_, ...), custom_call_target="tpu_custom_call" | custom-call | flops 25769803776 | bytes 50331648 | tf_op jit(solution)/shard_map/spread_rows/pallas_call | solution.py:612
  590.5 23.4 %feed_grads.3 = bf16[2048,1536]{1,0:T(8,128)(2,1)} custom-call(bf16[1024,2048]{1,0:T(8,128)(2,1)} %get-tuple-element.677.feed_ref.refs_0_, bf16[1024,2048]{1,0:T(8,128)(2,1)} %get-tuple-element.678.refs_1_.feed_ref, bf16[1024,2048]{1,0:T(8,128)(2,1)} %get-tuple-element.679.down_in_ref.refs_2_, bf16[1024,2048]{1,0:T(8,128)(2,1)} %get-tuple-element.680.refs_3_.down_in_ref, ...), custom_call_target="tpu_custom_call" | custom-call | flops 38654705664 | bytes 88080384 | tf_op jit(solution)/shard_map/feed_grads/pallas_call | solution.py:661
  637.2 13.2 %collective-permute-done.64 = bf16[256,2048]{1,0:T(8,128)(2,1)} collective-permute-done((bf16[256,2048]{1,0:T(8,128)(2,1)S(1)}, bf16[256,2048]{1,0:T(8,128)(2,1)}, u32[]{:S(2)}, u32[]{:S(2)}) %collective-permute-start.64) | collective-permute-done | bytes 1048608 | tf_op jit(solution)/shard_map/ppermute | solution.py:51
  666.4 18.8 %attention_backward.3 = (bf16[1024,512]{1,0:T(8,128)(2,1)S(1)}, bf16[1024,128]{1,0:T(8,128)(2,1)S(1)}, bf16[1024,128]{1,0:T(8,128)(2,1)S(1)}) custom-call(s32[8]{0:T(128)S(1)} %copy-done.7, bf16[1024,512]{1,0:T(8,128)(2,1)S(1)} %copy-done.21, bf16[1024,128]{1,0:T(8,128)(2,1)S(1)} %copy-done.23, bf16[1024,128]{1,0:T(8,128)(2,1)S(1)} %copy-done.25, ...), custom_call_target="tpu_custom_call" | custom-call | flops 64424509440 | bytes 8388608 | tf_op jit(solution)/shard_map/attention_backward/pallas_call | solution.py:395
  702.6 17.7 %two_grads.1 = bf16[2048,1408]{1,0:T(8,128)(2,1)} custom-call(bf16[1024,2048]{1,0:T(8,128)(2,1)} %copy-done.48, bf16[1024,2048]{1,0:T(8,128)(2,1)} %copy-done.49, bf16[1024,768]{1,0:T(8,128)(2,1)} %copy-done.88, bf16[1024,768]{1,0:T(8,128)(2,1)} %copy-done.89, bf16[1024,2048]{1,0:T(8,128)(2,1)} %get-tuple-element.746.refs_4_, ...), custom_call_target="tpu_custom_call" | custom-call | flops 32212254720 | bytes 84934656 | tf_op jit(solution)/shard_map/two_grads/pallas_call | solution.py:702
  724.2 13.2 %spread_rows.17 = (bf16[512,2048]{1,0:T(8,128)(2,1)}, bf16[256,2048]{1,0:T(8,128)(2,1)}, bf16[256,2048]{1,0:T(8,128)(2,1)}) custom-call(bf16[1024,1536]{1,0:T(8,128)(2,1)} %get-tuple-element.758.refs_7_.refs_0_, bf16[1024,512]{1,0:T(8,128)(2,1)} %get-tuple-element.759.refs_7_.refs_1_, ...), custom_call_target="tpu_custom_call" | custom-call | flops 25769803776 | bytes 50331648 | tf_op jit(solution)/shard_map/spread_rows/pallas_call | solution.py:612
  753.5 10.2 %collective-permute-done.73 = bf16[256,2048]{1,0:T(8,128)(2,1)S(1)} collective-permute-done((bf16[256,2048]{1,0:T(8,128)(2,1)}, bf16[256,2048]{1,0:T(8,128)(2,1)S(1)}, u32[]{:S(2)}, u32[]{:S(2)}) %collective-permute-start.73) | collective-permute-done | bytes 1048608 | tf_op jit(solution)/shard_map/ppermute | solution.py:51
  (612 shorter events, 368.4 us)
Async XLA Ops:
  7.2 58.4 %all-gather.5.cloned.1.call-start = ((), (), s32[]{:S(2)}) async-start(), calls=%async_computation.3 | async-start | bytes 4128768 | tf_op jit(solution)/shard_map/all_gather | solution.py:107
  21.7 106.6 %all-gather.7.cloned.1.call-start = ((), (), s32[]{:S(2)}) async-start(), calls=%async_computation.4 | async-start | bytes 2359296 | tf_op jit(solution)/shard_map/all_gather | solution.py:107
  52.4 215.5 %all-gather.9.cloned.1.call-start = ((), (), s32[]{:S(2)}) async-start(), calls=%async_computation.5 | async-start | bytes 21233664 | tf_op jit(solution)/shard_map/all_gather | solution.py:107
  98.6 237.5 %all-gather.11.cloned.1.call-start = ((), (), s32[]{:S(2)}) async-start(), calls=%async_computation.6 | async-start | bytes 7077888 | tf_op jit(solution)/shard_map/all_gather | solution.py:107
  167.7 35.4 %collective-permute-start.23 = (bf16[256,2048]{1,0:T(8,128)(2,1)S(1)}, bf16[256,2048]{1,0:T(8,128)(2,1)}, u32[]{:S(2)}, u32[]{:S(2)}) collective-permute-start(bf16[256,2048]{1,0:T(8,128)(2,1)S(1)} %copy-done.51), channel_id=1, source_target_pairs={{0,1},{1,0},{2,3},{3,2},{4,5},{5,4},{6,7},{7,6},{8,9},{9,8},{10,11... | collective-permute-start | bytes 3145736 | tf_op jit(solution)/shard_map/ppermute | solution.py:51
  167.9 37.3 %collective-permute-start.24 = (bf16[256,2048]{1,0:T(8,128)(2,1)S(1)}, bf16[256,2048]{1,0:T(8,128)(2,1)}, u32[]{:S(2)}, u32[]{:S(2)}) collective-permute-start(bf16[256,2048]{1,0:T(8,128)(2,1)S(1)} %copy-done.51), channel_id=1, source_target_pairs={{0,2},{1,3},{2,0},{3,1},{4,6},{5,7},{6,4},{7,5},{8,10},{9,11},{10,... | collective-permute-start | bytes 3145736 | tf_op jit(solution)/shard_map/ppermute | solution.py:51
  189.2 36.4 %collective-permute-start.21 = (bf16[256,2048]{1,0:T(8,128)(2,1)S(1)}, bf16[256,2048]{1,0:T(8,128)(2,1)S(1)}, u32[]{:S(2)}, u32[]{:S(2)}) collective-permute-start(bf16[256,2048]{1,0:T(8,128)(2,1)S(1)} %multiply_convert_fusion.1.refs_0_), channel_id=1, source_target_pairs={{0,1},{1,0},{2,3},{3,2},{4,5},{5,4},{6,7},{7,6},{8,9},{9,8},{10,11... | collective-permute-start | bytes 3145736 | tf_op jit(solution)/shard_map/ppermute | solution.py:51
  191.2 36.5 %collective-permute-start.22 = (bf16[256,2048]{1,0:T(8,128)(2,1)S(1)}, bf16[256,2048]{1,0:T(8,128)(2,1)}, u32[]{:S(2)}, u32[]{:S(2)}) collective-permute-start(bf16[256,2048]{1,0:T(8,128)(2,1)S(1)} %multiply_convert_fusion.1.refs_0_), channel_id=1, source_target_pairs={{0,2},{1,3},{2,0},{3,1},{4,6},{5,7},{6,4},{7,5},{8,10},{9,11},{10,... | collective-permute-start | bytes 3145736 | tf_op jit(solution)/shard_map/ppermute | solution.py:51
  252.1 48.6 %collective-permute-start.36 = (bf16[256,2048]{1,0:T(8,128)(2,1)}, bf16[256,2048]{1,0:T(8,128)(2,1)}, u32[]{:S(2)}, u32[]{:S(2)}) collective-permute-start(bf16[256,2048]{1,0:T(8,128)(2,1)} %get-tuple-element.664.refs_5_), channel_id=1, source_target_pairs={{0,1},{1,0},{2,3},{3,2},{4,5},{5,4},{6,7},{7,6},{8,9},{9,8},{10,11... | collective-permute-start | bytes 3145736 | tf_op jit(solution)/shard_map/ppermute | solution.py:51
  254.0 46.6 %collective-permute-start.37 = (bf16[256,2048]{1,0:T(8,128)(2,1)}, bf16[256,2048]{1,0:T(8,128)(2,1)}, u32[]{:S(2)}, u32[]{:S(2)}) collective-permute-start(bf16[256,2048]{1,0:T(8,128)(2,1)} %get-tuple-element.664.refs_5_), channel_id=1, source_target_pairs={{0,2},{1,3},{2,0},{3,1},{4,6},{5,7},{6,4},{7,5},{8,10},{9,11},{10,... | collective-permute-start | bytes 3145736 | tf_op jit(solution)/shard_map/ppermute | solution.py:51
  256.1 42.9 %collective-permute-start.32 = (bf16[256,2048]{1,0:T(8,128)(2,1)}, bf16[256,2048]{1,0:T(8,128)(2,1)}, u32[]{:S(2)}, u32[]{:S(2)}) collective-permute-start(bf16[256,2048]{1,0:T(8,128)(2,1)} %get-tuple-element.529), channel_id=1, source_target_pairs={{0,1},{1,0},{2,3},{3,2},{4,5},{5,4},{6,7},{7,6},{8,9},{9,8},{10,11... | collective-permute-start | bytes 3145736 | tf_op jit(solution)/shard_map/ppermute | solution.py:51
  256.6 42.4 %collective-permute-start.33 = (bf16[256,2048]{1,0:T(8,128)(2,1)}, bf16[256,2048]{1,0:T(8,128)(2,1)}, u32[]{:S(2)}, u32[]{:S(2)}) collective-permute-start(bf16[256,2048]{1,0:T(8,128)(2,1)} %get-tuple-element.530), channel_id=1, source_target_pairs={{0,2},{1,3},{2,0},{3,1},{4,6},{5,7},{6,4},{7,5},{8,10},{9,11},{10,... | collective-permute-start | bytes 3145736 | tf_op jit(solution)/shard_map/ppermute | solution.py:51
  256.6 393.8 %reduce-scatter.4.cloned.1.call-start = ((), (), s32[]{:S(2)}) async-start(), calls=%async_computation.7 | async-start | bytes 21233664 | tf_op jit(solution)/shard_map/reduce_scatter | solution.py:161
  303.6 72.1 %collective-permute-start.44 = (bf16[128,2048]{1,0:T(8,128)(2,1)}, bf16[128,2048]{1,0:T(8,128)(2,1)}, u32[]{:S(2)}, u32[]{:S(2)}) collective-permute-start(bf16[128,2048]{1,0:T(8,128)(2,1)} %slice.387), channel_id=1, source_target_pairs={{0,2},{1,3},{2,0},{3,1},{4,6},{5,7},{6,4},{7,5},{8,10},{9,11},{10,... | collective-permute-start | bytes 1572872 | tf_op jit(solution)/shard_map/ppermute | solution.py:51
  305.0 71.9 %collective-permute-start.45 = (bf16[128,2048]{1,0:T(8,128)(2,1)S(1)}, bf16[128,2048]{1,0:T(8,128)(2,1)}, u32[]{:S(2)}, u32[]{:S(2)}) collective-permute-start(bf16[128,2048]{1,0:T(8,128)(2,1)S(1)} %slice.388), channel_id=1, source_target_pairs={{0,1},{1,0},{2,3},{3,2},{4,5},{5,4},{6,7},{7,6},{8,9},{9,8},{10,11... | collective-permute-start | bytes 1572872 | tf_op jit(solution)/shard_map/ppermute | solution.py:51
  408.8 51.4 %collective-permute-start.46 = (bf16[128,2048]{1,0:T(8,128)(2,1)}, bf16[128,2048]{1,0:T(8,128)(2,1)S(1)}, u32[]{:S(2)}, u32[]{:S(2)}) collective-permute-start(bf16[128,2048]{1,0:T(8,128)(2,1)} %get-tuple-element.589), channel_id=1, source_target_pairs={{0,1},{1,0},{2,3},{3,2},{4,5},{5,4},{6,7},{7,6},{8,9},{9,8},{10,11... | collective-permute-start | bytes 1572872 | tf_op jit(solution)/shard_map/ppermute | solution.py:51
  409.4 50.8 %collective-permute-start.47 = (bf16[128,2048]{1,0:T(8,128)(2,1)}, bf16[128,2048]{1,0:T(8,128)(2,1)}, u32[]{:S(2)}, u32[]{:S(2)}) collective-permute-start(bf16[128,2048]{1,0:T(8,128)(2,1)} %get-tuple-element.590), channel_id=1, source_target_pairs={{0,2},{1,3},{2,0},{3,1},{4,6},{5,7},{6,4},{7,5},{8,10},{9,11},{10,... | collective-permute-start | bytes 1572872 | tf_op jit(solution)/shard_map/ppermute | solution.py:51
  460.3 260.0 %reduce-scatter.6.cloned.1.call-start = ((), (), s32[]{:S(2)}) async-start(), calls=%async_computation.8 | async-start | bytes 7077888 | tf_op jit(solution)/shard_map/reduce_scatter | solution.py:161
  650.4 132.8 %reduce-scatter.8.cloned.1.call-start = ((), (), s32[]{:S(2)}) async-start(), calls=%async_computation.9 | async-start | bytes 6488064 | tf_op jit(solution)/shard_map/reduce_scatter | solution.py:161
  654.6 39.4 %collective-permute-start.66 = (bf16[128,2048]{1,0:T(8,128)(2,1)}, bf16[128,2048]{1,0:T(8,128)(2,1)S(1)}, u32[]{:S(2)}, u32[]{:S(2)}) collective-permute-start(bf16[128,2048]{1,0:T(8,128)(2,1)} %get-tuple-element.709), channel_id=1, source_target_pairs={{0,1},{1,0},{2,3},{3,2},{4,5},{5,4},{6,7},{7,6},{8,9},{9,8},{10,11... | collective-permute-start | bytes 1572872 | tf_op jit(solution)/shard_map/ppermute | solution.py:51
  655.6 38.4 %collective-permute-start.67 = (bf16[128,2048]{1,0:T(8,128)(2,1)}, bf16[128,2048]{1,0:T(8,128)(2,1)}, u32[]{:S(2)}, u32[]{:S(2)}) collective-permute-start(bf16[128,2048]{1,0:T(8,128)(2,1)} %get-tuple-element.710), channel_id=1, source_target_pairs={{0,2},{1,3},{2,0},{3,1},{4,6},{5,7},{6,4},{7,5},{8,10},{9,11},{10,... | collective-permute-start | bytes 1572872 | tf_op jit(solution)/shard_map/ppermute | solution.py:51
  656.3 40.0 %collective-permute-start.70 = (bf16[64,4608]{1,0:T(8,128)(2,1)}, bf16[64,4608]{1,0:T(8,128)(2,1)S(1)}, u32[]{:S(2)}, u32[]{:S(2)}) collective-permute-start(bf16[64,4608]{1,0:T(8,128)(2,1)} %get-tuple-element.735), channel_id=1, source_target_pairs={{0,1},{1,0},{2,3},{3,2},{4,5},{5,4},{6,7},{7,6},{8,9},{9,8},{10,11... | collective-permute-start | bytes 1769480 | tf_op jit(solution)/shard_map/ppermute | solution.py:51
  657.5 38.9 %collective-permute-start.71 = (bf16[64,4608]{1,0:T(8,128)(2,1)}, bf16[64,4608]{1,0:T(8,128)(2,1)S(1)}, u32[]{:S(2)}, u32[]{:S(2)}) collective-permute-start(bf16[64,4608]{1,0:T(8,128)(2,1)} %get-tuple-element.736), channel_id=1, source_target_pairs={{0,2},{1,3},{2,0},{3,1},{4,6},{5,7},{6,4},{7,5},{8,10},{9,11},{10,... | collective-permute-start | bytes 1769480 | tf_op jit(solution)/shard_map/ppermute | solution.py:51
  658.7 37.7 %collective-permute-start.72 = (bf16[64,4608]{1,0:T(8,128)(2,1)}, bf16[64,4608]{1,0:T(8,128)(2,1)S(1)}, u32[]{:S(2)}, u32[]{:S(2)}) collective-permute-start(bf16[64,4608]{1,0:T(8,128)(2,1)} %get-tuple-element.737), channel_id=1, source_target_pairs={{0,3},{1,2},{2,1},{3,0},{4,7},{5,6},{6,5},{7,4},{8,11},{9,10},{10,... | collective-permute-start | bytes 1769480 | tf_op jit(solution)/shard_map/ppermute | solution.py:51
  (194 other events, 3621.6 us)
Sparse Core Ops, SparseCore 0:
  21.8 43.7 all-gather.4
  67.2 27.9 all-gather.6
  98.7 169.2 all-gather.8
  269.4 62.9 all-gather.10
  460.4 185.8 reduce-scatter.3
  650.5 66.6 reduce-scatter.5
  720.5 62.2 reduce-scatter.7

commit v6 on v5

--- a/solution.py
+++ b/solution.py
@@ -91,16 +91,8 @@
     def exchanged(self, received):
         if not square():
             return received[0]
-        rank = lax.axis_index("ctx")
         self.wait(*received[1:])
-
-        def lay(*received):
-            out = jnp.zeros((4,) + received[0].shape, received[0].dtype)
-            for member, value in enumerate(received):
-                out = lax.dynamic_update_index_in_dim(out, value, rank ^ member, 0)
-            return out
-
-        return self.run(lay, *received)
+        return self.run(stack_rows, received)
 
     def all_rows(self, received):
         mine = self.exchanged(received)
@@ -155,6 +147,29 @@
     low = parts[0][:half].astype(F32) + near[0][:half].astype(F32) + far[1].astype(F32)
     high = parts[0][half : 2 * half].astype(F32) + near[1][:half].astype(F32) + far[0].astype(F32)
     return jnp.concatenate([low, high], axis=0)
+
+
+def stack_kernel(place_ref, *refs):
+    rows = refs[0].shape[0]
+    for member, block in enumerate(refs[:-1]):
+        here = pl.ds(pl.multiple_of(place_ref[member] * rows, rows), rows)
+        refs[-1][here, :] = block[...]
+
+
+def stack_rows(blocks):
+    rows, width = blocks[0].shape
+    return pl.pallas_call(
+        stack_kernel,
+        grid_spec=pltpu.PrefetchScalarGridSpec(
+            num_scalar_prefetch=1,
+            grid=(1,),
+            in_specs=[pl.BlockSpec((rows, width), lambda i, p: (0, 0))] * 4,
+            out_specs=pl.BlockSpec((4 * rows, width), lambda i, p: (0, 0)),
+        ),
+        out_shape=jax.ShapeDtypeStruct((4 * rows, width), blocks[0].dtype),
+        compiler_params=pltpu.CompilerParams(vmem_limit_bytes=48 << 20),
+        name="stack_rows",
+    )(lax.axis_index("ctx") ^ jnp.arange(4, dtype=jnp.int32), *blocks)
 
 
 def sum_over_dp(grads):

time: 814 us -> 812 us (level)
  waiting for transfers between devices: 176 us -> 166 us
    unnamed x274 -> x269, local copies, waits for them, and re-layouts: 38.2 us -> 38.3 us
  transfers between devices with their start and end apart: 92 -> 92, of which waited for: 42 -> 41; matrix products, arithmetic and copies ran while one was open for 15% -> 15% of each run, Pallas kernels for 46% -> 46%
where the time goes in v6:
time: 812 us; the launch traced here: 803 us
  Pallas kernels  376 us (46%)
  waiting for transfers between devices  166 us (20%)
  starting transfers between devices  95.2 us (12%)
  local copies, waits for them, and re-layouts  73.4 us (9%)
  other arithmetic  65.5 us (8%)
  between operations  16.5 us (2%)
  matrix products  10.1 us (1%)
    ppermute x85, waiting for transfers between devices, send(): lax.ppermute(block, 'ctx', [(i, i ^ bits) for i in range(4)])  153 us
    pallas_call x9, Pallas kernels, spread_rows(): pl.pallas_call(functools.partial(spread_kernel, count=len(lefts), begun=l...  107 us
    ppermute x85, starting transfers between devices, send(): lax.ppermute(block, 'ctx', [(i, i ^ bits) for i in range(4)])  94.7 us
    pallas_call x2, Pallas kernels, feed_grads(): pl.pallas_call(functools.partial(token_kernel, seqs=seqs, pair_tiles=pair...  73.7 us
    pallas_call x2, Pallas kernels, feed_first(): pl.pallas_call(functools.partial(feed_kernel, plan=plan, count=len(feeds)...  61.1 us
    unnamed x269, local copies, waits for them, and re-layouts  38.3 us
    pallas_call x2, Pallas kernels, attention_backward(): pl.pallas_call(functools.partial(attention_backward_kernel, span=length /...  37.8 us
    pallas_call x2, Pallas kernels, attention_forward(): pl.pallas_call(functools.partial(attention_forward_kernel, span=length //...  30.6 us
  transfers between devices with their start and end apart: 92, of which 41 were waited for; matrix products, arithmetic and copies ran while one was open for 15% of the time, Pallas kernels for 46%

profile of v6, /device:TPU:0, one launch (start us, length us, event | category | flops | bytes accessed | tf_op | source)
XLA Modules:
  0.0 803.0 jit_solution(5970066620418348504)
XLA Ops:
  40.5 10.4 %collective-permute-done.5.refs_1_ = bf16[64,512]{1,0:T(8,128)(2,1)S(1)} collective-permute-done((bf16[64,512]{1,0:T(8,128)(2,1)S(1)}, bf16[64,512]{1,0:T(8,128)(2,1)S(1)}, u32[]{:S(2)}, u32[]{:S(2)}) %collective-permute-start.5) | collective-permute-done | bytes 65568 | tf_op jit(solution)/shard_map/ppermute | solution.py:51
  85.4 9.7 %collective-permute-done.12.refs_3_ = bf16[64,4608]{1,0:T(8,128)(2,1)S(1)} collective-permute-done((bf16[64,4608]{1,0:T(8,128)(2,1)}, bf16[64,4608]{1,0:T(8,128)(2,1)S(1)}, u32[]{:S(2)}, u32[]{:S(2)}) %collective-permute-start.12) | collective-permute-done | bytes 589856 | tf_op jit(solution)/shard_map/ppermute | solution.py:51
  106.6 15.3 %attention_forward.2 = (bf16[1024,512]{1,0:T(8,128)(2,1)S(1)}, bf16[1024,512]{1,0:T(8,128)(2,1)S(1)}, bf16[1024,128]{1,0:T(8,128)(2,1)S(1)}, bf16[1024,128]{1,0:T(8,128)(2,1)S(1)}, f32[4,4,512]{2,1,0:T(4,128)S(1)}) custom-call(s32[8]{0:T(128)S(1)} %get-tuple-element.626.slot_ref, f32[1024,768]{1,0:T(8,128)} %fusion.46.q_ref.k_ref.v_ref, ...), custom_call_target="tpu_custom_call" | custom-call | flops 25769803776 | bytes 8388608 | tf_op jit(solution)/shard_map/attention_forward/pallas_call | solution.py:356
  168.9 15.3 %attention_forward.3 = (bf16[1024,512]{1,0:T(8,128)(2,1)S(1)}, bf16[1024,512]{1,0:T(8,128)(2,1)S(1)}, bf16[1024,128]{1,0:T(8,128)(2,1)S(1)}, bf16[1024,128]{1,0:T(8,128)(2,1)S(1)}, f32[4,4,512]{2,1,0:T(4,128)S(1)}) custom-call(s32[8]{0:T(128)S(1)} %get-tuple-element.711.slot_ref, f32[1024,768]{1,0:T(8,128)} %fusion.47.q_ref.k_ref.v_ref, ...), custom_call_target="tpu_custom_call" | custom-call | flops 25769803776 | bytes 8388608 | tf_op jit(solution)/shard_map/attention_forward/pallas_call | solution.py:356
  206.0 18.7 %collective-permute-done.21.refs_1_ = bf16[256,2048]{1,0:T(8,128)(2,1)S(1)} collective-permute-done((bf16[256,2048]{1,0:T(8,128)(2,1)S(1)}, bf16[256,2048]{1,0:T(8,128)(2,1)S(1)}, u32[]{:S(2)}, u32[]{:S(2)}) %collective-permute-start.21) | collective-permute-done | bytes 1048608 | tf_op jit(solution)/shard_map/ppermute | solution.py:51
  256.6 10.0 %all-gather.9.cloned.1.call-done.refs_10_.refs_11_.refs_1_.refs_2_ = bf16[2048,4608]{1,0:T(8,128)(2,1)} async-done(((bf16[256,4608]{1,0:T(8,128)(2,1)}), bf16[2048,4608]{1,0:T(8,128)(2,1)}) %all-gather.9.cloned.1.call-update) | async-done | bytes 18874384 | tf_op jit(solution)/shard_map/all_gather | solution.py:99
  266.6 31.0 %feed_first.2 = (bf16[1024,1536]{1,0:T(8,128)(2,1)}, bf16[1024,3072]{1,0:T(8,128)(2,1)}, bf16[1024,2048]{1,0:T(8,128)(2,1)}, bf16[1024,2048]{1,0:T(8,128)(2,1)}) custom-call(bf16[256,2048]{1,0:T(8,128)(2,1)} %copy-done.76, bf16[256,2048]{1,0:T(8,128)(2,1)} %copy-done.101, bf16[256,2048]{1,0:T(8,128)(2,1)} %collective-permute-done.22.refs_2_, ...), custom_call_target="tpu_custom_call" | custom-call | flops 57982058496 | bytes 110100480 | tf_op jit(solution)/shard_map/feed_first/pallas_call | solution.py:540
  307.1 19.2 %spread_rows.11.refs_2_ = f32[1024,2048]{1,0:T(8,128)} custom-call(bf16[1024,3072]{1,0:T(8,128)(2,1)} %get-tuple-element.595.refs_0_.refs_4_, bf16[2048,4608]{1,0:T(8,128)(2,1)} %all-gather.9.cloned.1.call-done.refs_10_.refs_11_.refs_1_.refs_2_), custom_call_target="tpu_custom_call" | custom-call | flops 38654705664 | bytes 69206016 | tf_op jit(solution)/shard_map/spread_rows/pallas_call | solution.py:627
  336.7 13.5 %feed_middle.2 = (bf16[1024,512]{1,0:T(8,128)(2,1)}, bf16[1024,1024]{1,0:T(8,128)(2,1)}) custom-call(bf16[1024,2048]{1,0:T(8,128)(2,1)} %get-tuple-element.677.feed_ref.refs_0_, bf16[1024,2048]{1,0:T(8,128)(2,1)} %get-tuple-element.679.down_in_ref.refs_2_, bf16[2048,1536]{1,0:T(8,128)(2,1)} %all-gather.11.cloned.1.call-done.pair_ref.down_ref.refs_1_.refs_3_, ...), custom_call_target="tpu_custom_call" | custom-call | flops 19327352832 | bytes 53477376 | tf_op jit(solution)/shard_map/feed_middle/pallas_call | solution.py:561
  350.2 8.8 %collective-permute-done.38.refs_1_ = bf16[256,2048]{1,0:T(8,128)(2,1)S(1)} collective-permute-done((bf16[256,2048]{1,0:T(8,128)(2,1)S(1)}, bf16[256,2048]{1,0:T(8,128)(2,1)S(1)}, u32[]{:S(2)}, u32[]{:S(2)}) %collective-permute-start.38) | collective-permute-done | bytes 1048608 | tf_op jit(solution)/shard_map/ppermute | solution.py:51
  361.5 10.0 %spread_rows.12 = (bf16[512,2048]{1,0:T(8,128)(2,1)}, bf16[256,2048]{1,0:T(8,128)(2,1)}, bf16[256,2048]{1,0:T(8,128)(2,1)}) custom-call(bf16[1024,1024]{1,0:T(8,128)(2,1)} %get-tuple-element.681.refs_0_.refs_4_, bf16[2048,1536]{1,0:T(8,128)(2,1)} %all-gather.11.cloned.1.call-done.pair_ref.down_ref.refs_1_.refs_3_, f32[1024,2048]{1,0:T(8,128)} %spread_rows.11.refs_2_), custom_call_target="tpu_custom_call" | custom-call | flops 12884901888 | bytes 31457280 | tf_op jit(solution)/shard_map/spread_rows/pallas_call | solution.py:627
  375.3 30.1 %feed_first.3 = (bf16[1024,1536]{1,0:T(8,128)(2,1)}, bf16[1024,3072]{1,0:T(8,128)(2,1)}, bf16[1024,2048]{1,0:T(8,128)(2,1)}, bf16[1024,2048]{1,0:T(8,128)(2,1)}) custom-call(bf16[256,2048]{1,0:T(8,128)(2,1)} %copy-done.82, bf16[256,2048]{1,0:T(8,128)(2,1)} %copy-done.102, bf16[256,2048]{1,0:T(8,128)(2,1)} %copy-done.103, bf16[128,2048]{1,0:T(8,128)(2,1)} %copy-done.123, ...), custom_call_target="tpu_custom_call" | custom-call | flops 57982058496 | bytes 110100480 | tf_op jit(solution)/shard_map/feed_first/pallas_call | solution.py:540
  407.9 50.4 %feed_grads.2 = bf16[2048,4608]{1,0:T(8,128)(2,1)} custom-call(bf16[1024,2048]{1,0:T(8,128)(2,1)} %get-tuple-element.677.feed_ref.refs_0_, bf16[1024,2048]{1,0:T(8,128)(2,1)} %get-tuple-element.678.refs_1_.feed_ref, bf16[1024,2048]{1,0:T(8,128)(2,1)} %get-tuple-element.679.down_in_ref.refs_2_, bf16[1024,2048]{1,0:T(8,128)(2,1)} %get-tuple-element.680.refs_3_.down_in_ref, ...), custom_call_target="tpu_custom_call" | custom-call | flops 115964116992 | bytes 163577856 | tf_op jit(solution)/shard_map/feed_grads/pallas_call | solution.py:676
  469.1 13.6 %feed_middle.3 = (bf16[1024,512]{1,0:T(8,128)(2,1)}, bf16[1024,1024]{1,0:T(8,128)(2,1)}) custom-call(bf16[1024,2048]{1,0:T(8,128)(2,1)} %get-tuple-element.678.refs_1_.feed_ref, bf16[1024,2048]{1,0:T(8,128)(2,1)} %get-tuple-element.680.refs_3_.down_in_ref, bf16[2048,1536]{1,0:T(8,128)(2,1)} %all-gather.11.cloned.1.call-done.pair_ref.down_ref.refs_1_.refs_3_, ...), custom_call_target="tpu_custom_call" | custom-call | flops 19327352832 | bytes 53477376 | tf_op jit(solution)/shard_map/feed_middle/pallas_call | solution.py:561
  492.6 24.3 %spread_rows.13 = (bf16[512,2048]{1,0:T(8,128)(2,1)}, bf16[256,2048]{1,0:T(8,128)(2,1)}, bf16[256,2048]{1,0:T(8,128)(2,1)}) custom-call(bf16[1024,3072]{1,0:T(8,128)(2,1)} %get-tuple-element.619.refs_5_.refs_0_, bf16[1024,1024]{1,0:T(8,128)(2,1)} %get-tuple-element.682.refs_1_.refs_5_, ...), custom_call_target="tpu_custom_call" | custom-call | flops 51539607552 | bytes 88080384 | tf_op jit(solution)/shard_map/spread_rows/pallas_call | solution.py:627
  524.5 19.0 %attention_backward.2 = (bf16[1024,512]{1,0:T(8,128)(2,1)S(1)}, bf16[1024,128]{1,0:T(8,128)(2,1)S(1)}, bf16[1024,128]{1,0:T(8,128)(2,1)S(1)}) custom-call(s32[8]{0:T(128)S(1)} %copy-done.11, bf16[1024,512]{1,0:T(8,128)(2,1)S(1)} %get-tuple-element.627.queries_ref, bf16[1024,128]{1,0:T(8,128)(2,1)S(1)} %copy-done.29, bf16[1024,128]{1,0:T(8,128)(2,1)S(1)} %copy-done.31, ...), custom_call_target="tpu_custom_call" | custom-call | flops 64424509440 | bytes 8388608 | tf_op jit(solution)/shard_map/attention_backward/pallas_call | solution.py:410
  549.3 7.4 spread_rows.14
  558.8 13.5 %spread_rows.15 = (bf16[512,2048]{1,0:T(8,128)(2,1)}, bf16[256,2048]{1,0:T(8,128)(2,1)}, bf16[256,2048]{1,0:T(8,128)(2,1)}) custom-call(bf16[1024,1536]{1,0:T(8,128)(2,1)} %get-tuple-element.653.refs_6_.refs_0_, bf16[1024,512]{1,0:T(8,128)(2,1)} %get-tuple-element.683.refs_1_.refs_6_, ...), custom_call_target="tpu_custom_call" | custom-call | flops 25769803776 | bytes 50331648 | tf_op jit(solution)/shard_map/spread_rows/pallas_call | solution.py:627
  589.4 23.3 %feed_grads.3 = bf16[2048,1536]{1,0:T(8,128)(2,1)} custom-call(bf16[1024,2048]{1,0:T(8,128)(2,1)} %get-tuple-element.677.feed_ref.refs_0_, bf16[1024,2048]{1,0:T(8,128)(2,1)} %get-tuple-element.678.refs_1_.feed_ref, bf16[1024,2048]{1,0:T(8,128)(2,1)} %get-tuple-element.679.down_in_ref.refs_2_, bf16[1024,2048]{1,0:T(8,128)(2,1)} %get-tuple-element.680.refs_3_.down_in_ref, ...), custom_call_target="tpu_custom_call" | custom-call | flops 38654705664 | bytes 88080384 | tf_op jit(solution)/shard_map/feed_grads/pallas_call | solution.py:676
  635.3 12.9 %collective-permute-done.64 = bf16[256,2048]{1,0:T(8,128)(2,1)} collective-permute-done((bf16[256,2048]{1,0:T(8,128)(2,1)S(1)}, bf16[256,2048]{1,0:T(8,128)(2,1)}, u32[]{:S(2)}, u32[]{:S(2)}) %collective-permute-start.64) | collective-permute-done | bytes 1048608 | tf_op jit(solution)/shard_map/ppermute | solution.py:51
  664.9 18.8 %attention_backward.3 = (bf16[1024,512]{1,0:T(8,128)(2,1)S(1)}, bf16[1024,128]{1,0:T(8,128)(2,1)S(1)}, bf16[1024,128]{1,0:T(8,128)(2,1)S(1)}) custom-call(s32[8]{0:T(128)S(1)} %copy-done.9, bf16[1024,512]{1,0:T(8,128)(2,1)S(1)} %copy-done.23, bf16[1024,128]{1,0:T(8,128)(2,1)S(1)} %copy-done.25, bf16[1024,128]{1,0:T(8,128)(2,1)S(1)} %copy-done.27, ...), custom_call_target="tpu_custom_call" | custom-call | flops 64424509440 | bytes 8388608 | tf_op jit(solution)/shard_map/attention_backward/pallas_call | solution.py:410
  700.6 17.7 %two_grads.1 = bf16[2048,1408]{1,0:T(8,128)(2,1)} custom-call(bf16[1024,2048]{1,0:T(8,128)(2,1)} %copy-done.53, bf16[1024,2048]{1,0:T(8,128)(2,1)} %copy-done.54, bf16[1024,768]{1,0:T(8,128)(2,1)} %copy-done.88, bf16[1024,768]{1,0:T(8,128)(2,1)} %copy-done.89, bf16[1024,2048]{1,0:T(8,128)(2,1)} %get-tuple-element.746.refs_4_, ...), custom_call_target="tpu_custom_call" | custom-call | flops 32212254720 | bytes 84934656 | tf_op jit(solution)/shard_map/two_grads/pallas_call | solution.py:717
  722.7 13.3 %spread_rows.17 = (bf16[512,2048]{1,0:T(8,128)(2,1)}, bf16[256,2048]{1,0:T(8,128)(2,1)}, bf16[256,2048]{1,0:T(8,128)(2,1)}) custom-call(bf16[1024,1536]{1,0:T(8,128)(2,1)} %get-tuple-element.758.refs_7_.refs_0_, bf16[1024,512]{1,0:T(8,128)(2,1)} %get-tuple-element.759.refs_7_.refs_1_, ...), custom_call_target="tpu_custom_call" | custom-call | flops 25769803776 | bytes 50331648 | tf_op jit(solution)/shard_map/spread_rows/pallas_call | solution.py:627
  751.5 10.8 %collective-permute-done.73 = bf16[256,2048]{1,0:T(8,128)(2,1)S(1)} collective-permute-done((bf16[256,2048]{1,0:T(8,128)(2,1)}, bf16[256,2048]{1,0:T(8,128)(2,1)S(1)}, u32[]{:S(2)}, u32[]{:S(2)}) %collective-permute-start.73) | collective-permute-done | bytes 1048608 | tf_op jit(solution)/shard_map/ppermute | solution.py:51
  (592 shorter events, 369.6 us)
Async XLA Ops:
  7.2 58.2 %all-gather.5.cloned.1.call-start = ((), (), s32[]{:S(2)}) async-start(), calls=%async_computation.3 | async-start | bytes 4128768 | tf_op jit(solution)/shard_map/all_gather | solution.py:99
  21.5 105.9 %all-gather.7.cloned.1.call-start = ((), (), s32[]{:S(2)}) async-start(), calls=%async_computation.4 | async-start | bytes 2359296 | tf_op jit(solution)/shard_map/all_gather | solution.py:99
  52.6 214.0 %all-gather.9.cloned.1.call-start = ((), (), s32[]{:S(2)}) async-start(), calls=%async_computation.5 | async-start | bytes 21233664 | tf_op jit(solution)/shard_map/all_gather | solution.py:99
  97.2 237.4 %all-gather.11.cloned.1.call-start = ((), (), s32[]{:S(2)}) async-start(), calls=%async_computation.6 | async-start | bytes 7077888 | tf_op jit(solution)/shard_map/all_gather | solution.py:99
  166.8 35.4 %collective-permute-start.23 = (bf16[256,2048]{1,0:T(8,128)(2,1)S(1)}, bf16[256,2048]{1,0:T(8,128)(2,1)S(1)}, u32[]{:S(2)}, u32[]{:S(2)}) collective-permute-start(bf16[256,2048]{1,0:T(8,128)(2,1)S(1)} %copy-done.58), channel_id=1, source_target_pairs={{0,1},{1,0},{2,3},{3,2},{4,5},{5,4},{6,7},{7,6},{8,9},{9,8},{10,11... | collective-permute-start | bytes 3145736 | tf_op jit(solution)/shard_map/ppermute | solution.py:51
  167.0 37.2 %collective-permute-start.24 = (bf16[256,2048]{1,0:T(8,128)(2,1)S(1)}, bf16[256,2048]{1,0:T(8,128)(2,1)}, u32[]{:S(2)}, u32[]{:S(2)}) collective-permute-start(bf16[256,2048]{1,0:T(8,128)(2,1)S(1)} %copy-done.58), channel_id=1, source_target_pairs={{0,2},{1,3},{2,0},{3,1},{4,6},{5,7},{6,4},{7,5},{8,10},{9,11},{10,... | collective-permute-start | bytes 3145736 | tf_op jit(solution)/shard_map/ppermute | solution.py:51
  188.3 36.4 %collective-permute-start.21 = (bf16[256,2048]{1,0:T(8,128)(2,1)S(1)}, bf16[256,2048]{1,0:T(8,128)(2,1)S(1)}, u32[]{:S(2)}, u32[]{:S(2)}) collective-permute-start(bf16[256,2048]{1,0:T(8,128)(2,1)S(1)} %multiply_convert_fusion.1.refs_0_), channel_id=1, source_target_pairs={{0,1},{1,0},{2,3},{3,2},{4,5},{5,4},{6,7},{7,6},{8,9},{9,8},{10,11... | collective-permute-start | bytes 3145736 | tf_op jit(solution)/shard_map/ppermute | solution.py:51
  190.2 36.5 %collective-permute-start.22 = (bf16[256,2048]{1,0:T(8,128)(2,1)S(1)}, bf16[256,2048]{1,0:T(8,128)(2,1)}, u32[]{:S(2)}, u32[]{:S(2)}) collective-permute-start(bf16[256,2048]{1,0:T(8,128)(2,1)S(1)} %multiply_convert_fusion.1.refs_0_), channel_id=1, source_target_pairs={{0,2},{1,3},{2,0},{3,1},{4,6},{5,7},{6,4},{7,5},{8,10},{9,11},{10,... | collective-permute-start | bytes 3145736 | tf_op jit(solution)/shard_map/ppermute | solution.py:51
  252.4 395.8 %reduce-scatter.4.cloned.1.call-start = ((), (), s32[]{:S(2)}) async-start(), calls=%async_computation.7 | async-start | bytes 21233664 | tf_op jit(solution)/shard_map/reduce_scatter | solution.py:176
  252.5 46.8 %collective-permute-start.36 = (bf16[256,2048]{1,0:T(8,128)(2,1)S(1)}, bf16[256,2048]{1,0:T(8,128)(2,1)}, u32[]{:S(2)}, u32[]{:S(2)}) collective-permute-start(bf16[256,2048]{1,0:T(8,128)(2,1)S(1)} %copy-done.56), channel_id=1, source_target_pairs={{0,1},{1,0},{2,3},{3,2},{4,5},{5,4},{6,7},{7,6},{8,9},{9,8},{10,11... | collective-permute-start | bytes 3145736 | tf_op jit(solution)/shard_map/ppermute | solution.py:51
  253.7 45.5 %collective-permute-start.37 = (bf16[256,2048]{1,0:T(8,128)(2,1)S(1)}, bf16[256,2048]{1,0:T(8,128)(2,1)}, u32[]{:S(2)}, u32[]{:S(2)}) collective-permute-start(bf16[256,2048]{1,0:T(8,128)(2,1)S(1)} %copy-done.56), channel_id=1, source_target_pairs={{0,2},{1,3},{2,0},{3,1},{4,6},{5,7},{6,4},{7,5},{8,10},{9,11},{10,... | collective-permute-start | bytes 3145736 | tf_op jit(solution)/shard_map/ppermute | solution.py:51
  255.5 42.1 %collective-permute-start.32 = (bf16[256,2048]{1,0:T(8,128)(2,1)}, bf16[256,2048]{1,0:T(8,128)(2,1)}, u32[]{:S(2)}, u32[]{:S(2)}) collective-permute-start(bf16[256,2048]{1,0:T(8,128)(2,1)} %get-tuple-element.529), channel_id=1, source_target_pairs={{0,1},{1,0},{2,3},{3,2},{4,5},{5,4},{6,7},{7,6},{8,9},{9,8},{10,11... | collective-permute-start | bytes 3145736 | tf_op jit(solution)/shard_map/ppermute | solution.py:51
  256.1 41.5 %collective-permute-start.33 = (bf16[256,2048]{1,0:T(8,128)(2,1)}, bf16[256,2048]{1,0:T(8,128)(2,1)}, u32[]{:S(2)}, u32[]{:S(2)}) collective-permute-start(bf16[256,2048]{1,0:T(8,128)(2,1)} %get-tuple-element.530), channel_id=1, source_target_pairs={{0,2},{1,3},{2,0},{3,1},{4,6},{5,7},{6,4},{7,5},{8,10},{9,11},{10,... | collective-permute-start | bytes 3145736 | tf_op jit(solution)/shard_map/ppermute | solution.py:51
  303.0 70.0 %collective-permute-start.44 = (bf16[128,2048]{1,0:T(8,128)(2,1)}, bf16[128,2048]{1,0:T(8,128)(2,1)}, u32[]{:S(2)}, u32[]{:S(2)}) collective-permute-start(bf16[128,2048]{1,0:T(8,128)(2,1)} %slice.387), channel_id=1, source_target_pairs={{0,2},{1,3},{2,0},{3,1},{4,6},{5,7},{6,4},{7,5},{8,10},{9,11},{10,... | collective-permute-start | bytes 1572872 | tf_op jit(solution)/shard_map/ppermute | solution.py:51
  304.4 70.1 %collective-permute-start.45 = (bf16[128,2048]{1,0:T(8,128)(2,1)}, bf16[128,2048]{1,0:T(8,128)(2,1)}, u32[]{:S(2)}, u32[]{:S(2)}) collective-permute-start(bf16[128,2048]{1,0:T(8,128)(2,1)} %slice.388), channel_id=1, source_target_pairs={{0,1},{1,0},{2,3},{3,2},{4,5},{5,4},{6,7},{7,6},{8,9},{9,8},{10,11... | collective-permute-start | bytes 1572872 | tf_op jit(solution)/shard_map/ppermute | solution.py:51
  406.8 51.6 %collective-permute-start.46 = (bf16[128,2048]{1,0:T(8,128)(2,1)}, bf16[128,2048]{1,0:T(8,128)(2,1)}, u32[]{:S(2)}, u32[]{:S(2)}) collective-permute-start(bf16[128,2048]{1,0:T(8,128)(2,1)} %get-tuple-element.589), channel_id=1, source_target_pairs={{0,1},{1,0},{2,3},{3,2},{4,5},{5,4},{6,7},{7,6},{8,9},{9,8},{10,11... | collective-permute-start | bytes 1572872 | tf_op jit(solution)/shard_map/ppermute | solution.py:51
  407.3 51.0 %collective-permute-start.47 = (bf16[128,2048]{1,0:T(8,128)(2,1)}, bf16[128,2048]{1,0:T(8,128)(2,1)}, u32[]{:S(2)}, u32[]{:S(2)}) collective-permute-start(bf16[128,2048]{1,0:T(8,128)(2,1)} %get-tuple-element.590), channel_id=1, source_target_pairs={{0,2},{1,3},{2,0},{3,1},{4,6},{5,7},{6,4},{7,5},{8,10},{9,11},{10,... | collective-permute-start | bytes 1572872 | tf_op jit(solution)/shard_map/ppermute | solution.py:51
  458.4 259.9 %reduce-scatter.6.cloned.1.call-start = ((), (), s32[]{:S(2)}) async-start(), calls=%async_computation.8 | async-start | bytes 7077888 | tf_op jit(solution)/shard_map/reduce_scatter | solution.py:176
  648.2 133.7 %reduce-scatter.8.cloned.1.call-start = ((), (), s32[]{:S(2)}) async-start(), calls=%async_computation.9 | async-start | bytes 6488064 | tf_op jit(solution)/shard_map/reduce_scatter | solution.py:176
  652.4 40.0 %collective-permute-start.66 = (bf16[128,2048]{1,0:T(8,128)(2,1)}, bf16[128,2048]{1,0:T(8,128)(2,1)S(1)}, u32[]{:S(2)}, u32[]{:S(2)}) collective-permute-start(bf16[128,2048]{1,0:T(8,128)(2,1)} %get-tuple-element.709), channel_id=1, source_target_pairs={{0,1},{1,0},{2,3},{3,2},{4,5},{5,4},{6,7},{7,6},{8,9},{9,8},{10,11... | collective-permute-start | bytes 1572872 | tf_op jit(solution)/shard_map/ppermute | solution.py:51
  654.5 37.9 %collective-permute-start.67 = (bf16[128,2048]{1,0:T(8,128)(2,1)}, bf16[128,2048]{1,0:T(8,128)(2,1)}, u32[]{:S(2)}, u32[]{:S(2)}) collective-permute-start(bf16[128,2048]{1,0:T(8,128)(2,1)} %get-tuple-element.710), channel_id=1, source_target_pairs={{0,2},{1,3},{2,0},{3,1},{4,6},{5,7},{6,4},{7,5},{8,10},{9,11},{10,... | collective-permute-start | bytes 1572872 | tf_op jit(solution)/shard_map/ppermute | solution.py:51
  654.8 39.5 %collective-permute-start.70 = (bf16[64,4608]{1,0:T(8,128)(2,1)}, bf16[64,4608]{1,0:T(8,128)(2,1)S(1)}, u32[]{:S(2)}, u32[]{:S(2)}) collective-permute-start(bf16[64,4608]{1,0:T(8,128)(2,1)} %get-tuple-element.735), channel_id=1, source_target_pairs={{0,1},{1,0},{2,3},{3,2},{4,5},{5,4},{6,7},{7,6},{8,9},{9,8},{10,11... | collective-permute-start | bytes 1769480 | tf_op jit(solution)/shard_map/ppermute | solution.py:51
  655.3 39.0 %collective-permute-start.71 = (bf16[64,4608]{1,0:T(8,128)(2,1)}, bf16[64,4608]{1,0:T(8,128)(2,1)S(1)}, u32[]{:S(2)}, u32[]{:S(2)}) collective-permute-start(bf16[64,4608]{1,0:T(8,128)(2,1)} %get-tuple-element.736), channel_id=1, source_target_pairs={{0,2},{1,3},{2,0},{3,1},{4,6},{5,7},{6,4},{7,5},{8,10},{9,11},{10,... | collective-permute-start | bytes 1769480 | tf_op jit(solution)/shard_map/ppermute | solution.py:51
  656.6 37.7 %collective-permute-start.72 = (bf16[64,4608]{1,0:T(8,128)(2,1)}, bf16[64,4608]{1,0:T(8,128)(2,1)S(1)}, u32[]{:S(2)}, u32[]{:S(2)}) collective-permute-start(bf16[64,4608]{1,0:T(8,128)(2,1)} %get-tuple-element.737), channel_id=1, source_target_pairs={{0,3},{1,2},{2,1},{3,0},{4,7},{5,6},{6,5},{7,4},{8,11},{9,10},{10,... | collective-permute-start | bytes 1769480 | tf_op jit(solution)/shard_map/ppermute | solution.py:51
  (192 other events, 3895.2 us)
Sparse Core Ops, SparseCore 0:
  21.6 43.7 all-gather.4
  67.0 27.9 all-gather.6
  97.3 169.2 all-gather.8
  268.1 62.9 all-gather.10
  458.5 186.0 reduce-scatter.3
  648.3 67.5 reduce-scatter.5
  718.5 63.0 reduce-scatter.7
